TPU v7x, 32 devices: a whole 2x2x4 slice. The times are simulated.
32 devices in a mesh: ex: 16 (over z, y, core), hid: 2 (over x).
Axes of the slice: x: 2, y: 2, z: 4, core: 2. Of those that a mesh axis runs over, the one named last changes fastest.
Arguments:
- activations: bfloat16 [64, 192, 14336], P('ex', None, 'hid'), may hold values from -6 to 6
- out_grads: bfloat16 [64, 192, 4096], P('ex', None, 'hid'), may hold values from -6 to 6
- token_mask: int32 [64, 192], P('ex'), may hold values from 0 to 1, as said below
- proj_in: bfloat16 [14336, 64], P('hid'), may hold values from -0.046875 to 0.046875
- proj_out: bfloat16 [4096, 64], P('hid'), may hold values from -0.09375 to 0.09375
- inv_input: float32 [64, 64], replicated, as said below
- inv_output: float32 [64, 64], replicated, as said below
- query_feats: bfloat16 [1024, 4096], P('ex', 'hid'), may hold values from -6 to 6
Outputs:
- scores: float32 [1024, 64], P('ex', 'hid')
Inputs may be any that keep to these rules, and one draw needn't show every extreme that they name: `token_mask`: each row is 48 or more ones followed by zeros; some row is all ones. `inv_input`: symmetric. `inv_output`: symmetric.
All inputs are finite; a program needn't handle non-finite values.
Results may differ from a plain program's by a relative error of at most 0.0041.
Values may be sent and summed in bfloat16 or wider, within the bound.
No kernel may reach another device: no remote copies, remote signals or barrier semaphores. Data moves between devices by JAX's collectives and lax.ppermute only.
A program may use at most 64 MiB of HBM per device.

v0:
```python
import jax
import jax.numpy as jnp
from jax import lax
from jax.sharding import PartitionSpec as P


def local(
    activations, out_grads, token_mask, proj_in, proj_out, inv_input, inv_output, query_feats
):
    seq_count, length, unit_local = activations.shape
    rank_width = proj_in.shape[1]
    hid_size = lax.axis_size("hid")
    row_block = rank_width // hid_size
    my_index = lax.axis_index("hid")
    in_part = jnp.dot(
        activations.reshape(seq_count * length, unit_local),
        proj_in,
        preferred_element_type=jnp.float32,
    )
    in_part = jnp.dot(in_part, inv_input, precision=lax.Precision.HIGHEST)
    out_part = jnp.dot(
        out_grads.reshape(seq_count * length, out_grads.shape[2]),
        proj_out,
        preferred_element_type=jnp.float32,
    )
    token_weight = token_mask.astype(jnp.float32)
    tok_count = jnp.sum(token_weight, axis=1)
    in_full, out_full = lax.psum((in_part, out_part), "hid")
    in_mine = lax.dynamic_slice_in_dim(in_full, my_index * row_block, row_block, 1)
    masked = in_mine.reshape(seq_count, length, row_block) * token_weight[:, :, None]
    outer = jnp.einsum(
        "slr,slq->srq",
        masked,
        out_full.reshape(seq_count, length, rank_width),
        precision=lax.Precision.HIGHEST,
    )
    train_feats = (
        (outer / tok_count[:, None, None])
        .astype(jnp.bfloat16)
        .reshape(seq_count, row_block * rank_width)
    )
    query_count = query_feats.shape[0]
    queries = query_feats.reshape(query_count, row_block, rank_width).astype(jnp.float32)
    query_pre = jnp.einsum("qij,jk->qik", queries, inv_output, precision=lax.Precision.HIGHEST)
    query_pre = query_pre.astype(jnp.bfloat16).reshape(query_count, row_block * rank_width)
    partial_value = jnp.einsum(
        "qk,tk->qt",
        query_pre,
        lax.all_gather(train_feats, "ex", axis=0, tiled=True),
        preferred_element_type=jnp.float32,
    )
    return lax.psum_scatter(partial_value, "hid", scatter_dimension=1, tiled=True)


def solution(mesh):
    return jax.shard_map(
        local,
        mesh=mesh,
        in_specs=(
            P("ex", None, "hid"),
            P("ex", None, "hid"),
            P("ex", None),
            P("hid", None),
            P("hid", None),
            P(),
            P(),
            P("ex", "hid"),
        ),
        out_specs=P("ex", "hid"),
        check_vma=False,
    )
```

profile of v0, /device:TPU:0, one launch (start us, length us, event | category | flops | bytes accessed | tf_op | source)
XLA Modules:
  0.0 96.4 jit_solution(8763401855319154851)
XLA Ops:
  6.5 0.0 all-reduce.3.cloned.1.call-start
  6.5 1.9 %copy-done = bf16[4,192,2048]{2,1,0:T(8,128)(2,1)S(1)} copy-done((bf16[4,192,2048]{2,1,0:T(8,128)(2,1)S(1)}, bf16[4,192,2048]{2,1,0:T(8,128)(2,1)}, u32[]{:S(2)}) %copy-start) | copy-done | bytes 3145752
  8.4 2.0 %fusion.6 = f32[768,64]{0,1:T(8,128)S(1)} fusion(bf16[768,2048]{1,0:T(8,128)(2,1)S(1)} %bitcast.21, bf16[2048,64]{0,1:T(8,128)(2,1)} %param.12), kind=kOutput, calls=%fused_computation.11 | convolution fusion | flops 201326592 | bytes 3604480 | tf_op jit(solution)/shard_map/dot_general | solution.py:21
  10.5 0.9 reshape.28
  11.4 1.7 %copy.17 = f32[4,192,64]{1,2,0:T(8,128)} copy(f32[4,192,64]{1,0,2:T(4,128)} %reshape.28) | data formatting | bytes 393216 | tf_op jit(solution)/shard_map/reshape | solution.py:34
  13.1 7.8 %fusion.4 = f32[768,64]{0,1:T(8,128)S(1)} fusion(bf16[768,7168]{1,0:T(8,128)(2,1)} %bitcast.22, bf16[7168,64]{0,1:T(8,128)(2,1)} %param.11), kind=kOutput, calls=%fused_computation.9 | convolution fusion | flops 704643072 | bytes 12124160 | tf_op jit(solution)/shard_map/dot_general | solution.py:15
  20.9 1.1 %fusion.5 = f32[768,64]{0,1:T(8,128)} fusion(f32[768,64]{0,1:T(8,128)S(1)} %fusion.4, f32[64,64]{1,0:T(8,128)S(1)} %copy-done.3), kind=kOutput, calls=%fused_computation.10 | convolution fusion | flops 37748736 | bytes 409600 | tf_op jit(solution)/shard_map/dot_general | solution.py:20
  22.0 0.0 all-reduce.3.cloned.1.call-update
  22.0 0.0 reduce-scatter.2.cloned.1.call-start
  22.1 1.3 %reshape.23 = bf16[64,32,64]{2,1,0:T(8,128)(2,1)} reshape(bf16[64,2048]{1,0:T(8,128)(2,1)S(1)} %copy-done.1) | data formatting | bytes 524288 | tf_op jit(solution)/shard_map/reshape | solution.py:43
  23.4 1.6 %convolution_convert_fusion = bf16[64,32,64]{2,0,1:T(8,128)(2,1)S(1)} fusion(bf16[64,32,64]{2,1,0:T(8,128)(2,1)} %reshape.23, f32[64,64]{1,0:T(8,128)S(1)} %copy-done.2), kind=kOutput, calls=%fused_computation | convolution fusion | flops 100794368 | bytes 540672 | tf_op jit(solution)/shard_map/qij,jk->qik/dot_general | solution.py:44
  25.0 1.1 %copy.16 = bf16[64,32,64]{2,1,0:T(8,128)(2,1)} copy(bf16[64,32,64]{2,0,1:T(8,128)(2,1)S(1)} %convolution_convert_fusion) | data formatting | bytes 524288 | tf_op jit(solution)/shard_map/convert_element_type | solution.py:45
  26.2 1.5 %reshape.24 = bf16[64,2048]{1,0:T(8,128)(2,1)S(1)} reshape(bf16[64,32,64]{2,1,0:T(8,128)(2,1)} %copy.16) | data formatting | bytes 524288 | tf_op jit(solution)/shard_map/reshape | solution.py:45
  27.7 0.1 convert_reduce_fusion
  27.8 24.4 %all-reduce.3.cloned.1.call-done = (f32[4,192,64]{1,2,0:T(8,128)}, f32[768,64]{0,1:T(8,128)}) async-done(((f32[4,192,64]{1,2,0:T(8,128)}, f32[768,64]{0,1:T(8,128)}), (f32[4,192,64]{1,2,0:T(8,128)}, f32[768,64]{0,1:T(8,128)})) %all-reduce.3.cloned.1.call-update) | async-done | bytes 393232 | tf_op jit(solution)/shard_map/psum | solution.py:28
  52.2 1.5 %constant_dynamic-slice_fusion = f32[768,32]{0,1:T(8,128)} fusion(f32[768,64]{0,1:T(8,128)} %get-tuple-element.6, s32[]{:T(128)S(6)} %select_n.3), kind=kLoop, calls=%fused_computation.7 | loop fusion | bytes 196612 | tf_op jit(solution)/shard_map/dynamic_slice | solution.py:29
  53.7 1.0 %reshape.26 = f32[4,192,32]{1,0,2:T(4,128)S(1)} reshape(f32[768,32]{0,1:T(8,128)} %constant_dynamic-slice_fusion) | data formatting | bytes 196608 | tf_op jit(solution)/shard_map/reshape | solution.py:30
  54.8 1.3 %fusion = bf16[4,32,64]{2,1,0:T(8,128)(2,1)S(1)} fusion(f32[4,192,64]{1,2,0:T(8,128)} %get-tuple-element.5, f32[4,192,32]{1,0,2:T(4,128)S(1)} %bitcast.24, f32[4]{0:T(128)S(1)} %convert_reduce_fusion), kind=kOutput, calls=%fused_computation.2 | convolution fusion | flops 18890752 | bytes 311312 | tf_op jit(solution)/shard_map/slr,slq->srq/dot_general | solution.py:31
  56.1 0.1 reshape.30
  56.2 23.5 %all-gather = bf16[16,4,2048]{2,1,0:T(4,128)(2,1)} all-gather(bf16[1,4,2048]{2,1,0:T(4,128)(2,1)S(1)} %reshape.30), channel_id=1, replica_groups=mesh['ex'=16,'hid'=2] {'ex'}, dimensions={0}, use_global_device_ids=true | all-gather | bytes 278528 | tf_op jit(solution)/shard_map/all_gather | solution.py:49
  79.7 1.7 %reshape.31 = bf16[64,2048]{1,0:T(8,128)(2,1)} reshape(bf16[16,4,2048]{2,1,0:T(4,128)(2,1)} %all-gather) | data formatting | bytes 524288
  81.4 1.8 %fusion.7 = f32[64,64]{0,1:T(8,128)} fusion(bf16[64,2048]{1,0:T(8,128)(2,1)S(1)} %reshape.24, bf16[64,2048]{1,0:T(8,128)(2,1)} %reshape.31), kind=kOutput, calls=%fused_computation.12 | convolution fusion | flops 16777216 | bytes 540672 | tf_op jit(solution)/shard_map/qk,tk->qt/dot_general | solution.py:46
  83.2 0.0 reduce-scatter.2.cloned.1.call-update
  83.2 6.3 %reduce-scatter.2.cloned.1.call-done = f32[64,32]{0,1:T(8,128)} async-done(((f32[64,64]{0,1:T(8,128)}), f32[64,32]{0,1:T(8,128)}) %reduce-scatter.2.cloned.1.call-update) | async-done | bytes 8208 | tf_op jit(solution)/shard_map/reduce_scatter | solution.py:52
  (12 shorter events, 0.0 us)
Async XLA Ops:
  6.5 1.9 %copy-start = (bf16[4,192,2048]{2,1,0:T(8,128)(2,1)S(1)}, bf16[4,192,2048]{2,1,0:T(8,128)(2,1)}, u32[]{:S(2)}) copy-start(bf16[4,192,2048]{2,1,0:T(8,128)(2,1)} %param.9) | copy-start | bytes 9437188
  6.5 14.4 %copy-start.3 = (f32[64,64]{1,0:T(8,128)S(1)}, f32[64,64]{1,0:T(8,128)}, u32[]{:S(2)}) copy-start(f32[64,64]{1,0:T(8,128)} %param.13) | copy-start | bytes 49156
  6.5 16.9 %copy-start.2 = (f32[64,64]{1,0:T(8,128)S(1)}, f32[64,64]{1,0:T(8,128)}, u32[]{:S(2)}) copy-start(f32[64,64]{1,0:T(8,128)} %param.14) | copy-start | bytes 49156
  6.5 45.7 %all-reduce.3.cloned.1.call-start = ((), (), s32[]{:S(2)}) async-start(), calls=%async_computation.2 | async-start | bytes 917504 | tf_op jit(solution)/shard_map/psum | solution.py:28
  8.4 19.2 %copy-start.4 = (s32[4,192]{1,0:T(4,128)S(1)}, s32[4,192]{1,0:T(4,128)}, u32[]{:S(2)}) copy-start(s32[4,192]{1,0:T(4,128)} %param.10) | copy-start | bytes 9220
  11.4 10.7 %copy-start.1 = (bf16[64,2048]{1,0:T(8,128)(2,1)S(1)}, bf16[64,2048]{1,0:T(8,128)(2,1)}, u32[]{:S(2)}) copy-start(bf16[64,2048]{1,0:T(8,128)(2,1)} %param.15) | copy-start | bytes 786436
  22.0 67.5 %reduce-scatter.2.cloned.1.call-start = ((), (), s32[]{:S(2)}) async-start(), calls=%async_computation.1 | async-start | bytes 49152 | tf_op jit(solution)/shard_map/reduce_scatter | solution.py:52
Sparse Core Ops, SparseCore 0:
  22.1 30.0 all-reduce.2
  83.3 6.1 reduce-scatter.1
where the time goes:
time: 96.8 us; the launch traced here: 96.4 us
  waiting for transfers between devices  30.7 us (32%)
  blocking collectives  23.5 us (24%)
  matrix products  15.6 us (16%)
  between operations  13.5 us (14%)
  local copies, waits for them, and re-layouts  12.8 us (13%)
    psum x1, waiting for transfers between devices, local(): in_full, out_full = lax.psum((in_part, out_part), 'hid')  24.4 us
    all_gather x1, blocking collectives, local(): lax.all_gather(train_feats, 'ex', axis=0, tiled=True)  23.5 us
    dot_general x1, matrix products, local(): jnp.dot(activations.reshape(seq_count * length, unit_local), proj_in, pre...  7.81 us
    reduce_scatter x1, waiting for transfers between devices, local(): lax.psum_scatter(partial_value, 'hid', scatter_dimension=1, tiled=True)  6.31 us
    unnamed x13, local copies, waits for them, and re-layouts  3.7 us
    reshape x2, local copies, waits for them, and re-layouts, local(): out_full.reshape(seq_count, length, rank_width)  2.64 us
    dot_general x1, matrix products, local(): jnp.dot(out_grads.reshape(seq_count * length, out_grads.shape[2]), proj_o...  2.03 us
  transfers between devices with their start and end apart: 2, of which 2 were waited for; matrix products, arithmetic and copies ran while one was open for 6% of the time, Pallas kernels for 0%

commit v1 on v0

v1 whole, which is shorter than its diff:
```python
import functools

import jax
import jax.numpy as jnp
from jax import lax
from jax.experimental import pallas as pl
from jax.experimental.pallas import tpu as pltpu
from jax.sharding import PartitionSpec as P

F32 = jnp.float32
BF16 = jnp.bfloat16
NT = (((1,), (1,)), ((), ()))
TN = (((0,), (0,)), ((), ()))
VMEM = pl.BlockSpec(memory_space=pltpu.VMEM)
ANY = pl.BlockSpec(memory_space=pl.ANY)
HIGH = lax.Precision.HIGHEST


def params(mib):
    return pltpu.CompilerParams(vmem_limit_bytes=mib << 20)


def project_kernel(chunks, x_hbm, w_ref, *rest):
    out_ref = rest[0]
    sent_ref = rest[1] if len(rest) == 4 else None
    buf, sems = rest[-2:]
    rows = x_hbm.shape[0]
    step = rows // chunks
    copies = [
        pltpu.make_async_copy(
            x_hbm.at[pl.ds(c * step, step)], buf.at[pl.ds(c * step, step)], sems.at[c]
        )
        for c in range(chunks)
    ]
    for copy in copies:
        copy.start()
    half = rows // 2
    rank = w_ref.shape[0]
    for c in range(chunks):
        copies[c].wait()
        part = lax.dot_general(
            buf[pl.ds(c * step, step), :], w_ref[...], NT, preferred_element_type=F32
        )
        row, lane = (c * step) % half, (c * step) // half * rank
        out_ref[pl.ds(row, step), pl.ds(lane, rank)] = part
    if sent_ref is not None:
        sent_ref[...] = out_ref[...].astype(BF16)


def project(x, w_t, chunks, send, mib):
    rows, depth = x.shape
    rank = w_t.shape[0]
    shape = (rows // 2, 2 * rank)
    outs = [jax.ShapeDtypeStruct(shape, F32)]
    if send:
        outs.append(jax.ShapeDtypeStruct(shape, BF16))
    return pl.pallas_call(
        functools.partial(project_kernel, chunks),
        out_shape=outs,
        in_specs=[ANY, VMEM],
        out_specs=[VMEM] * len(outs),
        scratch_shapes=[
            pltpu.VMEM((rows, depth), BF16),
            pltpu.SemaphoreType.DMA((chunks,)),
        ],
        compiler_params=params(mib),
        cost_estimate=pl.CostEstimate(
            flops=2 * rows * depth * rank, bytes_accessed=2 * rows * depth, transcendentals=0
        ),
    )(x, w_t)


def outer_kernel(
    length, in_ref, own_ref, got_ref, mask_ref, inv_ref, part_ref, sent_ref, rows_ref, pairs_ref
):
    rank = inv_ref.shape[0]
    seqs = mask_ref.shape[0]
    counts = jnp.sum(mask_ref[...].astype(F32), axis=1, keepdims=True)
    lane = lax.broadcasted_iota(jnp.int32, (length, 2 * rank), 1)
    token = lax.broadcasted_iota(jnp.int32, (length, 2 * rank), 0).astype(F32)
    grams = [None] * seqs
    for pair in range(seqs // 2):
        rows = pl.ds(pair * length, length)
        low, high = counts[pair : pair + 1, :], counts[pair + seqs // 2 : pair + seqs // 2 + 1, :]
        real = token < jnp.where(lane < rank, low, high)
        inside = jnp.where(real, in_ref[rows, :], 0.0)
        outside = own_ref[rows, :] + got_ref[rows, :].astype(F32)
        both = lax.dot_general(
            inside, outside, TN, precision=HIGH, preferred_element_type=F32
        )
        grams[pair] = both[:rank, :rank] / low
        grams[pair + seqs // 2] = both[rank:, rank:] / high
    gram = jnp.concatenate(grams, axis=1)
    pre = lax.dot_general(inv_ref[...], gram, TN, precision=HIGH, preferred_element_type=F32)
    half = rank // 2
    for s in range(seqs):
        rows_ref[...] = pre[:, s * rank : (s + 1) * rank]
        pairs_ref[pl.ds(s * half, half), :] = jnp.concatenate(
            [rows_ref[pl.ds(0, half, stride=2), :], rows_ref[pl.ds(1, half, stride=2), :]], axis=1
        )
    for b in range(half):
        row = pairs_ref[pl.ds(b, seqs, stride=half), :]
        part_ref[:, pl.ds(b * 2 * rank, 2 * rank)] = row
    sent_ref[...] = part_ref[...].astype(BF16)


def outer(in_part, out_own, out_got, token_mask, inv_input):
    seqs, length = token_mask.shape
    rank = inv_input.shape[0]
    shape = (seqs, rank * rank)
    return pl.pallas_call(
        functools.partial(outer_kernel, length),
        out_shape=[jax.ShapeDtypeStruct(shape, F32), jax.ShapeDtypeStruct(shape, BF16)],
        in_specs=[VMEM] * 5,
        out_specs=[VMEM] * 2,
        scratch_shapes=[
            pltpu.VMEM((rank, rank), F32),
            pltpu.VMEM((seqs * rank // 2, 2 * rank), F32),
        ],
        compiler_params=params(16),
    )(in_part, out_own, out_got, token_mask, inv_input)


def query_kernel(query_ref, inv_ref, pre_ref):
    rank = inv_ref.shape[0]
    zero = jnp.zeros((rank, rank), F32)
    inv = inv_ref[...]
    block = jnp.concatenate(
        [jnp.concatenate([inv, zero], axis=1), jnp.concatenate([zero, inv], axis=1)], axis=0
    )
    top = block.astype(BF16)
    rest = block - top.astype(F32)
    middle = rest.astype(BF16)
    last = (rest - middle.astype(F32)).astype(BF16)
    for b in range(query_ref.shape[1] // (2 * rank)):
        lanes = pl.ds(b * 2 * rank, 2 * rank)
        query = query_ref[:, lanes]
        total = jnp.dot(query, last, preferred_element_type=F32)
        total += jnp.dot(query, middle, preferred_element_type=F32)
        total += jnp.dot(query, top, preferred_element_type=F32)
        pre_ref[:, lanes] = total.astype(BF16)


def precondition_queries(query_feats, inv_output):
    return pl.pallas_call(
        query_kernel,
        out_shape=jax.ShapeDtypeStruct(query_feats.shape, BF16),
        in_specs=[VMEM] * 2,
        out_specs=VMEM,
        compiler_params=params(16),
    )(query_feats, inv_output)


def score_kernel(place_ref, low_ref, high_ref, *rest):
    *pieces, out_ref, feats_ref = rest
    seqs = pieces[0].shape[0]
    for k, piece in enumerate(pieces):
        feats_ref[pl.ds(k * seqs, seqs), :] = piece[...].astype(F32)
    half = low_ref.shape[1]
    feats = feats_ref[...].astype(BF16)
    scores = lax.dot_general(feats[:, :half], low_ref[...], NT, preferred_element_type=F32)
    scores += lax.dot_general(feats[:, half:], high_ref[...], NT, preferred_element_type=F32)
    rows = scores.shape[0]
    at = lax.broadcasted_iota(jnp.int32, scores.shape, 0)
    place = place_ref[0]
    size = seqs
    while size < rows:
        swapped = jnp.where(
            (at & size) == 0, pltpu.roll(scores, rows - size, 0), pltpu.roll(scores, size, 0)
        )
        bit = (place & (size // seqs)) != 0
        scores = jnp.where(bit, swapped, scores)
        size *= 2
    out_ref[...] = scores


def score(place, low, high, pieces):
    seqs, feats = pieces[0].shape
    rows = seqs * len(pieces)
    return pl.pallas_call(
        score_kernel,
        out_shape=jax.ShapeDtypeStruct((rows, low.shape[0]), F32),
        in_specs=[pl.BlockSpec(memory_space=pltpu.SMEM)] + [VMEM] * (2 + len(pieces)),
        out_specs=VMEM,
        scratch_shapes=[pltpu.VMEM((rows, feats), F32)],
        compiler_params=params(16),
    )(place, low, high, *pieces)


def local_pair(
    activations, out_grads, token_mask, proj_in, proj_out, inv_input, inv_output, query_feats
):
    seqs, length, depth = activations.shape
    ex_size = lax.axis_size("ex")
    ex = lax.axis_index("ex")
    hid = lax.axis_index("hid")
    half = ex_size // 2
    swap_hid = [(0, 1), (1, 0)]

    out_own, out_sent = project(
        out_grads.reshape(seqs * length, -1), proj_out.T, 4, True, 16
    )
    out_got = lax.ppermute(out_sent, "hid", swap_hid)
    (in_part,) = project(activations.reshape(seqs * length, depth), proj_in.T, 8, False, 32)
    part, sent = outer(in_part, out_own, out_got, token_mask, inv_input)

    around, across = [], []
    for e in range(half):
        a, b, c, d = 2 * e + 1, 2 * e, 2 * (e + half), 2 * (e + half) + 1
        around += [(a, b), (b, c), (c, d), (d, a)]
        across += [(a, c), (c, a), (b, d), (d, b)]
    axes = ("ex", "hid")
    first = lax.ppermute(sent, axes, around)
    second = lax.ppermute(sent, axes, across)
    home = (ex // half) == hid
    mine = (
        first.astype(F32) + jnp.where(home, part, second.astype(F32))
    ).astype(BF16)

    query_own = precondition_queries(query_feats, inv_output)
    query_got = lax.ppermute(query_own, "hid", swap_hid)
    low = jnp.where(hid == 0, query_own, query_got)
    high = jnp.where(hid == 0, query_got, query_own)

    pieces = [mine]
    far = [k for k in range(2, half, 2)]
    pieces = {0: mine}
    for k in sorted(far, key=lambda k: -k):
        pieces[k] = lax.ppermute(mine, "ex", [(i, i ^ k) for i in range(ex_size)])
    for k in list(pieces):
        pieces[k ^ 1] = lax.ppermute(pieces[k], "ex", [(i, i ^ 1) for i in range(ex_size)])
    place = (ex % half).astype(jnp.int32).reshape(1)
    scores = score(place, low, high, [pieces[k] for k in range(half)])
    return scores.T


def local_any(
    activations, out_grads, token_mask, proj_in, proj_out, inv_input, inv_output, query_feats
):
    seq_count, length, unit_local = activations.shape
    rank_width = proj_in.shape[1]
    hid_size = lax.axis_size("hid")
    row_block = rank_width // hid_size
    my_index = lax.axis_index("hid")
    in_part = jnp.dot(
        activations.reshape(seq_count * length, unit_local),
        proj_in,
        preferred_element_type=F32,
    )
    in_part = jnp.dot(in_part, inv_input, precision=HIGH)
    out_part = jnp.dot(
        out_grads.reshape(seq_count * length, out_grads.shape[2]),
        proj_out,
        preferred_element_type=F32,
    )
    token_weight = token_mask.astype(F32)
    tok_count = jnp.sum(token_weight, axis=1)
    in_full, out_full = lax.psum((in_part, out_part), "hid")
    in_mine = lax.dynamic_slice_in_dim(in_full, my_index * row_block, row_block, 1)
    masked = in_mine.reshape(seq_count, length, row_block) * token_weight[:, :, None]
    outer_sum = jnp.einsum(
        "slr,slq->srq",
        masked,
        out_full.reshape(seq_count, length, rank_width),
        precision=HIGH,
    )
    train_feats = (
        (outer_sum / tok_count[:, None, None])
        .astype(BF16)
        .reshape(seq_count, row_block * rank_width)
    )
    query_count = query_feats.shape[0]
    queries = query_feats.reshape(query_count, row_block, rank_width).astype(F32)
    query_pre = jnp.einsum("qij,jk->qik", queries, inv_output, precision=HIGH)
    query_pre = query_pre.astype(BF16).reshape(query_count, row_block * rank_width)
    partial_value = jnp.einsum(
        "qk,tk->qt",
        query_pre,
        lax.all_gather(train_feats, "ex", axis=0, tiled=True),
        preferred_element_type=F32,
    )
    return lax.psum_scatter(partial_value, "hid", scatter_dimension=1, tiled=True)


def solution(mesh):
    ex_size, hid_size = mesh.shape["ex"], mesh.shape["hid"]
    paired = hid_size == 2 and ex_size >= 4 and ex_size & (ex_size - 1) == 0
    return jax.shard_map(
        local_pair if paired else local_any,
        mesh=mesh,
        in_specs=(
            P("ex", None, "hid"),
            P("ex", None, "hid"),
            P("ex", None),
            P("hid", None),
            P("hid", None),
            P(),
            P(),
            P("ex", "hid"),
        ),
        out_specs=P("ex", "hid"),
        check_vma=False,
    )
```

time: 96.8 us -> 41.1 us (0.42)
  blocking collectives: 23.5 us -> 0 us
  waiting for transfers between devices: 30.7 us -> 7.78 us
  matrix products: 15.6 us -> 0 us
  Pallas kernels: 0 us -> 13.5 us
  between operations: 13.5 us -> 0.09 us
  starting transfers between devices: 0.04 us -> 11.2 us
  local copies, waits for them, and re-layouts: 12.8 us -> 8.16 us
    psum x1 -> x0, waiting for transfers between devices: 24.4 us -> none  [local(): in_full, out_full = lax.psum((in_part, out_part), 'hid')]
    all_gather x1 -> x0, blocking collectives: 23.5 us -> none  [local(): lax.all_gather(train_feats, 'ex', axis=0, tiled=True)]
    dot_general x6 -> x0, matrix products: 15.6 us -> none  [the longest x1 7.81 us: local(): jnp.dot(activations.reshape(seq_count * length, unit_local), proj_in, pre...]
    pallas_call x0 -> x5, Pallas kernels: none -> 13.5 us  [the longest x2 11 us: project(): pl.pallas_call(functools.partial(project_kernel, chunks), out_shape=outs,...]
    ppermute x0 -> x11, starting transfers between devices: none -> 11.2 us  [the longest x3 3.55 us: local_pair(): pieces[k] = lax.ppermute(mine, 'ex', [(i, i ^ k) for i in range(ex_size)])]
    ppermute x0 -> x11, waiting for transfers between devices: none -> 7.78 us  [the longest x3 3.45 us: local_pair(): pieces[k] = lax.ppermute(mine, 'ex', [(i, i ^ k) for i in range(ex_size)])]
    reshape x5 -> x0, local copies, waits for them, and re-layouts: 6.46 us -> none  [the longest x2 2.64 us: local(): out_full.reshape(seq_count, length, rank_width)]
    reduce_scatter x1 -> x0, waiting for transfers between devices: 6.31 us -> none  [local(): lax.psum_scatter(partial_value, 'hid', scatter_dimension=1, tiled=True)]
  transfers between devices with their start and end apart: 2 -> 11, of which waited for: 2 -> 6; matrix products, arithmetic and copies ran while one was open for 6% -> 0% of each run, Pallas kernels for 0% -> 22%
where the time goes in v1:
time: 41.1 us; the launch traced here: 40.9 us
  Pallas kernels  13.5 us (33%)
  starting transfers between devices  11.2 us (27%)
  local copies, waits for them, and re-layouts  8.16 us (20%)
  waiting for transfers between devices  7.78 us (19%)
    pallas_call x2, Pallas kernels, project(): pl.pallas_call(functools.partial(project_kernel, chunks), out_shape=outs,...  11 us
    unnamed x16, local copies, waits for them, and re-layouts  8.16 us
    ppermute x3, starting transfers between devices, local_pair(): pieces[k] = lax.ppermute(mine, 'ex', [(i, i ^ k) for i in range(ex_size)])  3.55 us
    ppermute x3, waiting for transfers between devices, local_pair(): pieces[k] = lax.ppermute(mine, 'ex', [(i, i ^ k) for i in range(ex_size)])  3.45 us
    ppermute x1, waiting for transfers between devices, local_pair(): second = lax.ppermute(sent, axes, across)  3.17 us
    ppermute x1, starting transfers between devices, local_pair(): out_got = lax.ppermute(out_sent, 'hid', swap_hid)  3 us
    ppermute x1, starting transfers between devices, local_pair(): first = lax.ppermute(sent, axes, around)  2.64 us
    ppermute x1, starting transfers between devices, local_pair(): query_got = lax.ppermute(query_own, 'hid', swap_hid)  1.98 us
  transfers between devices with their start and end apart: 11, of which 6 were waited for; matrix products, arithmetic and copies ran while one was open for 0% of the time, Pallas kernels for 22%

profile of v1, /device:TPU:0, one launch (start us, length us, event | category | flops | bytes accessed | tf_op | source)
XLA Modules:
  0.0 40.9 jit_solution(2973417378320108450)
XLA Ops:
  0.0 1.9 %copy-done.1 = bf16[4,192,2048]{2,1,0:T(8,128)(2,1)S(1)} copy-done((bf16[4,192,2048]{2,1,0:T(8,128)(2,1)S(1)}, bf16[4,192,2048]{2,1,0:T(8,128)(2,1)}, u32[]{:S(2)}) %copy-start.1) | copy-done | bytes 3145752
  1.9 0.9 %copy-done.4 = bf16[2048,64]{0,1:T(8,128)(2,1)S(1)} copy-done((bf16[2048,64]{0,1:T(8,128)(2,1)S(1)}, bf16[2048,64]{0,1:T(8,128)(2,1)}, u32[]{:S(2)}) %copy-start.4) | copy-done | bytes 262168
  2.9 2.6 %shard_map.84 = (f32[384,128]{1,0:T(8,128)S(1)}, bf16[384,128]{1,0:T(8,128)(2,1)S(1)}) custom-call(bf16[768,2048]{1,0:T(8,128)(2,1)S(1)} %bitcast.7, bf16[64,2048]{1,0:T(8,128)(2,1)S(1)} %bitcast.9), custom_call_target="tpu_custom_call" | custom-call | flops 201326592 | bytes 3145728 | tf_op jit(solution)/shard_map/pallas_call | solution.py:57
  5.4 3.0 %collective-permute-start.1 = (bf16[384,128]{1,0:T(8,128)(2,1)S(1)}, bf16[384,128]{1,0:T(8,128)(2,1)S(1)}, u32[]{:S(2)}, u32[]{:S(2)}) collective-permute-start(bf16[384,128]{1,0:T(8,128)(2,1)S(1)} %get-tuple-element.10), channel_id=1, source_target_pairs={{0,1},{1,0},{2,3},{3,2},{4,5},{5,4},{6,7},{7,6},{8,9},{9,8},{10,11... | collective-permute-start | bytes 294920 | tf_op jit(solution)/shard_map/ppermute | solution.py:203
  8.4 4.1 %copy-done = bf16[4,192,7168]{2,1,0:T(8,128)(2,1)S(1)} copy-done((bf16[4,192,7168]{2,1,0:T(8,128)(2,1)S(1)}, bf16[4,192,7168]{2,1,0:T(8,128)(2,1)}, u32[]{:S(2)}) %copy-start) | copy-done | bytes 11010072
  12.6 1.2 %copy-done.2 = bf16[7168,64]{0,1:T(8,128)(2,1)S(1)} copy-done((bf16[7168,64]{0,1:T(8,128)(2,1)S(1)}, bf16[7168,64]{0,1:T(8,128)(2,1)}, u32[]{:S(2)}) %copy-start.2) | copy-done | bytes 917528
  13.7 8.4 %shard_map.83.in_ref = f32[384,128]{1,0:T(8,128)S(1)} custom-call(bf16[768,7168]{1,0:T(8,128)(2,1)S(1)} %bitcast.6, bf16[64,7168]{1,0:T(8,128)(2,1)S(1)} %bitcast.8), custom_call_target="tpu_custom_call" | custom-call | flops 704643072 | bytes 11010048 | tf_op jit(solution)/shard_map/pallas_call | solution.py:57
  22.2 1.0 %shard_map.85 = (f32[4,4096]{1,0:T(4,128)S(1)}, bf16[4,4096]{1,0:T(4,128)(2,1)S(1)}) custom-call(f32[384,128]{1,0:T(8,128)S(1)} %shard_map.83.in_ref, f32[384,128]{1,0:T(8,128)S(1)} %get-tuple-element.9.own_ref, bf16[384,128]{1,0:T(8,128)(2,1)S(1)} %collective-permute-done.1.got_ref, s32[4,192]{1,0:T(4,128)S(1)} %copy-done.7, f32[64,64]{1,0:T(8,128)S(1)} %copy-done.5), custom_call_target="tpu_custom_call" | custom-call | tf_op jit(solution)/shard_map/pallas_call | solution.py:111
  23.2 2.6 %collective-permute-start.2 = (bf16[4,4096]{1,0:T(4,128)(2,1)S(1)}, bf16[4,4096]{1,0:T(4,128)(2,1)S(1)}, u32[]{:S(2)}, u32[]{:S(2)}) collective-permute-start(bf16[4,4096]{1,0:T(4,128)(2,1)S(1)} %get-tuple-element.11), channel_id=1, source_target_pairs={{1,0},{0,16},{16,17},{17,1},{3,2},{2,18},{18,19},{19,3},{5,4},{4,2... | collective-permute-start | bytes 98312 | tf_op jit(solution)/shard_map/ppermute | solution.py:213
  25.9 0.1 collective-permute-start.3
  25.9 0.6 %shard_map.82 = bf16[64,2048]{1,0:T(8,128)(2,1)S(1)} custom-call(bf16[64,2048]{1,0:T(8,128)(2,1)S(1)} %copy-done.3, f32[64,64]{1,0:T(8,128)S(1)} %copy-done.6), custom_call_target="tpu_custom_call" | custom-call | tf_op jit(solution)/shard_map/pallas_call | solution.py:145
  26.5 2.0 %collective-permute-start = (bf16[64,2048]{1,0:T(8,128)(2,1)S(1)}, bf16[64,2048]{1,0:T(8,128)(2,1)S(1)}, u32[]{:S(2)}, u32[]{:S(2)}) collective-permute-start(bf16[64,2048]{1,0:T(8,128)(2,1)S(1)} %shard_map.82), channel_id=1, source_target_pairs={{0,1},{1,0},{2,3},{3,2},{4,5},{5,4},{6,7},{7,6},{8,9},{9,8},{10,11... | collective-permute-start | bytes 786440 | tf_op jit(solution)/shard_map/ppermute | solution.py:221
  28.5 0.0 collective-permute-done.2
  28.5 3.2 %collective-permute-done.3 = bf16[4,4096]{1,0:T(4,128)(2,1)S(1)} collective-permute-done((bf16[4,4096]{1,0:T(4,128)(2,1)S(1)}, bf16[4,4096]{1,0:T(4,128)(2,1)S(1)}, u32[]{:S(2)}, u32[]{:S(2)}) %collective-permute-start.3) | collective-permute-done | bytes 32800 | tf_op jit(solution)/shard_map/ppermute | solution.py:214
  31.7 2.6 %collective-permute-start.9 = (bf16[4,4096]{1,0:T(4,128)(2,1)S(1)}, bf16[4,4096]{1,0:T(4,128)(2,1)S(1)}, u32[]{:S(2)}, u32[]{:S(2)}) collective-permute-start(bf16[4,4096]{1,0:T(4,128)(2,1)S(1)} %add_convert_fusion.rest_0_), channel_id=1, source_target_pairs={{0,12},{2,14},{4,8},{6,10},{8,4},{10,6},{12,0},{14,2},{16,28},{18,... | collective-permute-start | bytes 98312 | tf_op jit(solution)/shard_map/ppermute | solution.py:229
  34.3 0.5 %collective-permute-start.5 = (bf16[4,4096]{1,0:T(4,128)(2,1)S(1)}, bf16[4,4096]{1,0:T(4,128)(2,1)S(1)}, u32[]{:S(2)}, u32[]{:S(2)}) collective-permute-start(bf16[4,4096]{1,0:T(4,128)(2,1)S(1)} %add_convert_fusion.rest_0_), channel_id=1, source_target_pairs={{0,4},{2,6},{4,0},{6,2},{8,12},{10,14},{12,8},{14,10},{16,20},{18,... | collective-permute-start | bytes 98312 | tf_op jit(solution)/shard_map/ppermute | solution.py:229
  34.8 0.4 %collective-permute-start.7 = (bf16[4,4096]{1,0:T(4,128)(2,1)S(1)}, bf16[4,4096]{1,0:T(4,128)(2,1)S(1)}, u32[]{:S(2)}, u32[]{:S(2)}) collective-permute-start(bf16[4,4096]{1,0:T(4,128)(2,1)S(1)} %add_convert_fusion.rest_0_), channel_id=1, source_target_pairs={{0,8},{2,10},{4,12},{6,14},{8,0},{10,2},{12,4},{14,6},{16,24},{18,... | collective-permute-start | bytes 98312 | tf_op jit(solution)/shard_map/ppermute | solution.py:229
  35.3 1.4 %collective-permute-done.9.rest_6_ = bf16[4,4096]{1,0:T(4,128)(2,1)S(1)} collective-permute-done((bf16[4,4096]{1,0:T(4,128)(2,1)S(1)}, bf16[4,4096]{1,0:T(4,128)(2,1)S(1)}, u32[]{:S(2)}, u32[]{:S(2)}) %collective-permute-start.9) | collective-permute-done | bytes 32800 | tf_op jit(solution)/shard_map/ppermute | solution.py:229
  36.6 1.6 %collective-permute-done.5.rest_2_ = bf16[4,4096]{1,0:T(4,128)(2,1)S(1)} collective-permute-done((bf16[4,4096]{1,0:T(4,128)(2,1)S(1)}, bf16[4,4096]{1,0:T(4,128)(2,1)S(1)}, u32[]{:S(2)}, u32[]{:S(2)}) %collective-permute-start.5) | collective-permute-done | bytes 32800 | tf_op jit(solution)/shard_map/ppermute | solution.py:229
  38.2 0.5 %collective-permute-done.7.rest_4_ = bf16[4,4096]{1,0:T(4,128)(2,1)S(1)} collective-permute-done((bf16[4,4096]{1,0:T(4,128)(2,1)S(1)}, bf16[4,4096]{1,0:T(4,128)(2,1)S(1)}, u32[]{:S(2)}, u32[]{:S(2)}) %collective-permute-start.7) | collective-permute-done | bytes 32800 | tf_op jit(solution)/shard_map/ppermute | solution.py:229
  38.7 0.0 collective-permute-start.8
  38.8 0.6 %collective-permute-done.6.rest_3_ = bf16[4,4096]{1,0:T(4,128)(2,1)S(1)} collective-permute-done((bf16[4,4096]{1,0:T(4,128)(2,1)S(1)}, bf16[4,4096]{1,0:T(4,128)(2,1)S(1)}, u32[]{:S(2)}, u32[]{:S(2)}) %collective-permute-start.6) | collective-permute-done | bytes 32800 | tf_op jit(solution)/shard_map/ppermute | solution.py:231
  39.4 0.5 %collective-permute-done.8.rest_5_ = bf16[4,4096]{1,0:T(4,128)(2,1)S(1)} collective-permute-done((bf16[4,4096]{1,0:T(4,128)(2,1)S(1)}, bf16[4,4096]{1,0:T(4,128)(2,1)S(1)}, u32[]{:S(2)}, u32[]{:S(2)}) %collective-permute-start.8) | collective-permute-done | bytes 32800 | tf_op jit(solution)/shard_map/ppermute | solution.py:231
  39.9 0.9 %shard_map.86 = f32[32,64]{1,0:T(8,128)} custom-call(s32[1]{0:T(128)} %bitcast.place_ref, bf16[64,2048]{1,0:T(8,128)(2,1)S(1)} %get-tuple-element.14.low_ref, bf16[64,2048]{1,0:T(8,128)(2,1)S(1)} %get-tuple-element.13.high_ref, bf16[4,4096]{1,0:T(4,128)(2,1)S(1)} %add_convert_fusion.rest_0_, bf16[4,4096]{1,0:T(4,128)(2,1)S(1)} %collective-permute-done.4.rest_1_, ...), custom_call_target="tpu_custom_call" | custom-call | tf_op jit(solution)/shard_map/pallas_call | solution.py:180
  (21 shorter events, 0.1 us)
Async XLA Ops:
  0.0 1.9 %copy-start.1 = (bf16[4,192,2048]{2,1,0:T(8,128)(2,1)S(1)}, bf16[4,192,2048]{2,1,0:T(8,128)(2,1)}, u32[]{:S(2)}) copy-start(bf16[4,192,2048]{2,1,0:T(8,128)(2,1)} %param.9) | copy-start | bytes 9437188
  1.9 0.9 %copy-start.4 = (bf16[2048,64]{0,1:T(8,128)(2,1)S(1)}, bf16[2048,64]{0,1:T(8,128)(2,1)}, u32[]{:S(2)}) copy-start(bf16[2048,64]{0,1:T(8,128)(2,1)} %param.12) | copy-start | bytes 786436
  2.8 19.4 %copy-start.5 = (f32[64,64]{1,0:T(8,128)S(1)}, f32[64,64]{1,0:T(8,128)}, u32[]{:S(2)}) copy-start(f32[64,64]{1,0:T(8,128)} %inv_ref.3) | copy-start | bytes 49156
  2.8 19.4 %copy-start.7 = (s32[4,192]{1,0:T(4,128)S(1)}, s32[4,192]{1,0:T(4,128)}, u32[]{:S(2)}) copy-start(s32[4,192]{1,0:T(4,128)} %mask_ref.1) | copy-start | bytes 9220
  2.8 23.1 %copy-start.3 = (bf16[64,2048]{1,0:T(8,128)(2,1)S(1)}, bf16[64,2048]{1,0:T(8,128)(2,1)}, u32[]{:S(2)}) copy-start(bf16[64,2048]{1,0:T(8,128)(2,1)} %query_ref.1) | copy-start | bytes 786436
  2.8 23.1 %copy-start.6 = (f32[64,64]{1,0:T(8,128)S(1)}, f32[64,64]{1,0:T(8,128)}, u32[]{:S(2)}) copy-start(f32[64,64]{1,0:T(8,128)} %inv_ref.2) | copy-start | bytes 49156
  5.4 16.8 %collective-permute-start.1 = (bf16[384,128]{1,0:T(8,128)(2,1)S(1)}, bf16[384,128]{1,0:T(8,128)(2,1)S(1)}, u32[]{:S(2)}, u32[]{:S(2)}) collective-permute-start(bf16[384,128]{1,0:T(8,128)(2,1)S(1)} %get-tuple-element.10), channel_id=1, source_target_pairs={{0,1},{1,0},{2,3},{3,2},{4,5},{5,4},{6,7},{7,6},{8,9},{9,8},{10,11... | collective-permute-start | bytes 294920 | tf_op jit(solution)/shard_map/ppermute | solution.py:203
  8.4 4.1 %copy-start = (bf16[4,192,7168]{2,1,0:T(8,128)(2,1)S(1)}, bf16[4,192,7168]{2,1,0:T(8,128)(2,1)}, u32[]{:S(2)}) copy-start(bf16[4,192,7168]{2,1,0:T(8,128)(2,1)} %param.8) | copy-start | bytes 33030148
  12.6 1.2 %copy-start.2 = (bf16[7168,64]{0,1:T(8,128)(2,1)S(1)}, bf16[7168,64]{0,1:T(8,128)(2,1)}, u32[]{:S(2)}) copy-start(bf16[7168,64]{0,1:T(8,128)(2,1)} %param.11) | copy-start | bytes 2752516
  23.2 5.3 %collective-permute-start.2 = (bf16[4,4096]{1,0:T(4,128)(2,1)S(1)}, bf16[4,4096]{1,0:T(4,128)(2,1)S(1)}, u32[]{:S(2)}, u32[]{:S(2)}) collective-permute-start(bf16[4,4096]{1,0:T(4,128)(2,1)S(1)} %get-tuple-element.11), channel_id=1, source_target_pairs={{1,0},{0,16},{16,17},{17,1},{3,2},{2,18},{18,19},{19,3},{5,4},{4,2... | collective-permute-start | bytes 98312 | tf_op jit(solution)/shard_map/ppermute | solution.py:213
  25.9 5.8 %collective-permute-start.3 = (bf16[4,4096]{1,0:T(4,128)(2,1)S(1)}, bf16[4,4096]{1,0:T(4,128)(2,1)S(1)}, u32[]{:S(2)}, u32[]{:S(2)}) collective-permute-start(bf16[4,4096]{1,0:T(4,128)(2,1)S(1)} %get-tuple-element.11), channel_id=1, source_target_pairs={{1,16},{16,1},{0,17},{17,0},{3,18},{18,3},{2,19},{19,2},{5,20},{20... | collective-permute-start | bytes 98312 | tf_op jit(solution)/shard_map/ppermute | solution.py:214
  26.5 12.2 %collective-permute-start = (bf16[64,2048]{1,0:T(8,128)(2,1)S(1)}, bf16[64,2048]{1,0:T(8,128)(2,1)S(1)}, u32[]{:S(2)}, u32[]{:S(2)}) collective-permute-start(bf16[64,2048]{1,0:T(8,128)(2,1)S(1)} %shard_map.82), channel_id=1, source_target_pairs={{0,1},{1,0},{2,3},{3,2},{4,5},{5,4},{6,7},{7,6},{8,9},{9,8},{10,11... | collective-permute-start | bytes 786440 | tf_op jit(solution)/shard_map/ppermute | solution.py:221
  31.7 4.9 %collective-permute-start.9 = (bf16[4,4096]{1,0:T(4,128)(2,1)S(1)}, bf16[4,4096]{1,0:T(4,128)(2,1)S(1)}, u32[]{:S(2)}, u32[]{:S(2)}) collective-permute-start(bf16[4,4096]{1,0:T(4,128)(2,1)S(1)} %add_convert_fusion.rest_0_), channel_id=1, source_target_pairs={{0,12},{2,14},{4,8},{6,10},{8,4},{10,6},{12,0},{14,2},{16,28},{18,... | collective-permute-start | bytes 98312 | tf_op jit(solution)/shard_map/ppermute | solution.py:229
  34.3 3.9 %collective-permute-start.5 = (bf16[4,4096]{1,0:T(4,128)(2,1)S(1)}, bf16[4,4096]{1,0:T(4,128)(2,1)S(1)}, u32[]{:S(2)}, u32[]{:S(2)}) collective-permute-start(bf16[4,4096]{1,0:T(4,128)(2,1)S(1)} %add_convert_fusion.rest_0_), channel_id=1, source_target_pairs={{0,4},{2,6},{4,0},{6,2},{8,12},{10,14},{12,8},{14,10},{16,20},{18,... | collective-permute-start | bytes 98312 | tf_op jit(solution)/shard_map/ppermute | solution.py:229
  34.8 3.9 %collective-permute-start.7 = (bf16[4,4096]{1,0:T(4,128)(2,1)S(1)}, bf16[4,4096]{1,0:T(4,128)(2,1)S(1)}, u32[]{:S(2)}, u32[]{:S(2)}) collective-permute-start(bf16[4,4096]{1,0:T(4,128)(2,1)S(1)} %add_convert_fusion.rest_0_), channel_id=1, source_target_pairs={{0,8},{2,10},{4,12},{6,14},{8,0},{10,2},{12,4},{14,6},{16,24},{18,... | collective-permute-start | bytes 98312 | tf_op jit(solution)/shard_map/ppermute | solution.py:229
  35.3 3.5 %collective-permute-start.4 = (bf16[4,4096]{1,0:T(4,128)(2,1)S(1)}, bf16[4,4096]{1,0:T(4,128)(2,1)S(1)}, u32[]{:S(2)}, u32[]{:S(2)}) collective-permute-start(bf16[4,4096]{1,0:T(4,128)(2,1)S(1)} %add_convert_fusion.rest_0_), channel_id=1, source_target_pairs={{0,2},{2,0},{4,6},{6,4},{8,10},{10,8},{12,14},{14,12},{16,18},{18,... | collective-permute-start | bytes 98312 | tf_op jit(solution)/shard_map/ppermute | solution.py:231
  36.6 2.2 %collective-permute-start.10 = (bf16[4,4096]{1,0:T(4,128)(2,1)S(1)}, bf16[4,4096]{1,0:T(4,128)(2,1)S(1)}, u32[]{:S(2)}, u32[]{:S(2)}) collective-permute-start(bf16[4,4096]{1,0:T(4,128)(2,1)S(1)} %collective-permute-done.9.rest_6_), channel_id=1, source_target_pairs={{0,2},{2,0},{4,6},{6,4},{8,10},{10,8},{12,14},{14,12},{16,18},{18,... | collective-permute-start | bytes 98312 | tf_op jit(solution)/shard_map/ppermute | solution.py:231
  38.2 1.2 %collective-permute-start.6 = (bf16[4,4096]{1,0:T(4,128)(2,1)S(1)}, bf16[4,4096]{1,0:T(4,128)(2,1)S(1)}, u32[]{:S(2)}, u32[]{:S(2)}) collective-permute-start(bf16[4,4096]{1,0:T(4,128)(2,1)S(1)} %collective-permute-done.5.rest_2_), channel_id=1, source_target_pairs={{0,2},{2,0},{4,6},{6,4},{8,10},{10,8},{12,14},{14,12},{16,18},{18,... | collective-permute-start | bytes 98312 | tf_op jit(solution)/shard_map/ppermute | solution.py:231
  38.7 1.2 %collective-permute-start.8 = (bf16[4,4096]{1,0:T(4,128)(2,1)S(1)}, bf16[4,4096]{1,0:T(4,128)(2,1)S(1)}, u32[]{:S(2)}, u32[]{:S(2)}) collective-permute-start(bf16[4,4096]{1,0:T(4,128)(2,1)S(1)} %collective-permute-done.7.rest_4_), channel_id=1, source_target_pairs={{0,2},{2,0},{4,6},{6,4},{8,10},{10,8},{12,14},{14,12},{16,18},{18,... | collective-permute-start | bytes 98312 | tf_op jit(solution)/shard_map/ppermute | solution.py:231

commit v2 on v1

--- a/solution.py
+++ b/solution.py
@@ -12,7 +12,7 @@
 NT = (((1,), (1,)), ((), ()))
 TN = (((0,), (0,)), ((), ()))
 VMEM = pl.BlockSpec(memory_space=pltpu.VMEM)
-ANY = pl.BlockSpec(memory_space=pl.ANY)
+HBM = pl.BlockSpec(memory_space=pltpu.HBM)
 HIGH = lax.Precision.HIGHEST
 
 
@@ -20,50 +20,80 @@
     return pltpu.CompilerParams(vmem_limit_bytes=mib << 20)
 
 
-def project_kernel(chunks, x_hbm, w_ref, *rest):
-    out_ref = rest[0]
-    sent_ref = rest[1] if len(rest) == 4 else None
-    buf, sems = rest[-2:]
+def hbm(x):
+    return pltpu.with_memory_space_constraint(x, pltpu.HBM)
+
+
+def out_kernel(chunks, x_hbm, w_hbm, out_ref, sent_ref, x_ref, wide_ref, tall_ref, sems):
     rows = x_hbm.shape[0]
     step = rows // chunks
+    weights = pltpu.make_async_copy(w_hbm, wide_ref, sems.at[chunks])
+    weights.start()
     copies = [
         pltpu.make_async_copy(
-            x_hbm.at[pl.ds(c * step, step)], buf.at[pl.ds(c * step, step)], sems.at[c]
+            x_hbm.at[pl.ds(c * step, step)], x_ref.at[pl.ds(c * step, step)], sems.at[c]
         )
         for c in range(chunks)
     ]
     for copy in copies:
         copy.start()
+    weights.wait()
+    tall_ref[...] = wide_ref[...].T
     half = rows // 2
-    rank = w_ref.shape[0]
-    for c in range(chunks):
-        copies[c].wait()
-        part = lax.dot_general(
-            buf[pl.ds(c * step, step), :], w_ref[...], NT, preferred_element_type=F32
-        )
-        row, lane = (c * step) % half, (c * step) // half * rank
-        out_ref[pl.ds(row, step), pl.ds(lane, rank)] = part
-    if sent_ref is not None:
-        sent_ref[...] = out_ref[...].astype(BF16)
-
-
-def project(x, w_t, chunks, send, mib):
+    rank = w_hbm.shape[0]
+    for side in range(2):
+        for copy in copies[side * chunks // 2 : (side + 1) * chunks // 2]:
+            copy.wait()
+        part = jnp.dot(
+            x_ref[pl.ds(side * half, half), :], tall_ref[...], preferred_element_type=F32
+        )
+        out_ref[:, pl.ds(side * rank, rank)] = part
+        sent_ref[:, pl.ds(side * rank, rank)] = part.astype(BF16)
+
+
+def project_out(x, w_t, chunks):
     rows, depth = x.shape
     rank = w_t.shape[0]
     shape = (rows // 2, 2 * rank)
-    outs = [jax.ShapeDtypeStruct(shape, F32)]
-    if send:
-        outs.append(jax.ShapeDtypeStruct(shape, BF16))
-    return pl.pallas_call(
-        functools.partial(project_kernel, chunks),
-        out_shape=outs,
-        in_specs=[ANY, VMEM],
-        out_specs=[VMEM] * len(outs),
+    return pl.pallas_call(
+        functools.partial(out_kernel, chunks),
+        out_shape=[jax.ShapeDtypeStruct(shape, F32), jax.ShapeDtypeStruct(shape, BF16)],
+        in_specs=[HBM, HBM],
+        out_specs=[VMEM] * 2,
         scratch_shapes=[
             pltpu.VMEM((rows, depth), BF16),
-            pltpu.SemaphoreType.DMA((chunks,)),
+            pltpu.VMEM((rank, depth), BF16),
+            pltpu.VMEM((depth, rank), BF16),
+            pltpu.SemaphoreType.DMA((chunks + 1,)),
         ],
-        compiler_params=params(mib),
+        compiler_params=params(16),
+        cost_estimate=pl.CostEstimate(
+            flops=60 * rows * depth * rank, bytes_accessed=60 * rows * depth, transcendentals=0
+        ),
+    )(hbm(x), hbm(w_t))
+
+
+def in_kernel(x_ref, w_ref, out_ref, tall_ref):
+    half = x_ref.shape[0] // 2
+    rank = w_ref.shape[0]
+    tall_ref[...] = w_ref[...].T
+    for side in range(2):
+        part = jnp.dot(
+            x_ref[pl.ds(side * half, half), :], tall_ref[...], preferred_element_type=F32
+        )
+        out_ref[:, pl.ds(side * rank, rank)] = part
+
+
+def project_in(x, w_t):
+    rows, depth = x.shape
+    rank = w_t.shape[0]
+    return pl.pallas_call(
+        in_kernel,
+        out_shape=jax.ShapeDtypeStruct((rows // 2, 2 * rank), F32),
+        in_specs=[VMEM, VMEM],
+        out_specs=VMEM,
+        scratch_shapes=[pltpu.VMEM((depth, rank), BF16)],
+        compiler_params=params(16),
         cost_estimate=pl.CostEstimate(
             flops=2 * rows * depth * rank, bytes_accessed=2 * rows * depth, transcendentals=0
         ),
@@ -197,11 +227,9 @@
     half = ex_size // 2
     swap_hid = [(0, 1), (1, 0)]
 
-    out_own, out_sent = project(
-        out_grads.reshape(seqs * length, -1), proj_out.T, 4, True, 16
-    )
+    out_own, out_sent = project_out(out_grads.reshape(seqs * length, -1), proj_out.T, 4)
     out_got = lax.ppermute(out_sent, "hid", swap_hid)
-    (in_part,) = project(activations.reshape(seqs * length, depth), proj_in.T, 8, False, 32)
+    in_part = project_in(activations.reshape(seqs * length, depth), proj_in.T)
     part, sent = outer(in_part, out_own, out_got, token_mask, inv_input)
 
     around, across = [], []

time: 41.1 us -> 28.8 us (0.70)
  local copies, waits for them, and re-layouts: 8.16 us -> 0.03 us
  Pallas kernels: 13.5 us -> 9.34 us
  starting transfers between devices: 11.2 us -> 12.3 us
  waiting for transfers between devices: 7.78 us -> 6.82 us
    unnamed x16 -> x12, local copies, waits for them, and re-layouts: 8.16 us -> 0.03 us
    pallas_call x2, Pallas kernels: 11 us -> 6.84 us  [the longest x1 3.63 us: project_out(): pl.pallas_call(functools.partial(out_kernel, chunks), out_shape=[jax.Shap...]
    ppermute x1, starting transfers between devices: 0.05 us -> 1.27 us  [local_pair(): second = lax.ppermute(sent, axes, across)]
    ppermute x1, waiting for transfers between devices: 3.17 us -> 2.21 us  [local_pair(): second = lax.ppermute(sent, axes, across)]
  transfers between devices with their start and end apart: 11 -> 11, of which waited for: 6 -> 6; matrix products, arithmetic and copies ran while one was open for 0% -> 0% of each run, Pallas kernels for 22% -> 13%
where the time goes in v2:
time: 28.8 us; the launch traced here: 28.7 us
  starting transfers between devices  12.3 us (43%)
  Pallas kernels  9.34 us (32%)
  waiting for transfers between devices  6.82 us (24%)
    pallas_call x1, Pallas kernels, project_out(): pl.pallas_call(functools.partial(out_kernel, chunks), out_shape=[jax.Shap...  3.63 us
    ppermute x3, starting transfers between devices, local_pair(): pieces[k] = lax.ppermute(mine, 'ex', [(i, i ^ k) for i in range(ex_size)])  3.55 us
    ppermute x3, waiting for transfers between devices, local_pair(): pieces[k] = lax.ppermute(mine, 'ex', [(i, i ^ k) for i in range(ex_size)])  3.45 us
    pallas_call x1, Pallas kernels, project_in(): pl.pallas_call(in_kernel, out_shape=jax.ShapeDtypeStruct((rows // 2, 2 *...  3.21 us
    ppermute x1, starting transfers between devices, local_pair(): out_got = lax.ppermute(out_sent, 'hid', swap_hid)  3 us
    ppermute x1, starting transfers between devices, local_pair(): first = lax.ppermute(sent, axes, around)  2.73 us
    ppermute x1, waiting for transfers between devices, local_pair(): second = lax.ppermute(sent, axes, across)  2.21 us
    ppermute x1, starting transfers between devices, local_pair(): query_got = lax.ppermute(query_own, 'hid', swap_hid)  1.73 us
  transfers between devices with their start and end apart: 11, of which 6 were waited for; matrix products, arithmetic and copies ran while one was open for 0% of the time, Pallas kernels for 13%

profile of v2, /device:TPU:0, one launch (start us, length us, event | category | flops | bytes accessed | tf_op | source)
XLA Modules:
  0.0 28.7 jit_solution(7111991892372339107)
XLA Ops:
  0.0 3.6 %shard_map.84 = (f32[384,128]{1,0:T(8,128)S(1)}, bf16[384,128]{1,0:T(8,128)(2,1)S(1)}) custom-call(bf16[768,2048]{1,0:T(8,128)(2,1)} %bitcast.8, bf16[64,2048]{1,0:T(8,128)(2,1)} %bitcast.9), custom_call_target="tpu_custom_call" | custom-call | flops 6039797760 | bytes 94371840 | tf_op jit(solution)/shard_map/pallas_call | solution.py:58
  3.6 0.0 copy-start.3
  3.7 0.0 copy-start.5
  3.7 0.0 copy-start.2
  3.7 0.0 copy-start.4
  3.7 3.0 %collective-permute-start.1 = (bf16[384,128]{1,0:T(8,128)(2,1)S(1)}, bf16[384,128]{1,0:T(8,128)(2,1)S(1)}, u32[]{:S(2)}, u32[]{:S(2)}) collective-permute-start(bf16[384,128]{1,0:T(8,128)(2,1)S(1)} %get-tuple-element.10), channel_id=1, source_target_pairs={{0,1},{1,0},{2,3},{3,2},{4,5},{5,4},{6,7},{7,6},{8,9},{9,8},{10,11... | collective-permute-start | bytes 294920 | tf_op jit(solution)/shard_map/ppermute | solution.py:231
  6.7 3.2 %shard_map.83.in_ref = f32[384,128]{1,0:T(8,128)S(1)} custom-call(bf16[768,7168]{1,0:T(8,128)(2,1)S(1)} %bitcast.6, bf16[64,7168]{1,0:T(8,128)(2,1)S(1)} %bitcast.7), custom_call_target="tpu_custom_call" | custom-call | flops 704643072 | bytes 11010048 | tf_op jit(solution)/shard_map/pallas_call | solution.py:90
  9.9 1.0 %shard_map.85 = (f32[4,4096]{1,0:T(4,128)S(1)}, bf16[4,4096]{1,0:T(4,128)(2,1)S(1)}) custom-call(f32[384,128]{1,0:T(8,128)S(1)} %shard_map.83.in_ref, f32[384,128]{1,0:T(8,128)S(1)} %get-tuple-element.9.own_ref, bf16[384,128]{1,0:T(8,128)(2,1)S(1)} %collective-permute-done.1.got_ref, s32[4,192]{1,0:T(4,128)S(1)} %copy-done.5, f32[64,64]{1,0:T(8,128)S(1)} %copy-done.3), custom_call_target="tpu_custom_call" | custom-call | tf_op jit(solution)/shard_map/pallas_call | solution.py:141
  10.9 2.7 %collective-permute-start.2 = (bf16[4,4096]{1,0:T(4,128)(2,1)S(1)}, bf16[4,4096]{1,0:T(4,128)(2,1)S(1)}, u32[]{:S(2)}, u32[]{:S(2)}) collective-permute-start(bf16[4,4096]{1,0:T(4,128)(2,1)S(1)} %get-tuple-element.11), channel_id=1, source_target_pairs={{1,0},{0,16},{16,17},{17,1},{3,2},{2,18},{18,19},{19,3},{5,4},{4,2... | collective-permute-start | bytes 98312 | tf_op jit(solution)/shard_map/ppermute | solution.py:241
  13.7 1.3 %collective-permute-start.3 = (bf16[4,4096]{1,0:T(4,128)(2,1)S(1)}, bf16[4,4096]{1,0:T(4,128)(2,1)S(1)}, u32[]{:S(2)}, u32[]{:S(2)}) collective-permute-start(bf16[4,4096]{1,0:T(4,128)(2,1)S(1)} %get-tuple-element.11), channel_id=1, source_target_pairs={{1,16},{16,1},{0,17},{17,0},{3,18},{18,3},{2,19},{19,2},{5,20},{20... | collective-permute-start | bytes 98312 | tf_op jit(solution)/shard_map/ppermute | solution.py:242
  14.9 0.6 %shard_map.82 = bf16[64,2048]{1,0:T(8,128)(2,1)S(1)} custom-call(bf16[64,2048]{1,0:T(8,128)(2,1)S(1)} %copy-done.2, f32[64,64]{1,0:T(8,128)S(1)} %copy-done.4), custom_call_target="tpu_custom_call" | custom-call | tf_op jit(solution)/shard_map/pallas_call | solution.py:175
  15.5 1.7 %collective-permute-start = (bf16[64,2048]{1,0:T(8,128)(2,1)S(1)}, bf16[64,2048]{1,0:T(8,128)(2,1)S(1)}, u32[]{:S(2)}, u32[]{:S(2)}) collective-permute-start(bf16[64,2048]{1,0:T(8,128)(2,1)S(1)} %shard_map.82), channel_id=1, source_target_pairs={{0,1},{1,0},{2,3},{3,2},{4,5},{5,4},{6,7},{7,6},{8,9},{9,8},{10,11... | collective-permute-start | bytes 786440 | tf_op jit(solution)/shard_map/ppermute | solution.py:249
  17.3 0.0 collective-permute-done.2
  17.3 2.2 %collective-permute-done.3 = bf16[4,4096]{1,0:T(4,128)(2,1)S(1)} collective-permute-done((bf16[4,4096]{1,0:T(4,128)(2,1)S(1)}, bf16[4,4096]{1,0:T(4,128)(2,1)S(1)}, u32[]{:S(2)}, u32[]{:S(2)}) %collective-permute-start.3) | collective-permute-done | bytes 32800 | tf_op jit(solution)/shard_map/ppermute | solution.py:242
  19.5 2.6 %collective-permute-start.9 = (bf16[4,4096]{1,0:T(4,128)(2,1)S(1)}, bf16[4,4096]{1,0:T(4,128)(2,1)S(1)}, u32[]{:S(2)}, u32[]{:S(2)}) collective-permute-start(bf16[4,4096]{1,0:T(4,128)(2,1)S(1)} %add_convert_fusion.rest_0_), channel_id=1, source_target_pairs={{0,12},{2,14},{4,8},{6,10},{8,4},{10,6},{12,0},{14,2},{16,28},{18,... | collective-permute-start | bytes 98312 | tf_op jit(solution)/shard_map/ppermute | solution.py:257
  22.1 0.5 %collective-permute-start.5 = (bf16[4,4096]{1,0:T(4,128)(2,1)S(1)}, bf16[4,4096]{1,0:T(4,128)(2,1)S(1)}, u32[]{:S(2)}, u32[]{:S(2)}) collective-permute-start(bf16[4,4096]{1,0:T(4,128)(2,1)S(1)} %add_convert_fusion.rest_0_), channel_id=1, source_target_pairs={{0,4},{2,6},{4,0},{6,2},{8,12},{10,14},{12,8},{14,10},{16,20},{18,... | collective-permute-start | bytes 98312 | tf_op jit(solution)/shard_map/ppermute | solution.py:257
  22.6 0.4 %collective-permute-start.7 = (bf16[4,4096]{1,0:T(4,128)(2,1)S(1)}, bf16[4,4096]{1,0:T(4,128)(2,1)S(1)}, u32[]{:S(2)}, u32[]{:S(2)}) collective-permute-start(bf16[4,4096]{1,0:T(4,128)(2,1)S(1)} %add_convert_fusion.rest_0_), channel_id=1, source_target_pairs={{0,8},{2,10},{4,12},{6,14},{8,0},{10,2},{12,4},{14,6},{16,24},{18,... | collective-permute-start | bytes 98312 | tf_op jit(solution)/shard_map/ppermute | solution.py:257
  23.1 1.6 %collective-permute-done.9.rest_6_ = bf16[4,4096]{1,0:T(4,128)(2,1)S(1)} collective-permute-done((bf16[4,4096]{1,0:T(4,128)(2,1)S(1)}, bf16[4,4096]{1,0:T(4,128)(2,1)S(1)}, u32[]{:S(2)}, u32[]{:S(2)}) %collective-permute-start.9) | collective-permute-done | bytes 32800 | tf_op jit(solution)/shard_map/ppermute | solution.py:257
  24.7 1.3 %collective-permute-done.5.rest_2_ = bf16[4,4096]{1,0:T(4,128)(2,1)S(1)} collective-permute-done((bf16[4,4096]{1,0:T(4,128)(2,1)S(1)}, bf16[4,4096]{1,0:T(4,128)(2,1)S(1)}, u32[]{:S(2)}, u32[]{:S(2)}) %collective-permute-start.5) | collective-permute-done | bytes 32800 | tf_op jit(solution)/shard_map/ppermute | solution.py:257
  26.0 0.5 %collective-permute-done.7.rest_4_ = bf16[4,4096]{1,0:T(4,128)(2,1)S(1)} collective-permute-done((bf16[4,4096]{1,0:T(4,128)(2,1)S(1)}, bf16[4,4096]{1,0:T(4,128)(2,1)S(1)}, u32[]{:S(2)}, u32[]{:S(2)}) %collective-permute-start.7) | collective-permute-done | bytes 32800 | tf_op jit(solution)/shard_map/ppermute | solution.py:257
  26.5 0.0 collective-permute-start.8
  26.6 0.6 %collective-permute-done.6.rest_3_ = bf16[4,4096]{1,0:T(4,128)(2,1)S(1)} collective-permute-done((bf16[4,4096]{1,0:T(4,128)(2,1)S(1)}, bf16[4,4096]{1,0:T(4,128)(2,1)S(1)}, u32[]{:S(2)}, u32[]{:S(2)}) %collective-permute-start.6) | collective-permute-done | bytes 32800 | tf_op jit(solution)/shard_map/ppermute | solution.py:259
  27.2 0.5 %collective-permute-done.8.rest_5_ = bf16[4,4096]{1,0:T(4,128)(2,1)S(1)} collective-permute-done((bf16[4,4096]{1,0:T(4,128)(2,1)S(1)}, bf16[4,4096]{1,0:T(4,128)(2,1)S(1)}, u32[]{:S(2)}, u32[]{:S(2)}) %collective-permute-start.8) | collective-permute-done | bytes 32800 | tf_op jit(solution)/shard_map/ppermute | solution.py:259
  27.7 0.9 %shard_map.86 = f32[32,64]{1,0:T(8,128)} custom-call(s32[1]{0:T(128)} %bitcast.place_ref, bf16[64,2048]{1,0:T(8,128)(2,1)S(1)} %get-tuple-element.14.low_ref, bf16[64,2048]{1,0:T(8,128)(2,1)S(1)} %get-tuple-element.13.high_ref, bf16[4,4096]{1,0:T(4,128)(2,1)S(1)} %add_convert_fusion.rest_0_, bf16[4,4096]{1,0:T(4,128)(2,1)S(1)} %collective-permute-done.4.rest_1_, ...), custom_call_target="tpu_custom_call" | custom-call | tf_op jit(solution)/shard_map/pallas_call | solution.py:210
  (17 shorter events, 0.1 us)
Async XLA Ops:
  0.0 6.7 %copy-start = (bf16[4,192,7168]{2,1,0:T(8,128)(2,1)S(1)}, bf16[4,192,7168]{2,1,0:T(8,128)(2,1)}, u32[]{:S(2)}) copy-start(bf16[4,192,7168]{2,1,0:T(8,128)(2,1)} %param.8) | copy-start | bytes 33030148
  0.0 6.7 %copy-start.1 = (bf16[7168,64]{0,1:T(8,128)(2,1)S(1)}, bf16[7168,64]{0,1:T(8,128)(2,1)}, u32[]{:S(2)}) copy-start(bf16[7168,64]{0,1:T(8,128)(2,1)} %param.11) | copy-start | bytes 2752516
  3.6 6.3 %copy-start.3 = (f32[64,64]{1,0:T(8,128)S(1)}, f32[64,64]{1,0:T(8,128)}, u32[]{:S(2)}) copy-start(f32[64,64]{1,0:T(8,128)} %inv_ref.3) | copy-start | bytes 49156
  3.7 6.3 %copy-start.5 = (s32[4,192]{1,0:T(4,128)S(1)}, s32[4,192]{1,0:T(4,128)}, u32[]{:S(2)}) copy-start(s32[4,192]{1,0:T(4,128)} %mask_ref.1) | copy-start | bytes 9220
  3.7 11.3 %copy-start.2 = (bf16[64,2048]{1,0:T(8,128)(2,1)S(1)}, bf16[64,2048]{1,0:T(8,128)(2,1)}, u32[]{:S(2)}) copy-start(bf16[64,2048]{1,0:T(8,128)(2,1)} %query_ref.1) | copy-start | bytes 786436
  3.7 11.3 %copy-start.4 = (f32[64,64]{1,0:T(8,128)S(1)}, f32[64,64]{1,0:T(8,128)}, u32[]{:S(2)}) copy-start(f32[64,64]{1,0:T(8,128)} %inv_ref.2) | copy-start | bytes 49156
  3.7 6.2 %collective-permute-start.1 = (bf16[384,128]{1,0:T(8,128)(2,1)S(1)}, bf16[384,128]{1,0:T(8,128)(2,1)S(1)}, u32[]{:S(2)}, u32[]{:S(2)}) collective-permute-start(bf16[384,128]{1,0:T(8,128)(2,1)S(1)} %get-tuple-element.10), channel_id=1, source_target_pairs={{0,1},{1,0},{2,3},{3,2},{4,5},{5,4},{6,7},{7,6},{8,9},{9,8},{10,11... | collective-permute-start | bytes 294920 | tf_op jit(solution)/shard_map/ppermute | solution.py:231
  10.9 6.3 %collective-permute-start.2 = (bf16[4,4096]{1,0:T(4,128)(2,1)S(1)}, bf16[4,4096]{1,0:T(4,128)(2,1)S(1)}, u32[]{:S(2)}, u32[]{:S(2)}) collective-permute-start(bf16[4,4096]{1,0:T(4,128)(2,1)S(1)} %get-tuple-element.11), channel_id=1, source_target_pairs={{1,0},{0,16},{16,17},{17,1},{3,2},{2,18},{18,19},{19,3},{5,4},{4,2... | collective-permute-start | bytes 98312 | tf_op jit(solution)/shard_map/ppermute | solution.py:241
  13.7 5.8 %collective-permute-start.3 = (bf16[4,4096]{1,0:T(4,128)(2,1)S(1)}, bf16[4,4096]{1,0:T(4,128)(2,1)S(1)}, u32[]{:S(2)}, u32[]{:S(2)}) collective-permute-start(bf16[4,4096]{1,0:T(4,128)(2,1)S(1)} %get-tuple-element.11), channel_id=1, source_target_pairs={{1,16},{16,1},{0,17},{17,0},{3,18},{18,3},{2,19},{19,2},{5,20},{20... | collective-permute-start | bytes 98312 | tf_op jit(solution)/shard_map/ppermute | solution.py:242
  15.5 11.0 %collective-permute-start = (bf16[64,2048]{1,0:T(8,128)(2,1)S(1)}, bf16[64,2048]{1,0:T(8,128)(2,1)S(1)}, u32[]{:S(2)}, u32[]{:S(2)}) collective-permute-start(bf16[64,2048]{1,0:T(8,128)(2,1)S(1)} %shard_map.82), channel_id=1, source_target_pairs={{0,1},{1,0},{2,3},{3,2},{4,5},{5,4},{6,7},{7,6},{8,9},{9,8},{10,11... | collective-permute-start | bytes 786440 | tf_op jit(solution)/shard_map/ppermute | solution.py:249
  19.5 5.2 %collective-permute-start.9 = (bf16[4,4096]{1,0:T(4,128)(2,1)S(1)}, bf16[4,4096]{1,0:T(4,128)(2,1)S(1)}, u32[]{:S(2)}, u32[]{:S(2)}) collective-permute-start(bf16[4,4096]{1,0:T(4,128)(2,1)S(1)} %add_convert_fusion.rest_0_), channel_id=1, source_target_pairs={{0,12},{2,14},{4,8},{6,10},{8,4},{10,6},{12,0},{14,2},{16,28},{18,... | collective-permute-start | bytes 98312 | tf_op jit(solution)/shard_map/ppermute | solution.py:257
  22.1 3.9 %collective-permute-start.5 = (bf16[4,4096]{1,0:T(4,128)(2,1)S(1)}, bf16[4,4096]{1,0:T(4,128)(2,1)S(1)}, u32[]{:S(2)}, u32[]{:S(2)}) collective-permute-start(bf16[4,4096]{1,0:T(4,128)(2,1)S(1)} %add_convert_fusion.rest_0_), channel_id=1, source_target_pairs={{0,4},{2,6},{4,0},{6,2},{8,12},{10,14},{12,8},{14,10},{16,20},{18,... | collective-permute-start | bytes 98312 | tf_op jit(solution)/shard_map/ppermute | solution.py:257
  22.6 3.9 %collective-permute-start.7 = (bf16[4,4096]{1,0:T(4,128)(2,1)S(1)}, bf16[4,4096]{1,0:T(4,128)(2,1)S(1)}, u32[]{:S(2)}, u32[]{:S(2)}) collective-permute-start(bf16[4,4096]{1,0:T(4,128)(2,1)S(1)} %add_convert_fusion.rest_0_), channel_id=1, source_target_pairs={{0,8},{2,10},{4,12},{6,14},{8,0},{10,2},{12,4},{14,6},{16,24},{18,... | collective-permute-start | bytes 98312 | tf_op jit(solution)/shard_map/ppermute | solution.py:257
  23.1 3.5 %collective-permute-start.4 = (bf16[4,4096]{1,0:T(4,128)(2,1)S(1)}, bf16[4,4096]{1,0:T(4,128)(2,1)S(1)}, u32[]{:S(2)}, u32[]{:S(2)}) collective-permute-start(bf16[4,4096]{1,0:T(4,128)(2,1)S(1)} %add_convert_fusion.rest_0_), channel_id=1, source_target_pairs={{0,2},{2,0},{4,6},{6,4},{8,10},{10,8},{12,14},{14,12},{16,18},{18,... | collective-permute-start | bytes 98312 | tf_op jit(solution)/shard_map/ppermute | solution.py:259
  24.7 1.9 %collective-permute-start.10 = (bf16[4,4096]{1,0:T(4,128)(2,1)S(1)}, bf16[4,4096]{1,0:T(4,128)(2,1)S(1)}, u32[]{:S(2)}, u32[]{:S(2)}) collective-permute-start(bf16[4,4096]{1,0:T(4,128)(2,1)S(1)} %collective-permute-done.9.rest_6_), channel_id=1, source_target_pairs={{0,2},{2,0},{4,6},{6,4},{8,10},{10,8},{12,14},{14,12},{16,18},{18,... | collective-permute-start | bytes 98312 | tf_op jit(solution)/shard_map/ppermute | solution.py:259
  26.0 1.2 %collective-permute-start.6 = (bf16[4,4096]{1,0:T(4,128)(2,1)S(1)}, bf16[4,4096]{1,0:T(4,128)(2,1)S(1)}, u32[]{:S(2)}, u32[]{:S(2)}) collective-permute-start(bf16[4,4096]{1,0:T(4,128)(2,1)S(1)} %collective-permute-done.5.rest_2_), channel_id=1, source_target_pairs={{0,2},{2,0},{4,6},{6,4},{8,10},{10,8},{12,14},{14,12},{16,18},{18,... | collective-permute-start | bytes 98312 | tf_op jit(solution)/shard_map/ppermute | solution.py:259
  26.5 1.2 %collective-permute-start.8 = (bf16[4,4096]{1,0:T(4,128)(2,1)S(1)}, bf16[4,4096]{1,0:T(4,128)(2,1)S(1)}, u32[]{:S(2)}, u32[]{:S(2)}) collective-permute-start(bf16[4,4096]{1,0:T(4,128)(2,1)S(1)} %collective-permute-done.7.rest_4_), channel_id=1, source_target_pairs={{0,2},{2,0},{4,6},{6,4},{8,10},{10,8},{12,14},{14,12},{16,18},{18,... | collective-permute-start | bytes 98312 | tf_op jit(solution)/shard_map/ppermute | solution.py:259

commit v3 on v2

--- a/solution.py
+++ b/solution.py
@@ -188,17 +188,17 @@
         feats_ref[pl.ds(k * seqs, seqs), :] = piece[...].astype(F32)
     half = low_ref.shape[1]
     feats = feats_ref[...].astype(BF16)
-    scores = lax.dot_general(feats[:, :half], low_ref[...], NT, preferred_element_type=F32)
-    scores += lax.dot_general(feats[:, half:], high_ref[...], NT, preferred_element_type=F32)
+    scores = lax.dot_general(low_ref[...], feats[:, :half], NT, preferred_element_type=F32)
+    scores += lax.dot_general(high_ref[...], feats[:, half:], NT, preferred_element_type=F32)
+    scores = scores.T
     rows = scores.shape[0]
     at = lax.broadcasted_iota(jnp.int32, scores.shape, 0)
-    place = place_ref[0]
     size = seqs
     while size < rows:
         swapped = jnp.where(
             (at & size) == 0, pltpu.roll(scores, rows - size, 0), pltpu.roll(scores, size, 0)
         )
-        bit = (place & (size // seqs)) != 0
+        bit = (place_ref[...] & (size // seqs)) != 0
         scores = jnp.where(bit, swapped, scores)
         size *= 2
     out_ref[...] = scores
@@ -210,7 +210,7 @@
     return pl.pallas_call(
         score_kernel,
         out_shape=jax.ShapeDtypeStruct((rows, low.shape[0]), F32),
-        in_specs=[pl.BlockSpec(memory_space=pltpu.SMEM)] + [VMEM] * (2 + len(pieces)),
+        in_specs=[VMEM] * (3 + len(pieces)),
         out_specs=VMEM,
         scratch_shapes=[pltpu.VMEM((rows, feats), F32)],
         compiler_params=params(16),
@@ -238,11 +238,11 @@
         around += [(a, b), (b, c), (c, d), (d, a)]
         across += [(a, c), (c, a), (b, d), (d, b)]
     axes = ("ex", "hid")
+    second = lax.ppermute(sent, axes, across)
     first = lax.ppermute(sent, axes, around)
-    second = lax.ppermute(sent, axes, across)
     home = (ex // half) == hid
     mine = (
-        first.astype(F32) + jnp.where(home, part, second.astype(F32))
+        jnp.where(home, part, second.astype(F32)) + first.astype(F32)
     ).astype(BF16)
 
     query_own = precondition_queries(query_feats, inv_output)
@@ -257,7 +257,7 @@
         pieces[k] = lax.ppermute(mine, "ex", [(i, i ^ k) for i in range(ex_size)])
     for k in list(pieces):
         pieces[k ^ 1] = lax.ppermute(pieces[k], "ex", [(i, i ^ 1) for i in range(ex_size)])
-    place = (ex % half).astype(jnp.int32).reshape(1)
+    place = jnp.full((seqs * half, query_feats.shape[0]), ex % half, jnp.int32)
     scores = score(place, low, high, [pieces[k] for k in range(half)])
     return scores.T
 

time: 28.8 us -> 28.2 us (0.979)
  waiting for transfers between devices: 6.82 us -> 6.15 us
    ppermute x1, starting transfers between devices: 1.27 us -> 3.67 us  [local_pair(): second = lax.ppermute(sent, axes, across)]
    ppermute x1, starting transfers between devices: 2.73 us -> 0.34 us  [local_pair(): first = lax.ppermute(sent, axes, around)]
    ppermute x1, waiting for transfers between devices: 2.21 us -> 0.01 us  [local_pair(): second = lax.ppermute(sent, axes, across)]
    ppermute x1, waiting for transfers between devices: 0.01 us -> 1.54 us  [local_pair(): first = lax.ppermute(sent, axes, around)]
  transfers between devices with their start and end apart: 11 -> 11, of which waited for: 6 -> 6; matrix products, arithmetic and copies ran while one was open for 0% -> 0% of each run, Pallas kernels for 13% -> 14%
where the time goes in v3:
time: 28.2 us; the launch traced here: 28.1 us
  starting transfers between devices  12.3 us (44%)
  Pallas kernels  9.4 us (33%)
  waiting for transfers between devices  6.15 us (22%)
    ppermute x1, starting transfers between devices, local_pair(): second = lax.ppermute(sent, axes, across)  3.67 us
    pallas_call x1, Pallas kernels, project_out(): pl.pallas_call(functools.partial(out_kernel, chunks), out_shape=[jax.Shap...  3.63 us
    ppermute x3, starting transfers between devices, local_pair(): pieces[k] = lax.ppermute(mine, 'ex', [(i, i ^ k) for i in range(ex_size)])  3.55 us
    ppermute x3, waiting for transfers between devices, local_pair(): pieces[k] = lax.ppermute(mine, 'ex', [(i, i ^ k) for i in range(ex_size)])  3.46 us
    pallas_call x1, Pallas kernels, project_in(): pl.pallas_call(in_kernel, out_shape=jax.ShapeDtypeStruct((rows // 2, 2 *...  3.21 us
    ppermute x1, starting transfers between devices, local_pair(): out_got = lax.ppermute(out_sent, 'hid', swap_hid)  3 us
    ppermute x1, starting transfers between devices, local_pair(): query_got = lax.ppermute(query_own, 'hid', swap_hid)  1.72 us
    ppermute x1, waiting for transfers between devices, local_pair(): first = lax.ppermute(sent, axes, around)  1.54 us
  transfers between devices with their start and end apart: 11, of which 6 were waited for; matrix products, arithmetic and copies ran while one was open for 0% of the time, Pallas kernels for 14%

profile of v3, /device:TPU:0, one launch (start us, length us, event | category | flops | bytes accessed | tf_op | source)
XLA Modules:
  0.0 28.1 jit_solution(3063801027376461254)
XLA Ops:
  0.0 3.6 %shard_map.84 = (f32[384,128]{1,0:T(8,128)S(1)}, bf16[384,128]{1,0:T(8,128)(2,1)S(1)}) custom-call(bf16[768,2048]{1,0:T(8,128)(2,1)} %bitcast.7, bf16[64,2048]{1,0:T(8,128)(2,1)} %bitcast.8), custom_call_target="tpu_custom_call" | custom-call | flops 6039797760 | bytes 94371840 | tf_op jit(solution)/shard_map/pallas_call | solution.py:58
  3.6 0.0 copy-start.3
  3.7 0.0 copy-start.5
  3.7 0.0 copy-start.2
  3.7 0.0 copy-start.4
  3.7 3.0 %collective-permute-start.1 = (bf16[384,128]{1,0:T(8,128)(2,1)S(1)}, bf16[384,128]{1,0:T(8,128)(2,1)S(1)}, u32[]{:S(2)}, u32[]{:S(2)}) collective-permute-start(bf16[384,128]{1,0:T(8,128)(2,1)S(1)} %get-tuple-element.10), channel_id=1, source_target_pairs={{0,1},{1,0},{2,3},{3,2},{4,5},{5,4},{6,7},{7,6},{8,9},{9,8},{10,11... | collective-permute-start | bytes 294920 | tf_op jit(solution)/shard_map/ppermute | solution.py:231
  6.7 3.2 %shard_map.83.in_ref = f32[384,128]{1,0:T(8,128)S(1)} custom-call(bf16[768,7168]{1,0:T(8,128)(2,1)S(1)} %bitcast.5, bf16[64,7168]{1,0:T(8,128)(2,1)S(1)} %bitcast.6), custom_call_target="tpu_custom_call" | custom-call | flops 704643072 | bytes 11010048 | tf_op jit(solution)/shard_map/pallas_call | solution.py:90
  9.9 0.0 collective-permute-done.1.got_ref
  9.9 1.0 %shard_map.85 = (f32[4,4096]{1,0:T(4,128)S(1)}, bf16[4,4096]{1,0:T(4,128)(2,1)S(1)}) custom-call(f32[384,128]{1,0:T(8,128)S(1)} %shard_map.83.in_ref, f32[384,128]{1,0:T(8,128)S(1)} %get-tuple-element.9.own_ref, bf16[384,128]{1,0:T(8,128)(2,1)S(1)} %collective-permute-done.1.got_ref, s32[4,192]{1,0:T(4,128)S(1)} %copy-done.5, f32[64,64]{1,0:T(8,128)S(1)} %copy-done.3), custom_call_target="tpu_custom_call" | custom-call | tf_op jit(solution)/shard_map/pallas_call | solution.py:141
  10.9 3.7 %collective-permute-start.2 = (bf16[4,4096]{1,0:T(4,128)(2,1)S(1)}, bf16[4,4096]{1,0:T(4,128)(2,1)S(1)}, u32[]{:S(2)}, u32[]{:S(2)}) collective-permute-start(bf16[4,4096]{1,0:T(4,128)(2,1)S(1)} %get-tuple-element.12), channel_id=1, source_target_pairs={{1,16},{16,1},{0,17},{17,0},{3,18},{18,3},{2,19},{19,2},{5,20},{20... | collective-permute-start | bytes 98312 | tf_op jit(solution)/shard_map/ppermute | solution.py:241
  14.6 0.3 %collective-permute-start.3 = (bf16[4,4096]{1,0:T(4,128)(2,1)S(1)}, bf16[4,4096]{1,0:T(4,128)(2,1)S(1)}, u32[]{:S(2)}, u32[]{:S(2)}) collective-permute-start(bf16[4,4096]{1,0:T(4,128)(2,1)S(1)} %get-tuple-element.12), channel_id=1, source_target_pairs={{1,0},{0,16},{16,17},{17,1},{3,2},{2,18},{18,19},{19,3},{5,4},{4,2... | collective-permute-start | bytes 98312 | tf_op jit(solution)/shard_map/ppermute | solution.py:242
  15.0 0.6 %shard_map.82 = bf16[64,2048]{1,0:T(8,128)(2,1)S(1)} custom-call(bf16[64,2048]{1,0:T(8,128)(2,1)S(1)} %copy-done.2, f32[64,64]{1,0:T(8,128)S(1)} %copy-done.4), custom_call_target="tpu_custom_call" | custom-call | tf_op jit(solution)/shard_map/pallas_call | solution.py:175
  15.6 1.7 %collective-permute-start = (bf16[64,2048]{1,0:T(8,128)(2,1)S(1)}, bf16[64,2048]{1,0:T(8,128)(2,1)S(1)}, u32[]{:S(2)}, u32[]{:S(2)}) collective-permute-start(bf16[64,2048]{1,0:T(8,128)(2,1)S(1)} %shard_map.82), channel_id=1, source_target_pairs={{0,1},{1,0},{2,3},{3,2},{4,5},{5,4},{6,7},{7,6},{8,9},{9,8},{10,11... | collective-permute-start | bytes 786440 | tf_op jit(solution)/shard_map/ppermute | solution.py:249
  17.3 1.5 %collective-permute-done.3 = bf16[4,4096]{1,0:T(4,128)(2,1)S(1)} collective-permute-done((bf16[4,4096]{1,0:T(4,128)(2,1)S(1)}, bf16[4,4096]{1,0:T(4,128)(2,1)S(1)}, u32[]{:S(2)}, u32[]{:S(2)}) %collective-permute-start.3) | collective-permute-done | bytes 32800 | tf_op jit(solution)/shard_map/ppermute | solution.py:242
  18.9 2.6 %collective-permute-start.9 = (bf16[4,4096]{1,0:T(4,128)(2,1)S(1)}, bf16[4,4096]{1,0:T(4,128)(2,1)S(1)}, u32[]{:S(2)}, u32[]{:S(2)}) collective-permute-start(bf16[4,4096]{1,0:T(4,128)(2,1)S(1)} %add_convert_fusion.rest_0_), channel_id=1, source_target_pairs={{0,12},{2,14},{4,8},{6,10},{8,4},{10,6},{12,0},{14,2},{16,28},{18,... | collective-permute-start | bytes 98312 | tf_op jit(solution)/shard_map/ppermute | solution.py:257
  21.5 0.5 %collective-permute-start.5 = (bf16[4,4096]{1,0:T(4,128)(2,1)S(1)}, bf16[4,4096]{1,0:T(4,128)(2,1)S(1)}, u32[]{:S(2)}, u32[]{:S(2)}) collective-permute-start(bf16[4,4096]{1,0:T(4,128)(2,1)S(1)} %add_convert_fusion.rest_0_), channel_id=1, source_target_pairs={{0,4},{2,6},{4,0},{6,2},{8,12},{10,14},{12,8},{14,10},{16,20},{18,... | collective-permute-start | bytes 98312 | tf_op jit(solution)/shard_map/ppermute | solution.py:257
  22.0 0.4 %collective-permute-start.7 = (bf16[4,4096]{1,0:T(4,128)(2,1)S(1)}, bf16[4,4096]{1,0:T(4,128)(2,1)S(1)}, u32[]{:S(2)}, u32[]{:S(2)}) collective-permute-start(bf16[4,4096]{1,0:T(4,128)(2,1)S(1)} %add_convert_fusion.rest_0_), channel_id=1, source_target_pairs={{0,8},{2,10},{4,12},{6,14},{8,0},{10,2},{12,4},{14,6},{16,24},{18,... | collective-permute-start | bytes 98312 | tf_op jit(solution)/shard_map/ppermute | solution.py:257
  22.4 1.4 %collective-permute-done.9.rest_6_ = bf16[4,4096]{1,0:T(4,128)(2,1)S(1)} collective-permute-done((bf16[4,4096]{1,0:T(4,128)(2,1)S(1)}, bf16[4,4096]{1,0:T(4,128)(2,1)S(1)}, u32[]{:S(2)}, u32[]{:S(2)}) %collective-permute-start.9) | collective-permute-done | bytes 32800 | tf_op jit(solution)/shard_map/ppermute | solution.py:257
  23.8 1.6 %collective-permute-done.5.rest_2_ = bf16[4,4096]{1,0:T(4,128)(2,1)S(1)} collective-permute-done((bf16[4,4096]{1,0:T(4,128)(2,1)S(1)}, bf16[4,4096]{1,0:T(4,128)(2,1)S(1)}, u32[]{:S(2)}, u32[]{:S(2)}) %collective-permute-start.5) | collective-permute-done | bytes 32800 | tf_op jit(solution)/shard_map/ppermute | solution.py:257
  25.4 0.5 %collective-permute-done.7.rest_4_ = bf16[4,4096]{1,0:T(4,128)(2,1)S(1)} collective-permute-done((bf16[4,4096]{1,0:T(4,128)(2,1)S(1)}, bf16[4,4096]{1,0:T(4,128)(2,1)S(1)}, u32[]{:S(2)}, u32[]{:S(2)}) %collective-permute-start.7) | collective-permute-done | bytes 32800 | tf_op jit(solution)/shard_map/ppermute | solution.py:257
  25.9 0.0 collective-permute-start.8
  26.0 0.6 %collective-permute-done.6.rest_3_ = bf16[4,4096]{1,0:T(4,128)(2,1)S(1)} collective-permute-done((bf16[4,4096]{1,0:T(4,128)(2,1)S(1)}, bf16[4,4096]{1,0:T(4,128)(2,1)S(1)}, u32[]{:S(2)}, u32[]{:S(2)}) %collective-permute-start.6) | collective-permute-done | bytes 32800 | tf_op jit(solution)/shard_map/ppermute | solution.py:259
  26.6 0.5 %collective-permute-done.8.rest_5_ = bf16[4,4096]{1,0:T(4,128)(2,1)S(1)} collective-permute-done((bf16[4,4096]{1,0:T(4,128)(2,1)S(1)}, bf16[4,4096]{1,0:T(4,128)(2,1)S(1)}, u32[]{:S(2)}, u32[]{:S(2)}) %collective-permute-start.8) | collective-permute-done | bytes 32800 | tf_op jit(solution)/shard_map/ppermute | solution.py:259
  27.1 1.0 %shard_map.86 = f32[32,64]{1,0:T(8,128)} custom-call(s32[32,64]{1,0:T(8,128)S(1)} %broadcast_in_dim.3.place_ref, bf16[64,2048]{1,0:T(8,128)(2,1)S(1)} %get-tuple-element.14.low_ref, bf16[64,2048]{1,0:T(8,128)(2,1)S(1)} %get-tuple-element.13.high_ref, bf16[4,4096]{1,0:T(4,128)(2,1)S(1)} %add_convert_fusion.rest_0_, ...), custom_call_target="tpu_custom_call" | custom-call | tf_op jit(solution)/shard_map/pallas_call | solution.py:210
  (18 shorter events, 0.1 us)
Async XLA Ops:
  0.0 6.7 %copy-start = (bf16[4,192,7168]{2,1,0:T(8,128)(2,1)S(1)}, bf16[4,192,7168]{2,1,0:T(8,128)(2,1)}, u32[]{:S(2)}) copy-start(bf16[4,192,7168]{2,1,0:T(8,128)(2,1)} %param.8) | copy-start | bytes 33030148
  0.0 6.7 %copy-start.1 = (bf16[7168,64]{0,1:T(8,128)(2,1)S(1)}, bf16[7168,64]{0,1:T(8,128)(2,1)}, u32[]{:S(2)}) copy-start(bf16[7168,64]{0,1:T(8,128)(2,1)} %param.11) | copy-start | bytes 2752516
  3.6 6.3 %copy-start.3 = (f32[64,64]{1,0:T(8,128)S(1)}, f32[64,64]{1,0:T(8,128)}, u32[]{:S(2)}) copy-start(f32[64,64]{1,0:T(8,128)} %inv_ref.3) | copy-start | bytes 49156
  3.7 6.3 %copy-start.5 = (s32[4,192]{1,0:T(4,128)S(1)}, s32[4,192]{1,0:T(4,128)}, u32[]{:S(2)}) copy-start(s32[4,192]{1,0:T(4,128)} %mask_ref.1) | copy-start | bytes 9220
  3.7 11.3 %copy-start.2 = (bf16[64,2048]{1,0:T(8,128)(2,1)S(1)}, bf16[64,2048]{1,0:T(8,128)(2,1)}, u32[]{:S(2)}) copy-start(bf16[64,2048]{1,0:T(8,128)(2,1)} %query_ref.1) | copy-start | bytes 786436
  3.7 11.3 %copy-start.4 = (f32[64,64]{1,0:T(8,128)S(1)}, f32[64,64]{1,0:T(8,128)}, u32[]{:S(2)}) copy-start(f32[64,64]{1,0:T(8,128)} %inv_ref.2) | copy-start | bytes 49156
  3.7 6.2 %collective-permute-start.1 = (bf16[384,128]{1,0:T(8,128)(2,1)S(1)}, bf16[384,128]{1,0:T(8,128)(2,1)S(1)}, u32[]{:S(2)}, u32[]{:S(2)}) collective-permute-start(bf16[384,128]{1,0:T(8,128)(2,1)S(1)} %get-tuple-element.10), channel_id=1, source_target_pairs={{0,1},{1,0},{2,3},{3,2},{4,5},{5,4},{6,7},{7,6},{8,9},{9,8},{10,11... | collective-permute-start | bytes 294920 | tf_op jit(solution)/shard_map/ppermute | solution.py:231
  10.9 6.3 %collective-permute-start.2 = (bf16[4,4096]{1,0:T(4,128)(2,1)S(1)}, bf16[4,4096]{1,0:T(4,128)(2,1)S(1)}, u32[]{:S(2)}, u32[]{:S(2)}) collective-permute-start(bf16[4,4096]{1,0:T(4,128)(2,1)S(1)} %get-tuple-element.12), channel_id=1, source_target_pairs={{1,16},{16,1},{0,17},{17,0},{3,18},{18,3},{2,19},{19,2},{5,20},{20... | collective-permute-start | bytes 98312 | tf_op jit(solution)/shard_map/ppermute | solution.py:241
  14.6 4.2 %collective-permute-start.3 = (bf16[4,4096]{1,0:T(4,128)(2,1)S(1)}, bf16[4,4096]{1,0:T(4,128)(2,1)S(1)}, u32[]{:S(2)}, u32[]{:S(2)}) collective-permute-start(bf16[4,4096]{1,0:T(4,128)(2,1)S(1)} %get-tuple-element.12), channel_id=1, source_target_pairs={{1,0},{0,16},{16,17},{17,1},{3,2},{2,18},{18,19},{19,3},{5,4},{4,2... | collective-permute-start | bytes 98312 | tf_op jit(solution)/shard_map/ppermute | solution.py:242
  15.6 10.3 %collective-permute-start = (bf16[64,2048]{1,0:T(8,128)(2,1)S(1)}, bf16[64,2048]{1,0:T(8,128)(2,1)S(1)}, u32[]{:S(2)}, u32[]{:S(2)}) collective-permute-start(bf16[64,2048]{1,0:T(8,128)(2,1)S(1)} %shard_map.82), channel_id=1, source_target_pairs={{0,1},{1,0},{2,3},{3,2},{4,5},{5,4},{6,7},{7,6},{8,9},{9,8},{10,11... | collective-permute-start | bytes 786440 | tf_op jit(solution)/shard_map/ppermute | solution.py:249
  18.9 5.0 %collective-permute-start.9 = (bf16[4,4096]{1,0:T(4,128)(2,1)S(1)}, bf16[4,4096]{1,0:T(4,128)(2,1)S(1)}, u32[]{:S(2)}, u32[]{:S(2)}) collective-permute-start(bf16[4,4096]{1,0:T(4,128)(2,1)S(1)} %add_convert_fusion.rest_0_), channel_id=1, source_target_pairs={{0,12},{2,14},{4,8},{6,10},{8,4},{10,6},{12,0},{14,2},{16,28},{18,... | collective-permute-start | bytes 98312 | tf_op jit(solution)/shard_map/ppermute | solution.py:257
  21.5 3.9 %collective-permute-start.5 = (bf16[4,4096]{1,0:T(4,128)(2,1)S(1)}, bf16[4,4096]{1,0:T(4,128)(2,1)S(1)}, u32[]{:S(2)}, u32[]{:S(2)}) collective-permute-start(bf16[4,4096]{1,0:T(4,128)(2,1)S(1)} %add_convert_fusion.rest_0_), channel_id=1, source_target_pairs={{0,4},{2,6},{4,0},{6,2},{8,12},{10,14},{12,8},{14,10},{16,20},{18,... | collective-permute-start | bytes 98312 | tf_op jit(solution)/shard_map/ppermute | solution.py:257
  22.0 3.9 %collective-permute-start.7 = (bf16[4,4096]{1,0:T(4,128)(2,1)S(1)}, bf16[4,4096]{1,0:T(4,128)(2,1)S(1)}, u32[]{:S(2)}, u32[]{:S(2)}) collective-permute-start(bf16[4,4096]{1,0:T(4,128)(2,1)S(1)} %add_convert_fusion.rest_0_), channel_id=1, source_target_pairs={{0,8},{2,10},{4,12},{6,14},{8,0},{10,2},{12,4},{14,6},{16,24},{18,... | collective-permute-start | bytes 98312 | tf_op jit(solution)/shard_map/ppermute | solution.py:257
  22.4 3.5 %collective-permute-start.4 = (bf16[4,4096]{1,0:T(4,128)(2,1)S(1)}, bf16[4,4096]{1,0:T(4,128)(2,1)S(1)}, u32[]{:S(2)}, u32[]{:S(2)}) collective-permute-start(bf16[4,4096]{1,0:T(4,128)(2,1)S(1)} %add_convert_fusion.rest_0_), channel_id=1, source_target_pairs={{0,2},{2,0},{4,6},{6,4},{8,10},{10,8},{12,14},{14,12},{16,18},{18,... | collective-permute-start | bytes 98312 | tf_op jit(solution)/shard_map/ppermute | solution.py:259
  23.8 2.1 %collective-permute-start.10 = (bf16[4,4096]{1,0:T(4,128)(2,1)S(1)}, bf16[4,4096]{1,0:T(4,128)(2,1)S(1)}, u32[]{:S(2)}, u32[]{:S(2)}) collective-permute-start(bf16[4,4096]{1,0:T(4,128)(2,1)S(1)} %collective-permute-done.9.rest_6_), channel_id=1, source_target_pairs={{0,2},{2,0},{4,6},{6,4},{8,10},{10,8},{12,14},{14,12},{16,18},{18,... | collective-permute-start | bytes 98312 | tf_op jit(solution)/shard_map/ppermute | solution.py:259
  25.4 1.2 %collective-permute-start.6 = (bf16[4,4096]{1,0:T(4,128)(2,1)S(1)}, bf16[4,4096]{1,0:T(4,128)(2,1)S(1)}, u32[]{:S(2)}, u32[]{:S(2)}) collective-permute-start(bf16[4,4096]{1,0:T(4,128)(2,1)S(1)} %collective-permute-done.5.rest_2_), channel_id=1, source_target_pairs={{0,2},{2,0},{4,6},{6,4},{8,10},{10,8},{12,14},{14,12},{16,18},{18,... | collective-permute-start | bytes 98312 | tf_op jit(solution)/shard_map/ppermute | solution.py:259
  25.9 1.2 %collective-permute-start.8 = (bf16[4,4096]{1,0:T(4,128)(2,1)S(1)}, bf16[4,4096]{1,0:T(4,128)(2,1)S(1)}, u32[]{:S(2)}, u32[]{:S(2)}) collective-permute-start(bf16[4,4096]{1,0:T(4,128)(2,1)S(1)} %collective-permute-done.7.rest_4_), channel_id=1, source_target_pairs={{0,2},{2,0},{4,6},{6,4},{8,10},{10,8},{12,14},{14,12},{16,18},{18,... | collective-permute-start | bytes 98312 | tf_op jit(solution)/shard_map/ppermute | solution.py:259

commit v4 on v3

--- a/solution.py
+++ b/solution.py
@@ -236,13 +236,13 @@
     for e in range(half):
         a, b, c, d = 2 * e + 1, 2 * e, 2 * (e + half), 2 * (e + half) + 1
         around += [(a, b), (b, c), (c, d), (d, a)]
-        across += [(a, c), (c, a), (b, d), (d, b)]
+        across += [(a, c), (c, a), (b, b ^ 2), (d, d ^ 2)]
     axes = ("ex", "hid")
     second = lax.ppermute(sent, axes, across)
     first = lax.ppermute(sent, axes, around)
     home = (ex // half) == hid
     mine = (
-        jnp.where(home, part, second.astype(F32)) + first.astype(F32)
+        first.astype(F32) + jnp.where(home, part, second.astype(F32))
     ).astype(BF16)
 
     query_own = precondition_queries(query_feats, inv_output)

time: 28.2 us -> 26.9 us (0.954)
  waiting for transfers between devices: 6.15 us -> 4.6 us
    ppermute x1, starting transfers between devices: 3.67 us -> 0.01 us  [local_pair(): second = lax.ppermute(sent, axes, across)]
    ppermute x1, starting transfers between devices: 0.34 us -> 2.73 us  [local_pair(): first = lax.ppermute(sent, axes, around)]
    ppermute x1, waiting for transfers between devices: 1.54 us -> 0.01 us  [local_pair(): first = lax.ppermute(sent, axes, around)]
    ppermute x1, starting transfers between devices: 1.72 us -> 2.99 us  [local_pair(): query_got = lax.ppermute(query_own, 'hid', swap_hid)]
  transfers between devices with their start and end apart: 11 -> 11, of which waited for: 6 -> 5; matrix products, arithmetic and copies ran while one was open for 0% -> 0% of each run, Pallas kernels for 14% -> 14%
where the time goes in v4:
time: 26.9 us; the launch traced here: 26.5 us
  starting transfers between devices  12.3 us (46%)
  Pallas kernels  9.4 us (35%)
  waiting for transfers between devices  4.6 us (17%)
    pallas_call x1, Pallas kernels, project_out(): pl.pallas_call(functools.partial(out_kernel, chunks), out_shape=[jax.Shap...  3.63 us
    ppermute x3, starting transfers between devices, local_pair(): pieces[k] = lax.ppermute(mine, 'ex', [(i, i ^ k) for i in range(ex_size)])  3.55 us
    ppermute x3, waiting for transfers between devices, local_pair(): pieces[k] = lax.ppermute(mine, 'ex', [(i, i ^ k) for i in range(ex_size)])  3.45 us
    pallas_call x1, Pallas kernels, project_in(): pl.pallas_call(in_kernel, out_shape=jax.ShapeDtypeStruct((rows // 2, 2 *...  3.21 us
    ppermute x1, starting transfers between devices, local_pair(): out_got = lax.ppermute(out_sent, 'hid', swap_hid)  3 us
    ppermute x1, starting transfers between devices, local_pair(): query_got = lax.ppermute(query_own, 'hid', swap_hid)  2.99 us
    ppermute x1, starting transfers between devices, local_pair(): first = lax.ppermute(sent, axes, around)  2.73 us
    ppermute x4, waiting for transfers between devices, local_pair(): lax.ppermute(pieces[k], 'ex', [(i, i ^ 1) for i in range(ex_size)])  1.14 us
  transfers between devices with their start and end apart: 11, of which 5 were waited for; matrix products, arithmetic and copies ran while one was open for 0% of the time, Pallas kernels for 14%

profile of v4, /device:TPU:0, one launch (start us, length us, event | category | flops | bytes accessed | tf_op | source)
XLA Modules:
  0.0 26.5 jit_solution(100365188720709786)
XLA Ops:
  0.0 3.6 %shard_map.84 = (f32[384,128]{1,0:T(8,128)S(1)}, bf16[384,128]{1,0:T(8,128)(2,1)S(1)}) custom-call(bf16[768,2048]{1,0:T(8,128)(2,1)} %bitcast.7, bf16[64,2048]{1,0:T(8,128)(2,1)} %bitcast.8), custom_call_target="tpu_custom_call" | custom-call | flops 6039797760 | bytes 94371840 | tf_op jit(solution)/shard_map/pallas_call | solution.py:58
  3.6 0.0 copy-start.3
  3.7 0.0 copy-start.5
  3.7 0.0 copy-start.2
  3.7 0.0 copy-start.4
  3.7 3.0 %collective-permute-start.1 = (bf16[384,128]{1,0:T(8,128)(2,1)S(1)}, bf16[384,128]{1,0:T(8,128)(2,1)S(1)}, u32[]{:S(2)}, u32[]{:S(2)}) collective-permute-start(bf16[384,128]{1,0:T(8,128)(2,1)S(1)} %get-tuple-element.10), channel_id=1, source_target_pairs={{0,1},{1,0},{2,3},{3,2},{4,5},{5,4},{6,7},{7,6},{8,9},{9,8},{10,11... | collective-permute-start | bytes 294920 | tf_op jit(solution)/shard_map/ppermute | solution.py:231
  6.7 3.2 %shard_map.83.in_ref = f32[384,128]{1,0:T(8,128)S(1)} custom-call(bf16[768,7168]{1,0:T(8,128)(2,1)S(1)} %bitcast.5, bf16[64,7168]{1,0:T(8,128)(2,1)S(1)} %bitcast.6), custom_call_target="tpu_custom_call" | custom-call | flops 704643072 | bytes 11010048 | tf_op jit(solution)/shard_map/pallas_call | solution.py:90
  9.9 0.0 collective-permute-done.1.got_ref
  9.9 1.0 %shard_map.85 = (f32[4,4096]{1,0:T(4,128)S(1)}, bf16[4,4096]{1,0:T(4,128)(2,1)S(1)}) custom-call(f32[384,128]{1,0:T(8,128)S(1)} %shard_map.83.in_ref, f32[384,128]{1,0:T(8,128)S(1)} %get-tuple-element.9.own_ref, bf16[384,128]{1,0:T(8,128)(2,1)S(1)} %collective-permute-done.1.got_ref, s32[4,192]{1,0:T(4,128)S(1)} %copy-done.5, f32[64,64]{1,0:T(8,128)S(1)} %copy-done.3), custom_call_target="tpu_custom_call" | custom-call | tf_op jit(solution)/shard_map/pallas_call | solution.py:141
  10.9 2.7 %collective-permute-start.2 = (bf16[4,4096]{1,0:T(4,128)(2,1)S(1)}, bf16[4,4096]{1,0:T(4,128)(2,1)S(1)}, u32[]{:S(2)}, u32[]{:S(2)}) collective-permute-start(bf16[4,4096]{1,0:T(4,128)(2,1)S(1)} %get-tuple-element.11), channel_id=1, source_target_pairs={{1,0},{0,16},{16,17},{17,1},{3,2},{2,18},{18,19},{19,3},{5,4},{4,2... | collective-permute-start | bytes 98312 | tf_op jit(solution)/shard_map/ppermute | solution.py:242
  13.7 0.0 collective-permute-start.3
  13.7 0.6 %shard_map.82 = bf16[64,2048]{1,0:T(8,128)(2,1)S(1)} custom-call(bf16[64,2048]{1,0:T(8,128)(2,1)S(1)} %copy-done.2, f32[64,64]{1,0:T(8,128)S(1)} %copy-done.4), custom_call_target="tpu_custom_call" | custom-call | tf_op jit(solution)/shard_map/pallas_call | solution.py:175
  14.3 3.0 %collective-permute-start = (bf16[64,2048]{1,0:T(8,128)(2,1)S(1)}, bf16[64,2048]{1,0:T(8,128)(2,1)S(1)}, u32[]{:S(2)}, u32[]{:S(2)}) collective-permute-start(bf16[64,2048]{1,0:T(8,128)(2,1)S(1)} %shard_map.82), channel_id=1, source_target_pairs={{0,1},{1,0},{2,3},{3,2},{4,5},{5,4},{6,7},{7,6},{8,9},{9,8},{10,11... | collective-permute-start | bytes 786440 | tf_op jit(solution)/shard_map/ppermute | solution.py:249
  17.3 2.6 %collective-permute-start.9 = (bf16[4,4096]{1,0:T(4,128)(2,1)S(1)}, bf16[4,4096]{1,0:T(4,128)(2,1)S(1)}, u32[]{:S(2)}, u32[]{:S(2)}) collective-permute-start(bf16[4,4096]{1,0:T(4,128)(2,1)S(1)} %add_convert_fusion.rest_0_), channel_id=1, source_target_pairs={{0,12},{2,14},{4,8},{6,10},{8,4},{10,6},{12,0},{14,2},{16,28},{18,... | collective-permute-start | bytes 98312 | tf_op jit(solution)/shard_map/ppermute | solution.py:257
  19.9 0.5 %collective-permute-start.5 = (bf16[4,4096]{1,0:T(4,128)(2,1)S(1)}, bf16[4,4096]{1,0:T(4,128)(2,1)S(1)}, u32[]{:S(2)}, u32[]{:S(2)}) collective-permute-start(bf16[4,4096]{1,0:T(4,128)(2,1)S(1)} %add_convert_fusion.rest_0_), channel_id=1, source_target_pairs={{0,4},{2,6},{4,0},{6,2},{8,12},{10,14},{12,8},{14,10},{16,20},{18,... | collective-permute-start | bytes 98312 | tf_op jit(solution)/shard_map/ppermute | solution.py:257
  20.4 0.4 %collective-permute-start.7 = (bf16[4,4096]{1,0:T(4,128)(2,1)S(1)}, bf16[4,4096]{1,0:T(4,128)(2,1)S(1)}, u32[]{:S(2)}, u32[]{:S(2)}) collective-permute-start(bf16[4,4096]{1,0:T(4,128)(2,1)S(1)} %add_convert_fusion.rest_0_), channel_id=1, source_target_pairs={{0,8},{2,10},{4,12},{6,14},{8,0},{10,2},{12,4},{14,6},{16,24},{18,... | collective-permute-start | bytes 98312 | tf_op jit(solution)/shard_map/ppermute | solution.py:257
  20.9 1.3 %collective-permute-done.9.rest_6_ = bf16[4,4096]{1,0:T(4,128)(2,1)S(1)} collective-permute-done((bf16[4,4096]{1,0:T(4,128)(2,1)S(1)}, bf16[4,4096]{1,0:T(4,128)(2,1)S(1)}, u32[]{:S(2)}, u32[]{:S(2)}) %collective-permute-start.9) | collective-permute-done | bytes 32800 | tf_op jit(solution)/shard_map/ppermute | solution.py:257
  22.2 0.0 collective-permute-start.10
  22.2 1.6 %collective-permute-done.5.rest_2_ = bf16[4,4096]{1,0:T(4,128)(2,1)S(1)} collective-permute-done((bf16[4,4096]{1,0:T(4,128)(2,1)S(1)}, bf16[4,4096]{1,0:T(4,128)(2,1)S(1)}, u32[]{:S(2)}, u32[]{:S(2)}) %collective-permute-start.5) | collective-permute-done | bytes 32800 | tf_op jit(solution)/shard_map/ppermute | solution.py:257
  23.8 0.5 %collective-permute-done.7.rest_4_ = bf16[4,4096]{1,0:T(4,128)(2,1)S(1)} collective-permute-done((bf16[4,4096]{1,0:T(4,128)(2,1)S(1)}, bf16[4,4096]{1,0:T(4,128)(2,1)S(1)}, u32[]{:S(2)}, u32[]{:S(2)}) %collective-permute-start.7) | collective-permute-done | bytes 32800 | tf_op jit(solution)/shard_map/ppermute | solution.py:257
  24.3 0.0 collective-permute-start.8
  24.4 0.6 %collective-permute-done.6.rest_3_ = bf16[4,4096]{1,0:T(4,128)(2,1)S(1)} collective-permute-done((bf16[4,4096]{1,0:T(4,128)(2,1)S(1)}, bf16[4,4096]{1,0:T(4,128)(2,1)S(1)}, u32[]{:S(2)}, u32[]{:S(2)}) %collective-permute-start.6) | collective-permute-done | bytes 32800 | tf_op jit(solution)/shard_map/ppermute | solution.py:259
  25.0 0.5 %collective-permute-done.8.rest_5_ = bf16[4,4096]{1,0:T(4,128)(2,1)S(1)} collective-permute-done((bf16[4,4096]{1,0:T(4,128)(2,1)S(1)}, bf16[4,4096]{1,0:T(4,128)(2,1)S(1)}, u32[]{:S(2)}, u32[]{:S(2)}) %collective-permute-start.8) | collective-permute-done | bytes 32800 | tf_op jit(solution)/shard_map/ppermute | solution.py:259
  25.5 1.0 %shard_map.86 = f32[32,64]{1,0:T(8,128)} custom-call(s32[32,64]{1,0:T(8,128)S(1)} %broadcast_in_dim.3.place_ref, bf16[64,2048]{1,0:T(8,128)(2,1)S(1)} %get-tuple-element.14.low_ref, bf16[64,2048]{1,0:T(8,128)(2,1)S(1)} %get-tuple-element.13.high_ref, bf16[4,4096]{1,0:T(4,128)(2,1)S(1)} %add_convert_fusion.rest_0_, ...), custom_call_target="tpu_custom_call" | custom-call | tf_op jit(solution)/shard_map/pallas_call | solution.py:210
  (18 shorter events, 0.1 us)
Async XLA Ops:
  0.0 6.7 %copy-start = (bf16[4,192,7168]{2,1,0:T(8,128)(2,1)S(1)}, bf16[4,192,7168]{2,1,0:T(8,128)(2,1)}, u32[]{:S(2)}) copy-start(bf16[4,192,7168]{2,1,0:T(8,128)(2,1)} %param.8) | copy-start | bytes 33030148
  0.0 6.7 %copy-start.1 = (bf16[7168,64]{0,1:T(8,128)(2,1)S(1)}, bf16[7168,64]{0,1:T(8,128)(2,1)}, u32[]{:S(2)}) copy-start(bf16[7168,64]{0,1:T(8,128)(2,1)} %param.11) | copy-start | bytes 2752516
  3.6 6.3 %copy-start.3 = (f32[64,64]{1,0:T(8,128)S(1)}, f32[64,64]{1,0:T(8,128)}, u32[]{:S(2)}) copy-start(f32[64,64]{1,0:T(8,128)} %inv_ref.3) | copy-start | bytes 49156
  3.7 6.3 %copy-start.5 = (s32[4,192]{1,0:T(4,128)S(1)}, s32[4,192]{1,0:T(4,128)}, u32[]{:S(2)}) copy-start(s32[4,192]{1,0:T(4,128)} %mask_ref.1) | copy-start | bytes 9220
  3.7 10.0 %copy-start.2 = (bf16[64,2048]{1,0:T(8,128)(2,1)S(1)}, bf16[64,2048]{1,0:T(8,128)(2,1)}, u32[]{:S(2)}) copy-start(bf16[64,2048]{1,0:T(8,128)(2,1)} %query_ref.1) | copy-start | bytes 786436
  3.7 10.0 %copy-start.4 = (f32[64,64]{1,0:T(8,128)S(1)}, f32[64,64]{1,0:T(8,128)}, u32[]{:S(2)}) copy-start(f32[64,64]{1,0:T(8,128)} %inv_ref.2) | copy-start | bytes 49156
  3.7 6.2 %collective-permute-start.1 = (bf16[384,128]{1,0:T(8,128)(2,1)S(1)}, bf16[384,128]{1,0:T(8,128)(2,1)S(1)}, u32[]{:S(2)}, u32[]{:S(2)}) collective-permute-start(bf16[384,128]{1,0:T(8,128)(2,1)S(1)} %get-tuple-element.10), channel_id=1, source_target_pairs={{0,1},{1,0},{2,3},{3,2},{4,5},{5,4},{6,7},{7,6},{8,9},{9,8},{10,11... | collective-permute-start | bytes 294920 | tf_op jit(solution)/shard_map/ppermute | solution.py:231
  10.9 6.3 %collective-permute-start.2 = (bf16[4,4096]{1,0:T(4,128)(2,1)S(1)}, bf16[4,4096]{1,0:T(4,128)(2,1)S(1)}, u32[]{:S(2)}, u32[]{:S(2)}) collective-permute-start(bf16[4,4096]{1,0:T(4,128)(2,1)S(1)} %get-tuple-element.11), channel_id=1, source_target_pairs={{1,0},{0,16},{16,17},{17,1},{3,2},{2,18},{18,19},{19,3},{5,4},{4,2... | collective-permute-start | bytes 98312 | tf_op jit(solution)/shard_map/ppermute | solution.py:242
  13.7 3.6 %collective-permute-start.3 = (bf16[4,4096]{1,0:T(4,128)(2,1)S(1)}, bf16[4,4096]{1,0:T(4,128)(2,1)S(1)}, u32[]{:S(2)}, u32[]{:S(2)}) collective-permute-start(bf16[4,4096]{1,0:T(4,128)(2,1)S(1)} %get-tuple-element.11), channel_id=1, source_target_pairs={{1,16},{16,1},{0,2},{17,19},{3,18},{18,3},{2,0},{19,17},{5,20},{20... | collective-permute-start | bytes 98312 | tf_op jit(solution)/shard_map/ppermute | solution.py:241
  14.3 10.1 %collective-permute-start = (bf16[64,2048]{1,0:T(8,128)(2,1)S(1)}, bf16[64,2048]{1,0:T(8,128)(2,1)S(1)}, u32[]{:S(2)}, u32[]{:S(2)}) collective-permute-start(bf16[64,2048]{1,0:T(8,128)(2,1)S(1)} %shard_map.82), channel_id=1, source_target_pairs={{0,1},{1,0},{2,3},{3,2},{4,5},{5,4},{6,7},{7,6},{8,9},{9,8},{10,11... | collective-permute-start | bytes 786440 | tf_op jit(solution)/shard_map/ppermute | solution.py:249
  17.3 4.9 %collective-permute-start.9 = (bf16[4,4096]{1,0:T(4,128)(2,1)S(1)}, bf16[4,4096]{1,0:T(4,128)(2,1)S(1)}, u32[]{:S(2)}, u32[]{:S(2)}) collective-permute-start(bf16[4,4096]{1,0:T(4,128)(2,1)S(1)} %add_convert_fusion.rest_0_), channel_id=1, source_target_pairs={{0,12},{2,14},{4,8},{6,10},{8,4},{10,6},{12,0},{14,2},{16,28},{18,... | collective-permute-start | bytes 98312 | tf_op jit(solution)/shard_map/ppermute | solution.py:257
  19.9 3.9 %collective-permute-start.5 = (bf16[4,4096]{1,0:T(4,128)(2,1)S(1)}, bf16[4,4096]{1,0:T(4,128)(2,1)S(1)}, u32[]{:S(2)}, u32[]{:S(2)}) collective-permute-start(bf16[4,4096]{1,0:T(4,128)(2,1)S(1)} %add_convert_fusion.rest_0_), channel_id=1, source_target_pairs={{0,4},{2,6},{4,0},{6,2},{8,12},{10,14},{12,8},{14,10},{16,20},{18,... | collective-permute-start | bytes 98312 | tf_op jit(solution)/shard_map/ppermute | solution.py:257
  20.4 3.9 %collective-permute-start.7 = (bf16[4,4096]{1,0:T(4,128)(2,1)S(1)}, bf16[4,4096]{1,0:T(4,128)(2,1)S(1)}, u32[]{:S(2)}, u32[]{:S(2)}) collective-permute-start(bf16[4,4096]{1,0:T(4,128)(2,1)S(1)} %add_convert_fusion.rest_0_), channel_id=1, source_target_pairs={{0,8},{2,10},{4,12},{6,14},{8,0},{10,2},{12,4},{14,6},{16,24},{18,... | collective-permute-start | bytes 98312 | tf_op jit(solution)/shard_map/ppermute | solution.py:257
  20.9 3.5 %collective-permute-start.4 = (bf16[4,4096]{1,0:T(4,128)(2,1)S(1)}, bf16[4,4096]{1,0:T(4,128)(2,1)S(1)}, u32[]{:S(2)}, u32[]{:S(2)}) collective-permute-start(bf16[4,4096]{1,0:T(4,128)(2,1)S(1)} %add_convert_fusion.rest_0_), channel_id=1, source_target_pairs={{0,2},{2,0},{4,6},{6,4},{8,10},{10,8},{12,14},{14,12},{16,18},{18,... | collective-permute-start | bytes 98312 | tf_op jit(solution)/shard_map/ppermute | solution.py:259
  22.2 2.2 %collective-permute-start.10 = (bf16[4,4096]{1,0:T(4,128)(2,1)S(1)}, bf16[4,4096]{1,0:T(4,128)(2,1)S(1)}, u32[]{:S(2)}, u32[]{:S(2)}) collective-permute-start(bf16[4,4096]{1,0:T(4,128)(2,1)S(1)} %collective-permute-done.9.rest_6_), channel_id=1, source_target_pairs={{0,2},{2,0},{4,6},{6,4},{8,10},{10,8},{12,14},{14,12},{16,18},{18,... | collective-permute-start | bytes 98312 | tf_op jit(solution)/shard_map/ppermute | solution.py:259
  23.8 1.2 %collective-permute-start.6 = (bf16[4,4096]{1,0:T(4,128)(2,1)S(1)}, bf16[4,4096]{1,0:T(4,128)(2,1)S(1)}, u32[]{:S(2)}, u32[]{:S(2)}) collective-permute-start(bf16[4,4096]{1,0:T(4,128)(2,1)S(1)} %collective-permute-done.5.rest_2_), channel_id=1, source_target_pairs={{0,2},{2,0},{4,6},{6,4},{8,10},{10,8},{12,14},{14,12},{16,18},{18,... | collective-permute-start | bytes 98312 | tf_op jit(solution)/shard_map/ppermute | solution.py:259
  24.3 1.2 %collective-permute-start.8 = (bf16[4,4096]{1,0:T(4,128)(2,1)S(1)}, bf16[4,4096]{1,0:T(4,128)(2,1)S(1)}, u32[]{:S(2)}, u32[]{:S(2)}) collective-permute-start(bf16[4,4096]{1,0:T(4,128)(2,1)S(1)} %collective-permute-done.7.rest_4_), channel_id=1, source_target_pairs={{0,2},{2,0},{4,6},{6,4},{8,10},{10,8},{12,14},{14,12},{16,18},{18,... | collective-permute-start | bytes 98312 | tf_op jit(solution)/shard_map/ppermute | solution.py:259

commit v5 on v4

--- a/solution.py
+++ b/solution.py
@@ -24,10 +24,36 @@
     return pltpu.with_memory_space_constraint(x, pltpu.HBM)
 
 
-def out_kernel(chunks, x_hbm, w_hbm, out_ref, sent_ref, x_ref, wide_ref, tall_ref, sems):
+def precondition(query_ref, inv_ref, block_ref, pre_ref):
+    rank = inv_ref.shape[0]
+    block_ref[...] = jnp.zeros_like(block_ref)
+    block_ref[pl.ds(0, rank), pl.ds(0, rank)] = inv_ref[...]
+    block_ref[pl.ds(rank, rank), pl.ds(rank, rank)] = inv_ref[...]
+    block = block_ref[...]
+    top = block.astype(BF16)
+    rest = block - top.astype(F32)
+    middle = rest.astype(BF16)
+    last = (rest - middle.astype(F32)).astype(BF16)
+    for b in range(query_ref.shape[1] // (2 * rank)):
+        lanes = pl.ds(b * 2 * rank, 2 * rank)
+        query = query_ref[:, lanes]
+        total = jnp.dot(query, last, preferred_element_type=F32)
+        total += jnp.dot(query, middle, preferred_element_type=F32)
+        total += jnp.dot(query, top, preferred_element_type=F32)
+        pre_ref[:, lanes] = total.astype(BF16)
+
+
+def out_kernel(
+    chunks, x_hbm, w_hbm, query_hbm, inv_hbm, out_ref, sent_ref, pre_ref,
+    x_ref, wide_ref, tall_ref, query_ref, inv_ref, block_ref, sems,
+):
     rows = x_hbm.shape[0]
     step = rows // chunks
     weights = pltpu.make_async_copy(w_hbm, wide_ref, sems.at[chunks])
+    inverse = pltpu.make_async_copy(inv_hbm, inv_ref, sems.at[chunks + 1])
+    queries = pltpu.make_async_copy(query_hbm, query_ref, sems.at[chunks + 2])
+    inverse.start()
+    queries.start()
     weights.start()
     copies = [
         pltpu.make_async_copy(
@@ -37,6 +63,9 @@
     ]
     for copy in copies:
         copy.start()
+    inverse.wait()
+    queries.wait()
+    precondition(query_ref, inv_ref, block_ref, pre_ref)
     weights.wait()
     tall_ref[...] = wide_ref[...].T
     half = rows // 2
@@ -51,26 +80,33 @@
         sent_ref[:, pl.ds(side * rank, rank)] = part.astype(BF16)
 
 
-def project_out(x, w_t, chunks):
+def project_out(x, w_t, query, inv, chunks):
     rows, depth = x.shape
     rank = w_t.shape[0]
     shape = (rows // 2, 2 * rank)
     return pl.pallas_call(
         functools.partial(out_kernel, chunks),
-        out_shape=[jax.ShapeDtypeStruct(shape, F32), jax.ShapeDtypeStruct(shape, BF16)],
-        in_specs=[HBM, HBM],
-        out_specs=[VMEM] * 2,
+        out_shape=[
+            jax.ShapeDtypeStruct(shape, F32),
+            jax.ShapeDtypeStruct(shape, BF16),
+            jax.ShapeDtypeStruct(query.shape, BF16),
+        ],
+        in_specs=[HBM] * 4,
+        out_specs=[VMEM] * 3,
         scratch_shapes=[
             pltpu.VMEM((rows, depth), BF16),
             pltpu.VMEM((rank, depth), BF16),
             pltpu.VMEM((depth, rank), BF16),
-            pltpu.SemaphoreType.DMA((chunks + 1,)),
+            pltpu.VMEM(query.shape, BF16),
+            pltpu.VMEM(inv.shape, F32),
+            pltpu.VMEM((2 * rank, 2 * rank), F32),
+            pltpu.SemaphoreType.DMA((chunks + 3,)),
         ],
         compiler_params=params(16),
         cost_estimate=pl.CostEstimate(
             flops=60 * rows * depth * rank, bytes_accessed=60 * rows * depth, transcendentals=0
         ),
-    )(hbm(x), hbm(w_t))
+    )(hbm(x), hbm(w_t), hbm(query), hbm(inv))
 
 
 def in_kernel(x_ref, w_ref, out_ref, tall_ref):
@@ -151,34 +187,18 @@
     )(in_part, out_own, out_got, token_mask, inv_input)
 
 
-def query_kernel(query_ref, inv_ref, pre_ref):
-    rank = inv_ref.shape[0]
-    zero = jnp.zeros((rank, rank), F32)
-    inv = inv_ref[...]
-    block = jnp.concatenate(
-        [jnp.concatenate([inv, zero], axis=1), jnp.concatenate([zero, inv], axis=1)], axis=0
-    )
-    top = block.astype(BF16)
-    rest = block - top.astype(F32)
-    middle = rest.astype(BF16)
-    last = (rest - middle.astype(F32)).astype(BF16)
-    for b in range(query_ref.shape[1] // (2 * rank)):
-        lanes = pl.ds(b * 2 * rank, 2 * rank)
-        query = query_ref[:, lanes]
-        total = jnp.dot(query, last, preferred_element_type=F32)
-        total += jnp.dot(query, middle, preferred_element_type=F32)
-        total += jnp.dot(query, top, preferred_element_type=F32)
-        pre_ref[:, lanes] = total.astype(BF16)
-
-
-def precondition_queries(query_feats, inv_output):
-    return pl.pallas_call(
-        query_kernel,
-        out_shape=jax.ShapeDtypeStruct(query_feats.shape, BF16),
-        in_specs=[VMEM] * 2,
+def pass_kernel(x_ref, y_ref):
+    y_ref[...] = x_ref[...]
+
+
+def pass_on(x):
+    return pl.pallas_call(
+        pass_kernel,
+        out_shape=jax.ShapeDtypeStruct(x.shape, x.dtype),
+        in_specs=[VMEM],
         out_specs=VMEM,
         compiler_params=params(16),
-    )(query_feats, inv_output)
+    )(x)
 
 
 def score_kernel(place_ref, low_ref, high_ref, *rest):
@@ -227,25 +247,28 @@
     half = ex_size // 2
     swap_hid = [(0, 1), (1, 0)]
 
-    out_own, out_sent = project_out(out_grads.reshape(seqs * length, -1), proj_out.T, 4)
+    out_own, out_sent, query_own = project_out(
+        out_grads.reshape(seqs * length, -1), proj_out.T, query_feats, inv_output, 4
+    )
     out_got = lax.ppermute(out_sent, "hid", swap_hid)
     in_part = project_in(activations.reshape(seqs * length, depth), proj_in.T)
     part, sent = outer(in_part, out_own, out_got, token_mask, inv_input)
 
-    around, across = [], []
+    alpha, beta = [], []
     for e in range(half):
         a, b, c, d = 2 * e + 1, 2 * e, 2 * (e + half), 2 * (e + half) + 1
-        around += [(a, b), (b, c), (c, d), (d, a)]
-        across += [(a, c), (c, a), (b, b ^ 2), (d, d ^ 2)]
+        alpha += [(a, b), (b, c), (c, a), (d, d ^ 2)]
+        beta += [(c, d), (d, a), (a, c), (b, b ^ 2)]
     axes = ("ex", "hid")
-    second = lax.ppermute(sent, axes, across)
-    first = lax.ppermute(sent, axes, around)
+    second = lax.ppermute(sent, axes, beta)
+    first = lax.ppermute(sent, axes, alpha)
     home = (ex // half) == hid
     mine = (
-        first.astype(F32) + jnp.where(home, part, second.astype(F32))
+        jnp.where(home & (hid == 0), part, second.astype(F32))
+        + jnp.where(home & (hid == 1), part, first.astype(F32))
     ).astype(BF16)
 
-    query_own = precondition_queries(query_feats, inv_output)
+    query_own = pass_on(query_own)
     query_got = lax.ppermute(query_own, "hid", swap_hid)
     low = jnp.where(hid == 0, query_own, query_got)
     high = jnp.where(hid == 0, query_got, query_own)

time: 26.9 us -> 26.8 us (level)
  the two profiles are of different devices: /device:TPU:0 before, /device:TPU:25 now
where the time goes in v5:
time: 26.8 us; the launch traced here: 26.6 us
  starting transfers between devices  12.5 us (47%)
  Pallas kernels  9.17 us (34%)
  waiting for transfers between devices  4.65 us (17%)
    ppermute x4, starting transfers between devices, local_pair(): lax.ppermute(pieces[k], 'ex', [(i, i ^ 1) for i in range(ex_size)])  6.41 us
    pallas_call x1, Pallas kernels, project_out(): pl.pallas_call(functools.partial(out_kernel, chunks), out_shape=[jax.Shap...  3.99 us
    pallas_call x1, Pallas kernels, project_in(): pl.pallas_call(in_kernel, out_shape=jax.ShapeDtypeStruct((rows // 2, 2 *...  3.21 us
    ppermute x3, starting transfers between devices, local_pair(): pieces[k] = lax.ppermute(mine, 'ex', [(i, i ^ k) for i in range(ex_size)])  2.71 us
    ppermute x1, waiting for transfers between devices, local_pair(): second = lax.ppermute(sent, axes, beta)  2 us
    ppermute x1, waiting for transfers between devices, local_pair(): first = lax.ppermute(sent, axes, alpha)  1.85 us
    ppermute x1, starting transfers between devices, local_pair(): out_got = lax.ppermute(out_sent, 'hid', swap_hid)  1.28 us
    ppermute x1, starting transfers between devices, local_pair(): first = lax.ppermute(sent, axes, alpha)  1.03 us
  transfers between devices with their start and end apart: 11, of which 3 were waited for; matrix products, arithmetic and copies ran while one was open for 0% of the time, Pallas kernels for 12%

profile of v5, /device:TPU:25, one launch (start us, length us, event | category | flops | bytes accessed | tf_op | source)
XLA Modules:
  0.0 26.6 jit_solution(18134220139673791500)
XLA Ops:
  0.0 4.0 %shard_map.82 = (f32[384,128]{1,0:T(8,128)S(1)}, bf16[384,128]{1,0:T(8,128)(2,1)S(1)}, bf16[64,2048]{1,0:T(8,128)(2,1)S(1)}) custom-call(bf16[768,2048]{1,0:T(8,128)(2,1)} %bitcast.7, bf16[64,2048]{1,0:T(8,128)(2,1)} %bitcast.8, bf16[64,2048]{1,0:T(8,128)(2,1)} %query_hbm.1, f32[64,64]{1,0:T(8,128)} %inv_hbm.1), custom_call_target="tpu_custom_call" | custom-call | flops 6039797760 | bytes 94371840 | tf_op jit(solution)/shard_map/pallas_call | solution.py:87
  4.0 0.0 copy-start.2
  4.0 0.0 copy-start.3
  4.0 1.3 %collective-permute-start.1 = (bf16[384,128]{1,0:T(8,128)(2,1)S(1)}, bf16[384,128]{1,0:T(8,128)(2,1)S(1)}, u32[]{:S(2)}, u32[]{:S(2)}) collective-permute-start(bf16[384,128]{1,0:T(8,128)(2,1)S(1)} %get-tuple-element.12), channel_id=1, source_target_pairs={{0,1},{1,0},{2,3},{3,2},{4,5},{5,4},{6,7},{7,6},{8,9},{9,8},{10,11... | collective-permute-start | bytes 294920 | tf_op jit(solution)/shard_map/ppermute | solution.py:253
  5.3 0.1 copy-done.1
  5.4 3.2 %shard_map.84.in_ref = f32[384,128]{1,0:T(8,128)S(1)} custom-call(bf16[768,7168]{1,0:T(8,128)(2,1)S(1)} %bitcast.5, bf16[64,7168]{1,0:T(8,128)(2,1)S(1)} %bitcast.6), custom_call_target="tpu_custom_call" | custom-call | flops 704643072 | bytes 11010048 | tf_op jit(solution)/shard_map/pallas_call | solution.py:126
  8.6 0.0 collective-permute-done.1.got_ref
  8.7 1.0 %shard_map.85 = (f32[4,4096]{1,0:T(4,128)S(1)}, bf16[4,4096]{1,0:T(4,128)(2,1)S(1)}) custom-call(f32[384,128]{1,0:T(8,128)S(1)} %shard_map.84.in_ref, f32[384,128]{1,0:T(8,128)S(1)} %get-tuple-element.11.own_ref, bf16[384,128]{1,0:T(8,128)(2,1)S(1)} %collective-permute-done.1.got_ref, s32[4,192]{1,0:T(4,128)S(1)} %copy-done.3, f32[64,64]{1,0:T(8,128)S(1)} %copy-done.2), custom_call_target="tpu_custom_call" | custom-call | tf_op jit(solution)/shard_map/pallas_call | solution.py:177
  9.7 1.0 %collective-permute-start.3 = (bf16[4,4096]{1,0:T(4,128)(2,1)S(1)}, bf16[4,4096]{1,0:T(4,128)(2,1)S(1)}, u32[]{:S(2)}, u32[]{:S(2)}) collective-permute-start(bf16[4,4096]{1,0:T(4,128)(2,1)S(1)} %get-tuple-element.14), channel_id=1, source_target_pairs={{1,0},{0,16},{16,1},{17,19},{3,2},{2,18},{18,3},{19,17},{5,4},{4,2... | collective-permute-start | bytes 98312 | tf_op jit(solution)/shard_map/ppermute | solution.py:264
  10.7 0.9 %collective-permute-start.2 = (bf16[4,4096]{1,0:T(4,128)(2,1)S(1)}, bf16[4,4096]{1,0:T(4,128)(2,1)S(1)}, u32[]{:S(2)}, u32[]{:S(2)}) collective-permute-start(bf16[4,4096]{1,0:T(4,128)(2,1)S(1)} %get-tuple-element.14), channel_id=1, source_target_pairs={{16,17},{17,1},{1,16},{0,2},{18,19},{19,3},{3,18},{2,0},{20,21},{2... | collective-permute-start | bytes 98312 | tf_op jit(solution)/shard_map/ppermute | solution.py:263
  11.7 0.1 collective-permute-start
  11.8 1.8 %collective-permute-done.3 = bf16[4,4096]{1,0:T(4,128)(2,1)S(1)} collective-permute-done((bf16[4,4096]{1,0:T(4,128)(2,1)S(1)}, bf16[4,4096]{1,0:T(4,128)(2,1)S(1)}, u32[]{:S(2)}, u32[]{:S(2)}) %collective-permute-start.3) | collective-permute-done | bytes 32800 | tf_op jit(solution)/shard_map/ppermute | solution.py:264
  13.6 2.0 %collective-permute-done.2 = bf16[4,4096]{1,0:T(4,128)(2,1)S(1)} collective-permute-done((bf16[4,4096]{1,0:T(4,128)(2,1)S(1)}, bf16[4,4096]{1,0:T(4,128)(2,1)S(1)}, u32[]{:S(2)}, u32[]{:S(2)}) %collective-permute-start.2) | collective-permute-done | bytes 32800 | tf_op jit(solution)/shard_map/ppermute | solution.py:263
  15.7 1.0 %collective-permute-start.9 = (bf16[4,4096]{1,0:T(4,128)(2,1)S(1)}, bf16[4,4096]{1,0:T(4,128)(2,1)S(1)}, u32[]{:S(2)}, u32[]{:S(2)}) collective-permute-start(bf16[4,4096]{1,0:T(4,128)(2,1)S(1)} %add_convert_fusion.rest_0_), channel_id=1, source_target_pairs={{0,12},{2,14},{4,8},{6,10},{8,4},{10,6},{12,0},{14,2},{16,28},{18,... | collective-permute-start | bytes 98312 | tf_op jit(solution)/shard_map/ppermute | solution.py:280
  16.6 1.5 %collective-permute-start.7 = (bf16[4,4096]{1,0:T(4,128)(2,1)S(1)}, bf16[4,4096]{1,0:T(4,128)(2,1)S(1)}, u32[]{:S(2)}, u32[]{:S(2)}) collective-permute-start(bf16[4,4096]{1,0:T(4,128)(2,1)S(1)} %add_convert_fusion.rest_0_), channel_id=1, source_target_pairs={{0,8},{2,10},{4,12},{6,14},{8,0},{10,2},{12,4},{14,6},{16,24},{18,... | collective-permute-start | bytes 98312 | tf_op jit(solution)/shard_map/ppermute | solution.py:280
  18.1 0.2 collective-permute-start.5
  18.4 3.0 %collective-permute-start.4 = (bf16[4,4096]{1,0:T(4,128)(2,1)S(1)}, bf16[4,4096]{1,0:T(4,128)(2,1)S(1)}, u32[]{:S(2)}, u32[]{:S(2)}) collective-permute-start(bf16[4,4096]{1,0:T(4,128)(2,1)S(1)} %add_convert_fusion.rest_0_), channel_id=1, source_target_pairs={{0,2},{2,0},{4,6},{6,4},{8,10},{10,8},{12,14},{14,12},{16,18},{18,... | collective-permute-start | bytes 98312 | tf_op jit(solution)/shard_map/ppermute | solution.py:282
  21.4 0.0 collective-permute-done.9.rest_6_
  21.4 1.3 %collective-permute-start.10 = (bf16[4,4096]{1,0:T(4,128)(2,1)S(1)}, bf16[4,4096]{1,0:T(4,128)(2,1)S(1)}, u32[]{:S(2)}, u32[]{:S(2)}) collective-permute-start(bf16[4,4096]{1,0:T(4,128)(2,1)S(1)} %collective-permute-done.9.rest_6_), channel_id=1, source_target_pairs={{0,2},{2,0},{4,6},{6,4},{8,10},{10,8},{12,14},{14,12},{16,18},{18,... | collective-permute-start | bytes 98312 | tf_op jit(solution)/shard_map/ppermute | solution.py:282
  22.7 0.4 %collective-permute-start.8 = (bf16[4,4096]{1,0:T(4,128)(2,1)S(1)}, bf16[4,4096]{1,0:T(4,128)(2,1)S(1)}, u32[]{:S(2)}, u32[]{:S(2)}) collective-permute-start(bf16[4,4096]{1,0:T(4,128)(2,1)S(1)} %collective-permute-done.7.rest_4_), channel_id=1, source_target_pairs={{0,2},{2,0},{4,6},{6,4},{8,10},{10,8},{12,14},{14,12},{16,18},{18,... | collective-permute-start | bytes 98312 | tf_op jit(solution)/shard_map/ppermute | solution.py:282
  23.1 0.0 collective-permute-done.5.rest_2_
  23.1 1.7 %collective-permute-start.6 = (bf16[4,4096]{1,0:T(4,128)(2,1)S(1)}, bf16[4,4096]{1,0:T(4,128)(2,1)S(1)}, u32[]{:S(2)}, u32[]{:S(2)}) collective-permute-start(bf16[4,4096]{1,0:T(4,128)(2,1)S(1)} %collective-permute-done.5.rest_2_), channel_id=1, source_target_pairs={{0,2},{2,0},{4,6},{6,4},{8,10},{10,8},{12,14},{14,12},{16,18},{18,... | collective-permute-start | bytes 98312 | tf_op jit(solution)/shard_map/ppermute | solution.py:282
  24.9 0.8 %collective-permute-done.6.rest_3_ = bf16[4,4096]{1,0:T(4,128)(2,1)S(1)} collective-permute-done((bf16[4,4096]{1,0:T(4,128)(2,1)S(1)}, bf16[4,4096]{1,0:T(4,128)(2,1)S(1)}, u32[]{:S(2)}, u32[]{:S(2)}) %collective-permute-start.6) | collective-permute-done | bytes 32800 | tf_op jit(solution)/shard_map/ppermute | solution.py:282
  25.7 1.0 %shard_map.86 = f32[32,64]{1,0:T(8,128)} custom-call(s32[32,64]{1,0:T(8,128)S(1)} %broadcast_in_dim.3.place_ref, bf16[64,2048]{1,0:T(8,128)(2,1)S(1)} %get-tuple-element.16.low_ref, bf16[64,2048]{1,0:T(8,128)(2,1)S(1)} %get-tuple-element.15.high_ref, bf16[4,4096]{1,0:T(4,128)(2,1)S(1)} %add_convert_fusion.rest_0_, ...), custom_call_target="tpu_custom_call" | custom-call | tf_op jit(solution)/shard_map/pallas_call | solution.py:230
  (14 shorter events, 0.1 us)
Async XLA Ops:
  0.0 5.3 %copy-start = (bf16[4,192,7168]{2,1,0:T(8,128)(2,1)S(1)}, bf16[4,192,7168]{2,1,0:T(8,128)(2,1)}, u32[]{:S(2)}) copy-start(bf16[4,192,7168]{2,1,0:T(8,128)(2,1)} %param.8) | copy-start | bytes 33030148
  0.0 5.4 %copy-start.1 = (bf16[7168,64]{0,1:T(8,128)(2,1)S(1)}, bf16[7168,64]{0,1:T(8,128)(2,1)}, u32[]{:S(2)}) copy-start(bf16[7168,64]{0,1:T(8,128)(2,1)} %param.11) | copy-start | bytes 2752516
  4.0 4.7 %copy-start.2 = (f32[64,64]{1,0:T(8,128)S(1)}, f32[64,64]{1,0:T(8,128)}, u32[]{:S(2)}) copy-start(f32[64,64]{1,0:T(8,128)} %inv_ref.1) | copy-start | bytes 49156
  4.0 4.7 %copy-start.3 = (s32[4,192]{1,0:T(4,128)S(1)}, s32[4,192]{1,0:T(4,128)}, u32[]{:S(2)}) copy-start(s32[4,192]{1,0:T(4,128)} %mask_ref.1) | copy-start | bytes 9220
  4.0 4.6 %collective-permute-start.1 = (bf16[384,128]{1,0:T(8,128)(2,1)S(1)}, bf16[384,128]{1,0:T(8,128)(2,1)S(1)}, u32[]{:S(2)}, u32[]{:S(2)}) collective-permute-start(bf16[384,128]{1,0:T(8,128)(2,1)S(1)} %get-tuple-element.12), channel_id=1, source_target_pairs={{0,1},{1,0},{2,3},{3,2},{4,5},{5,4},{6,7},{7,6},{8,9},{9,8},{10,11... | collective-permute-start | bytes 294920 | tf_op jit(solution)/shard_map/ppermute | solution.py:253
  9.7 4.0 %collective-permute-start.3 = (bf16[4,4096]{1,0:T(4,128)(2,1)S(1)}, bf16[4,4096]{1,0:T(4,128)(2,1)S(1)}, u32[]{:S(2)}, u32[]{:S(2)}) collective-permute-start(bf16[4,4096]{1,0:T(4,128)(2,1)S(1)} %get-tuple-element.14), channel_id=1, source_target_pairs={{1,0},{0,16},{16,1},{17,19},{3,2},{2,18},{18,3},{19,17},{5,4},{4,2... | collective-permute-start | bytes 98312 | tf_op jit(solution)/shard_map/ppermute | solution.py:264
  10.7 4.9 %collective-permute-start.2 = (bf16[4,4096]{1,0:T(4,128)(2,1)S(1)}, bf16[4,4096]{1,0:T(4,128)(2,1)S(1)}, u32[]{:S(2)}, u32[]{:S(2)}) collective-permute-start(bf16[4,4096]{1,0:T(4,128)(2,1)S(1)} %get-tuple-element.14), channel_id=1, source_target_pairs={{16,17},{17,1},{1,16},{0,2},{18,19},{19,3},{3,18},{2,0},{20,21},{2... | collective-permute-start | bytes 98312 | tf_op jit(solution)/shard_map/ppermute | solution.py:263
  11.7 13.1 %collective-permute-start = (bf16[64,2048]{1,0:T(8,128)(2,1)S(1)}, bf16[64,2048]{1,0:T(8,128)(2,1)S(1)}, u32[]{:S(2)}, u32[]{:S(2)}) collective-permute-start(bf16[64,2048]{1,0:T(8,128)(2,1)S(1)} %shard_map.83), channel_id=1, source_target_pairs={{0,1},{1,0},{2,3},{3,2},{4,5},{5,4},{6,7},{7,6},{8,9},{9,8},{10,11... | collective-permute-start | bytes 786440 | tf_op jit(solution)/shard_map/ppermute | solution.py:272
  15.7 5.7 %collective-permute-start.9 = (bf16[4,4096]{1,0:T(4,128)(2,1)S(1)}, bf16[4,4096]{1,0:T(4,128)(2,1)S(1)}, u32[]{:S(2)}, u32[]{:S(2)}) collective-permute-start(bf16[4,4096]{1,0:T(4,128)(2,1)S(1)} %add_convert_fusion.rest_0_), channel_id=1, source_target_pairs={{0,12},{2,14},{4,8},{6,10},{8,4},{10,6},{12,0},{14,2},{16,28},{18,... | collective-permute-start | bytes 98312 | tf_op jit(solution)/shard_map/ppermute | solution.py:280
  16.6 6.1 %collective-permute-start.7 = (bf16[4,4096]{1,0:T(4,128)(2,1)S(1)}, bf16[4,4096]{1,0:T(4,128)(2,1)S(1)}, u32[]{:S(2)}, u32[]{:S(2)}) collective-permute-start(bf16[4,4096]{1,0:T(4,128)(2,1)S(1)} %add_convert_fusion.rest_0_), channel_id=1, source_target_pairs={{0,8},{2,10},{4,12},{6,14},{8,0},{10,2},{12,4},{14,6},{16,24},{18,... | collective-permute-start | bytes 98312 | tf_op jit(solution)/shard_map/ppermute | solution.py:280
  18.1 5.0 %collective-permute-start.5 = (bf16[4,4096]{1,0:T(4,128)(2,1)S(1)}, bf16[4,4096]{1,0:T(4,128)(2,1)S(1)}, u32[]{:S(2)}, u32[]{:S(2)}) collective-permute-start(bf16[4,4096]{1,0:T(4,128)(2,1)S(1)} %add_convert_fusion.rest_0_), channel_id=1, source_target_pairs={{0,4},{2,6},{4,0},{6,2},{8,12},{10,14},{12,8},{14,10},{16,20},{18,... | collective-permute-start | bytes 98312 | tf_op jit(solution)/shard_map/ppermute | solution.py:280
  18.4 6.5 %collective-permute-start.4 = (bf16[4,4096]{1,0:T(4,128)(2,1)S(1)}, bf16[4,4096]{1,0:T(4,128)(2,1)S(1)}, u32[]{:S(2)}, u32[]{:S(2)}) collective-permute-start(bf16[4,4096]{1,0:T(4,128)(2,1)S(1)} %add_convert_fusion.rest_0_), channel_id=1, source_target_pairs={{0,2},{2,0},{4,6},{6,4},{8,10},{10,8},{12,14},{14,12},{16,18},{18,... | collective-permute-start | bytes 98312 | tf_op jit(solution)/shard_map/ppermute | solution.py:282
  21.4 3.5 %collective-permute-start.10 = (bf16[4,4096]{1,0:T(4,128)(2,1)S(1)}, bf16[4,4096]{1,0:T(4,128)(2,1)S(1)}, u32[]{:S(2)}, u32[]{:S(2)}) collective-permute-start(bf16[4,4096]{1,0:T(4,128)(2,1)S(1)} %collective-permute-done.9.rest_6_), channel_id=1, source_target_pairs={{0,2},{2,0},{4,6},{6,4},{8,10},{10,8},{12,14},{14,12},{16,18},{18,... | collective-permute-start | bytes 98312 | tf_op jit(solution)/shard_map/ppermute | solution.py:282
  22.7 2.2 %collective-permute-start.8 = (bf16[4,4096]{1,0:T(4,128)(2,1)S(1)}, bf16[4,4096]{1,0:T(4,128)(2,1)S(1)}, u32[]{:S(2)}, u32[]{:S(2)}) collective-permute-start(bf16[4,4096]{1,0:T(4,128)(2,1)S(1)} %collective-permute-done.7.rest_4_), channel_id=1, source_target_pairs={{0,2},{2,0},{4,6},{6,4},{8,10},{10,8},{12,14},{14,12},{16,18},{18,... | collective-permute-start | bytes 98312 | tf_op jit(solution)/shard_map/ppermute | solution.py:282
  23.1 2.5 %collective-permute-start.6 = (bf16[4,4096]{1,0:T(4,128)(2,1)S(1)}, bf16[4,4096]{1,0:T(4,128)(2,1)S(1)}, u32[]{:S(2)}, u32[]{:S(2)}) collective-permute-start(bf16[4,4096]{1,0:T(4,128)(2,1)S(1)} %collective-permute-done.5.rest_2_), channel_id=1, source_target_pairs={{0,2},{2,0},{4,6},{6,4},{8,10},{10,8},{12,14},{14,12},{16,18},{18,... | collective-permute-start | bytes 98312 | tf_op jit(solution)/shard_map/ppermute | solution.py:282

commit v6 on v5

--- a/solution.py
+++ b/solution.py
@@ -136,11 +136,28 @@
     )(x, w_t)
 
 
+def split(x):
+    top = x.astype(BF16)
+    return top, (x - top.astype(F32)).astype(BF16)
+
+
+def precise_dot(a, b, dims):
+    (top_a, rest_a), (top_b, rest_b) = split(a), split(b)
+    axis_a, axis_b = dims
+    return lax.dot_general(
+        jnp.concatenate([top_a, top_a, rest_a], axis=axis_a),
+        jnp.concatenate([top_b, rest_b, top_b], axis=axis_b),
+        (((axis_a,), (axis_b,)), ((), ())),
+        preferred_element_type=F32,
+    )
+
+
 def outer_kernel(
-    length, in_ref, own_ref, got_ref, mask_ref, inv_ref, part_ref, sent_ref, rows_ref, pairs_ref
+    length, in_ref, own_ref, got_ref, mask_ref, inv_ref, part_ref, sent_ref, pairs_ref
 ):
     rank = inv_ref.shape[0]
     seqs = mask_ref.shape[0]
+    half = rank // 2
     counts = jnp.sum(mask_ref[...].astype(F32), axis=1, keepdims=True)
     lane = lax.broadcasted_iota(jnp.int32, (length, 2 * rank), 1)
     token = lax.broadcasted_iota(jnp.int32, (length, 2 * rank), 0).astype(F32)
@@ -151,23 +168,22 @@
         real = token < jnp.where(lane < rank, low, high)
         inside = jnp.where(real, in_ref[rows, :], 0.0)
         outside = own_ref[rows, :] + got_ref[rows, :].astype(F32)
-        both = lax.dot_general(
-            inside, outside, TN, precision=HIGH, preferred_element_type=F32
-        )
+        both = precise_dot(inside, outside, (0, 0))
         grams[pair] = both[:rank, :rank] / low
         grams[pair + seqs // 2] = both[rank:, rank:] / high
     gram = jnp.concatenate(grams, axis=1)
-    pre = lax.dot_general(inv_ref[...], gram, TN, precision=HIGH, preferred_element_type=F32)
-    half = rank // 2
+    mixed = jnp.concatenate(
+        [inv_ref[pl.ds(0, half, stride=2), :], inv_ref[pl.ds(1, half, stride=2), :]], axis=0
+    )
+    pre = precise_dot(mixed, gram, (1, 0))
     for s in range(seqs):
-        rows_ref[...] = pre[:, s * rank : (s + 1) * rank]
-        pairs_ref[pl.ds(s * half, half), :] = jnp.concatenate(
-            [rows_ref[pl.ds(0, half, stride=2), :], rows_ref[pl.ds(1, half, stride=2), :]], axis=1
-        )
+        one = pre[:, s * rank : (s + 1) * rank]
+        pairs_ref[pl.ds(s * half, half), :] = jnp.concatenate([one[:half], one[half:]], axis=1)
     for b in range(half):
         row = pairs_ref[pl.ds(b, seqs, stride=half), :]
-        part_ref[:, pl.ds(b * 2 * rank, 2 * rank)] = row
-    sent_ref[...] = part_ref[...].astype(BF16)
+        lanes = pl.ds(b * 2 * rank, 2 * rank)
+        part_ref[:, lanes] = row
+        sent_ref[:, lanes] = row.astype(BF16)
 
 
 def outer(in_part, out_own, out_got, token_mask, inv_input):
@@ -180,7 +196,6 @@
         in_specs=[VMEM] * 5,
         out_specs=[VMEM] * 2,
         scratch_shapes=[
-            pltpu.VMEM((rank, rank), F32),
             pltpu.VMEM((seqs * rank // 2, 2 * rank), F32),
         ],
         compiler_params=params(16),

time: 26.8 us -> 26.5 us (0.989)
  Pallas kernels: 9.17 us -> 8.87 us
    pallas_call x1, Pallas kernels: 1 us -> 0.69 us  [outer(): pl.pallas_call(functools.partial(outer_kernel, length), out_shape=[jax.Sh...]
where the time goes in v6:
time: 26.5 us; the launch traced here: 26.3 us
  starting transfers between devices  12.5 us (47%)
  Pallas kernels  8.87 us (33%)
  waiting for transfers between devices  4.65 us (18%)
    ppermute x4, starting transfers between devices, local_pair(): lax.ppermute(pieces[k], 'ex', [(i, i ^ 1) for i in range(ex_size)])  6.41 us
    pallas_call x1, Pallas kernels, project_out(): pl.pallas_call(functools.partial(out_kernel, chunks), out_shape=[jax.Shap...  3.99 us
    pallas_call x1, Pallas kernels, project_in(): pl.pallas_call(in_kernel, out_shape=jax.ShapeDtypeStruct((rows // 2, 2 *...  3.21 us
    ppermute x3, starting transfers between devices, local_pair(): pieces[k] = lax.ppermute(mine, 'ex', [(i, i ^ k) for i in range(ex_size)])  2.71 us
    ppermute x1, waiting for transfers between devices, local_pair(): second = lax.ppermute(sent, axes, beta)  2 us
    ppermute x1, waiting for transfers between devices, local_pair(): first = lax.ppermute(sent, axes, alpha)  1.85 us
    ppermute x1, starting transfers between devices, local_pair(): out_got = lax.ppermute(out_sent, 'hid', swap_hid)  1.28 us
    ppermute x1, starting transfers between devices, local_pair(): first = lax.ppermute(sent, axes, alpha)  1.03 us
  transfers between devices with their start and end apart: 11, of which 3 were waited for; matrix products, arithmetic and copies ran while one was open for 0% of the time, Pallas kernels for 12%

profile of v6, /device:TPU:25, one launch (start us, length us, event | category | flops | bytes accessed | tf_op | source)
XLA Modules:
  0.0 26.3 jit_solution(5822604762917347281)
XLA Ops:
  0.0 4.0 %shard_map.82 = (f32[384,128]{1,0:T(8,128)S(1)}, bf16[384,128]{1,0:T(8,128)(2,1)S(1)}, bf16[64,2048]{1,0:T(8,128)(2,1)S(1)}) custom-call(bf16[768,2048]{1,0:T(8,128)(2,1)} %bitcast.7, bf16[64,2048]{1,0:T(8,128)(2,1)} %bitcast.8, bf16[64,2048]{1,0:T(8,128)(2,1)} %query_hbm.1, f32[64,64]{1,0:T(8,128)} %inv_hbm.1), custom_call_target="tpu_custom_call" | custom-call | flops 6039797760 | bytes 94371840 | tf_op jit(solution)/shard_map/pallas_call | solution.py:87
  4.0 0.0 copy-start.2
  4.0 0.0 copy-start.3
  4.0 1.3 %collective-permute-start.1 = (bf16[384,128]{1,0:T(8,128)(2,1)S(1)}, bf16[384,128]{1,0:T(8,128)(2,1)S(1)}, u32[]{:S(2)}, u32[]{:S(2)}) collective-permute-start(bf16[384,128]{1,0:T(8,128)(2,1)S(1)} %get-tuple-element.12), channel_id=1, source_target_pairs={{0,1},{1,0},{2,3},{3,2},{4,5},{5,4},{6,7},{7,6},{8,9},{9,8},{10,11... | collective-permute-start | bytes 294920 | tf_op jit(solution)/shard_map/ppermute | solution.py:268
  5.3 0.1 copy-done.1
  5.4 3.2 %shard_map.84.in_ref = f32[384,128]{1,0:T(8,128)S(1)} custom-call(bf16[768,7168]{1,0:T(8,128)(2,1)S(1)} %bitcast.5, bf16[64,7168]{1,0:T(8,128)(2,1)S(1)} %bitcast.6), custom_call_target="tpu_custom_call" | custom-call | flops 704643072 | bytes 11010048 | tf_op jit(solution)/shard_map/pallas_call | solution.py:126
  8.6 0.0 collective-permute-done.1.got_ref
  8.7 0.7 %shard_map.85 = (f32[4,4096]{1,0:T(4,128)S(1)}, bf16[4,4096]{1,0:T(4,128)(2,1)S(1)}) custom-call(f32[384,128]{1,0:T(8,128)S(1)} %shard_map.84.in_ref, f32[384,128]{1,0:T(8,128)S(1)} %get-tuple-element.11.own_ref, bf16[384,128]{1,0:T(8,128)(2,1)S(1)} %collective-permute-done.1.got_ref, s32[4,192]{1,0:T(4,128)S(1)} %copy-done.3, f32[64,64]{1,0:T(8,128)S(1)} %copy-done.2), custom_call_target="tpu_custom_call" | custom-call | tf_op jit(solution)/shard_map/pallas_call | solution.py:193
  9.4 1.0 %collective-permute-start.3 = (bf16[4,4096]{1,0:T(4,128)(2,1)S(1)}, bf16[4,4096]{1,0:T(4,128)(2,1)S(1)}, u32[]{:S(2)}, u32[]{:S(2)}) collective-permute-start(bf16[4,4096]{1,0:T(4,128)(2,1)S(1)} %get-tuple-element.14), channel_id=1, source_target_pairs={{1,0},{0,16},{16,1},{17,19},{3,2},{2,18},{18,3},{19,17},{5,4},{4,2... | collective-permute-start | bytes 98312 | tf_op jit(solution)/shard_map/ppermute | solution.py:279
  10.4 0.9 %collective-permute-start.2 = (bf16[4,4096]{1,0:T(4,128)(2,1)S(1)}, bf16[4,4096]{1,0:T(4,128)(2,1)S(1)}, u32[]{:S(2)}, u32[]{:S(2)}) collective-permute-start(bf16[4,4096]{1,0:T(4,128)(2,1)S(1)} %get-tuple-element.14), channel_id=1, source_target_pairs={{16,17},{17,1},{1,16},{0,2},{18,19},{19,3},{3,18},{2,0},{20,21},{2... | collective-permute-start | bytes 98312 | tf_op jit(solution)/shard_map/ppermute | solution.py:278
  11.4 0.1 collective-permute-start
  11.5 1.8 %collective-permute-done.3 = bf16[4,4096]{1,0:T(4,128)(2,1)S(1)} collective-permute-done((bf16[4,4096]{1,0:T(4,128)(2,1)S(1)}, bf16[4,4096]{1,0:T(4,128)(2,1)S(1)}, u32[]{:S(2)}, u32[]{:S(2)}) %collective-permute-start.3) | collective-permute-done | bytes 32800 | tf_op jit(solution)/shard_map/ppermute | solution.py:279
  13.3 2.0 %collective-permute-done.2 = bf16[4,4096]{1,0:T(4,128)(2,1)S(1)} collective-permute-done((bf16[4,4096]{1,0:T(4,128)(2,1)S(1)}, bf16[4,4096]{1,0:T(4,128)(2,1)S(1)}, u32[]{:S(2)}, u32[]{:S(2)}) %collective-permute-start.2) | collective-permute-done | bytes 32800 | tf_op jit(solution)/shard_map/ppermute | solution.py:278
  15.4 1.0 %collective-permute-start.9 = (bf16[4,4096]{1,0:T(4,128)(2,1)S(1)}, bf16[4,4096]{1,0:T(4,128)(2,1)S(1)}, u32[]{:S(2)}, u32[]{:S(2)}) collective-permute-start(bf16[4,4096]{1,0:T(4,128)(2,1)S(1)} %add_convert_fusion.rest_0_), channel_id=1, source_target_pairs={{0,12},{2,14},{4,8},{6,10},{8,4},{10,6},{12,0},{14,2},{16,28},{18,... | collective-permute-start | bytes 98312 | tf_op jit(solution)/shard_map/ppermute | solution.py:295
  16.3 1.5 %collective-permute-start.7 = (bf16[4,4096]{1,0:T(4,128)(2,1)S(1)}, bf16[4,4096]{1,0:T(4,128)(2,1)S(1)}, u32[]{:S(2)}, u32[]{:S(2)}) collective-permute-start(bf16[4,4096]{1,0:T(4,128)(2,1)S(1)} %add_convert_fusion.rest_0_), channel_id=1, source_target_pairs={{0,8},{2,10},{4,12},{6,14},{8,0},{10,2},{12,4},{14,6},{16,24},{18,... | collective-permute-start | bytes 98312 | tf_op jit(solution)/shard_map/ppermute | solution.py:295
  17.8 0.2 collective-permute-start.5
  18.1 3.0 %collective-permute-start.4 = (bf16[4,4096]{1,0:T(4,128)(2,1)S(1)}, bf16[4,4096]{1,0:T(4,128)(2,1)S(1)}, u32[]{:S(2)}, u32[]{:S(2)}) collective-permute-start(bf16[4,4096]{1,0:T(4,128)(2,1)S(1)} %add_convert_fusion.rest_0_), channel_id=1, source_target_pairs={{0,2},{2,0},{4,6},{6,4},{8,10},{10,8},{12,14},{14,12},{16,18},{18,... | collective-permute-start | bytes 98312 | tf_op jit(solution)/shard_map/ppermute | solution.py:297
  21.0 0.0 collective-permute-done.9.rest_6_
  21.0 1.3 %collective-permute-start.10 = (bf16[4,4096]{1,0:T(4,128)(2,1)S(1)}, bf16[4,4096]{1,0:T(4,128)(2,1)S(1)}, u32[]{:S(2)}, u32[]{:S(2)}) collective-permute-start(bf16[4,4096]{1,0:T(4,128)(2,1)S(1)} %collective-permute-done.9.rest_6_), channel_id=1, source_target_pairs={{0,2},{2,0},{4,6},{6,4},{8,10},{10,8},{12,14},{14,12},{16,18},{18,... | collective-permute-start | bytes 98312 | tf_op jit(solution)/shard_map/ppermute | solution.py:297
  22.4 0.4 %collective-permute-start.8 = (bf16[4,4096]{1,0:T(4,128)(2,1)S(1)}, bf16[4,4096]{1,0:T(4,128)(2,1)S(1)}, u32[]{:S(2)}, u32[]{:S(2)}) collective-permute-start(bf16[4,4096]{1,0:T(4,128)(2,1)S(1)} %collective-permute-done.7.rest_4_), channel_id=1, source_target_pairs={{0,2},{2,0},{4,6},{6,4},{8,10},{10,8},{12,14},{14,12},{16,18},{18,... | collective-permute-start | bytes 98312 | tf_op jit(solution)/shard_map/ppermute | solution.py:297
  22.8 0.0 collective-permute-done.5.rest_2_
  22.8 1.7 %collective-permute-start.6 = (bf16[4,4096]{1,0:T(4,128)(2,1)S(1)}, bf16[4,4096]{1,0:T(4,128)(2,1)S(1)}, u32[]{:S(2)}, u32[]{:S(2)}) collective-permute-start(bf16[4,4096]{1,0:T(4,128)(2,1)S(1)} %collective-permute-done.5.rest_2_), channel_id=1, source_target_pairs={{0,2},{2,0},{4,6},{6,4},{8,10},{10,8},{12,14},{14,12},{16,18},{18,... | collective-permute-start | bytes 98312 | tf_op jit(solution)/shard_map/ppermute | solution.py:297
  24.6 0.8 %collective-permute-done.6.rest_3_ = bf16[4,4096]{1,0:T(4,128)(2,1)S(1)} collective-permute-done((bf16[4,4096]{1,0:T(4,128)(2,1)S(1)}, bf16[4,4096]{1,0:T(4,128)(2,1)S(1)}, u32[]{:S(2)}, u32[]{:S(2)}) %collective-permute-start.6) | collective-permute-done | bytes 32800 | tf_op jit(solution)/shard_map/ppermute | solution.py:297
  25.3 1.0 %shard_map.86 = f32[32,64]{1,0:T(8,128)} custom-call(s32[32,64]{1,0:T(8,128)S(1)} %broadcast_in_dim.3.place_ref, bf16[64,2048]{1,0:T(8,128)(2,1)S(1)} %get-tuple-element.16.low_ref, bf16[64,2048]{1,0:T(8,128)(2,1)S(1)} %get-tuple-element.15.high_ref, bf16[4,4096]{1,0:T(4,128)(2,1)S(1)} %add_convert_fusion.rest_0_, ...), custom_call_target="tpu_custom_call" | custom-call | tf_op jit(solution)/shard_map/pallas_call | solution.py:245
  (14 shorter events, 0.1 us)
Async XLA Ops:
  0.0 5.3 %copy-start = (bf16[4,192,7168]{2,1,0:T(8,128)(2,1)S(1)}, bf16[4,192,7168]{2,1,0:T(8,128)(2,1)}, u32[]{:S(2)}) copy-start(bf16[4,192,7168]{2,1,0:T(8,128)(2,1)} %param.8) | copy-start | bytes 33030148
  0.0 5.4 %copy-start.1 = (bf16[7168,64]{0,1:T(8,128)(2,1)S(1)}, bf16[7168,64]{0,1:T(8,128)(2,1)}, u32[]{:S(2)}) copy-start(bf16[7168,64]{0,1:T(8,128)(2,1)} %param.11) | copy-start | bytes 2752516
  4.0 4.7 %copy-start.2 = (f32[64,64]{1,0:T(8,128)S(1)}, f32[64,64]{1,0:T(8,128)}, u32[]{:S(2)}) copy-start(f32[64,64]{1,0:T(8,128)} %inv_ref.1) | copy-start | bytes 49156
  4.0 4.7 %copy-start.3 = (s32[4,192]{1,0:T(4,128)S(1)}, s32[4,192]{1,0:T(4,128)}, u32[]{:S(2)}) copy-start(s32[4,192]{1,0:T(4,128)} %mask_ref.1) | copy-start | bytes 9220
  4.0 4.6 %collective-permute-start.1 = (bf16[384,128]{1,0:T(8,128)(2,1)S(1)}, bf16[384,128]{1,0:T(8,128)(2,1)S(1)}, u32[]{:S(2)}, u32[]{:S(2)}) collective-permute-start(bf16[384,128]{1,0:T(8,128)(2,1)S(1)} %get-tuple-element.12), channel_id=1, source_target_pairs={{0,1},{1,0},{2,3},{3,2},{4,5},{5,4},{6,7},{7,6},{8,9},{9,8},{10,11... | collective-permute-start | bytes 294920 | tf_op jit(solution)/shard_map/ppermute | solution.py:268
  9.4 4.0 %collective-permute-start.3 = (bf16[4,4096]{1,0:T(4,128)(2,1)S(1)}, bf16[4,4096]{1,0:T(4,128)(2,1)S(1)}, u32[]{:S(2)}, u32[]{:S(2)}) collective-permute-start(bf16[4,4096]{1,0:T(4,128)(2,1)S(1)} %get-tuple-element.14), channel_id=1, source_target_pairs={{1,0},{0,16},{16,1},{17,19},{3,2},{2,18},{18,3},{19,17},{5,4},{4,2... | collective-permute-start | bytes 98312 | tf_op jit(solution)/shard_map/ppermute | solution.py:279
  10.4 4.9 %collective-permute-start.2 = (bf16[4,4096]{1,0:T(4,128)(2,1)S(1)}, bf16[4,4096]{1,0:T(4,128)(2,1)S(1)}, u32[]{:S(2)}, u32[]{:S(2)}) collective-permute-start(bf16[4,4096]{1,0:T(4,128)(2,1)S(1)} %get-tuple-element.14), channel_id=1, source_target_pairs={{16,17},{17,1},{1,16},{0,2},{18,19},{19,3},{3,18},{2,0},{20,21},{2... | collective-permute-start | bytes 98312 | tf_op jit(solution)/shard_map/ppermute | solution.py:278
  11.4 13.1 %collective-permute-start = (bf16[64,2048]{1,0:T(8,128)(2,1)S(1)}, bf16[64,2048]{1,0:T(8,128)(2,1)S(1)}, u32[]{:S(2)}, u32[]{:S(2)}) collective-permute-start(bf16[64,2048]{1,0:T(8,128)(2,1)S(1)} %shard_map.83), channel_id=1, source_target_pairs={{0,1},{1,0},{2,3},{3,2},{4,5},{5,4},{6,7},{7,6},{8,9},{9,8},{10,11... | collective-permute-start | bytes 786440 | tf_op jit(solution)/shard_map/ppermute | solution.py:287
  15.4 5.7 %collective-permute-start.9 = (bf16[4,4096]{1,0:T(4,128)(2,1)S(1)}, bf16[4,4096]{1,0:T(4,128)(2,1)S(1)}, u32[]{:S(2)}, u32[]{:S(2)}) collective-permute-start(bf16[4,4096]{1,0:T(4,128)(2,1)S(1)} %add_convert_fusion.rest_0_), channel_id=1, source_target_pairs={{0,12},{2,14},{4,8},{6,10},{8,4},{10,6},{12,0},{14,2},{16,28},{18,... | collective-permute-start | bytes 98312 | tf_op jit(solution)/shard_map/ppermute | solution.py:295
  16.3 6.1 %collective-permute-start.7 = (bf16[4,4096]{1,0:T(4,128)(2,1)S(1)}, bf16[4,4096]{1,0:T(4,128)(2,1)S(1)}, u32[]{:S(2)}, u32[]{:S(2)}) collective-permute-start(bf16[4,4096]{1,0:T(4,128)(2,1)S(1)} %add_convert_fusion.rest_0_), channel_id=1, source_target_pairs={{0,8},{2,10},{4,12},{6,14},{8,0},{10,2},{12,4},{14,6},{16,24},{18,... | collective-permute-start | bytes 98312 | tf_op jit(solution)/shard_map/ppermute | solution.py:295
  17.8 5.0 %collective-permute-start.5 = (bf16[4,4096]{1,0:T(4,128)(2,1)S(1)}, bf16[4,4096]{1,0:T(4,128)(2,1)S(1)}, u32[]{:S(2)}, u32[]{:S(2)}) collective-permute-start(bf16[4,4096]{1,0:T(4,128)(2,1)S(1)} %add_convert_fusion.rest_0_), channel_id=1, source_target_pairs={{0,4},{2,6},{4,0},{6,2},{8,12},{10,14},{12,8},{14,10},{16,20},{18,... | collective-permute-start | bytes 98312 | tf_op jit(solution)/shard_map/ppermute | solution.py:295
  18.1 6.5 %collective-permute-start.4 = (bf16[4,4096]{1,0:T(4,128)(2,1)S(1)}, bf16[4,4096]{1,0:T(4,128)(2,1)S(1)}, u32[]{:S(2)}, u32[]{:S(2)}) collective-permute-start(bf16[4,4096]{1,0:T(4,128)(2,1)S(1)} %add_convert_fusion.rest_0_), channel_id=1, source_target_pairs={{0,2},{2,0},{4,6},{6,4},{8,10},{10,8},{12,14},{14,12},{16,18},{18,... | collective-permute-start | bytes 98312 | tf_op jit(solution)/shard_map/ppermute | solution.py:297
  21.0 3.5 %collective-permute-start.10 = (bf16[4,4096]{1,0:T(4,128)(2,1)S(1)}, bf16[4,4096]{1,0:T(4,128)(2,1)S(1)}, u32[]{:S(2)}, u32[]{:S(2)}) collective-permute-start(bf16[4,4096]{1,0:T(4,128)(2,1)S(1)} %collective-permute-done.9.rest_6_), channel_id=1, source_target_pairs={{0,2},{2,0},{4,6},{6,4},{8,10},{10,8},{12,14},{14,12},{16,18},{18,... | collective-permute-start | bytes 98312 | tf_op jit(solution)/shard_map/ppermute | solution.py:297
  22.4 2.2 %collective-permute-start.8 = (bf16[4,4096]{1,0:T(4,128)(2,1)S(1)}, bf16[4,4096]{1,0:T(4,128)(2,1)S(1)}, u32[]{:S(2)}, u32[]{:S(2)}) collective-permute-start(bf16[4,4096]{1,0:T(4,128)(2,1)S(1)} %collective-permute-done.7.rest_4_), channel_id=1, source_target_pairs={{0,2},{2,0},{4,6},{6,4},{8,10},{10,8},{12,14},{14,12},{16,18},{18,... | collective-permute-start | bytes 98312 | tf_op jit(solution)/shard_map/ppermute | solution.py:297
  22.8 2.5 %collective-permute-start.6 = (bf16[4,4096]{1,0:T(4,128)(2,1)S(1)}, bf16[4,4096]{1,0:T(4,128)(2,1)S(1)}, u32[]{:S(2)}, u32[]{:S(2)}) collective-permute-start(bf16[4,4096]{1,0:T(4,128)(2,1)S(1)} %collective-permute-done.5.rest_2_), channel_id=1, source_target_pairs={{0,2},{2,0},{4,6},{6,4},{8,10},{10,8},{12,14},{14,12},{16,18},{18,... | collective-permute-start | bytes 98312 | tf_op jit(solution)/shard_map/ppermute | solution.py:297

commit v7 on v6

--- a/solution.py
+++ b/solution.py
@@ -272,8 +272,8 @@
     alpha, beta = [], []
     for e in range(half):
         a, b, c, d = 2 * e + 1, 2 * e, 2 * (e + half), 2 * (e + half) + 1
-        alpha += [(a, b), (b, c), (c, a), (d, d ^ 2)]
-        beta += [(c, d), (d, a), (a, c), (b, b ^ 2)]
+        alpha += [(a, b), (b, c ^ 2), (c, a ^ 2), (d, d ^ 2)]
+        beta += [(c, d), (d, a ^ 2), (a, c ^ 2), (b, b ^ 2)]
     axes = ("ex", "hid")
     second = lax.ppermute(sent, axes, beta)
     first = lax.ppermute(sent, axes, alpha)
@@ -288,14 +288,12 @@
     low = jnp.where(hid == 0, query_own, query_got)
     high = jnp.where(hid == 0, query_got, query_own)
 
-    pieces = [mine]
-    far = [k for k in range(2, half, 2)]
     pieces = {0: mine}
-    for k in sorted(far, key=lambda k: -k):
+    for k in range(half - 1, 1, -2):
         pieces[k] = lax.ppermute(mine, "ex", [(i, i ^ k) for i in range(ex_size)])
     for k in list(pieces):
         pieces[k ^ 1] = lax.ppermute(pieces[k], "ex", [(i, i ^ 1) for i in range(ex_size)])
-    place = jnp.full((seqs * half, query_feats.shape[0]), ex % half, jnp.int32)
+    place = jnp.full((seqs * half, query_feats.shape[0]), ex % half ^ jnp.where(home, 0, 1), jnp.int32)
     scores = score(place, low, high, [pieces[k] for k in range(half)])
     return scores.T
 

time: 26.5 us -> 25.1 us (0.947)
  the two profiles are of different devices: /device:TPU:25 before, /device:TPU:17 now
where the time goes in v7:
time: 25.1 us; the launch traced here: 25 us
  Pallas kernels  8.87 us (35%)
  starting transfers between devices  8.06 us (32%)
  waiting for transfers between devices  7.75 us (31%)
    pallas_call x1, Pallas kernels, project_out(): pl.pallas_call(functools.partial(out_kernel, chunks), out_shape=[jax.Shap...  3.99 us
    pallas_call x1, Pallas kernels, project_in(): pl.pallas_call(in_kernel, out_shape=jax.ShapeDtypeStruct((rows // 2, 2 *...  3.21 us
    ppermute x3, starting transfers between devices, local_pair(): pieces[k] = lax.ppermute(mine, 'ex', [(i, i ^ k) for i in range(ex_size)])  3.19 us
    ppermute x3, waiting for transfers between devices, local_pair(): pieces[k] = lax.ppermute(mine, 'ex', [(i, i ^ k) for i in range(ex_size)])  2.56 us
    ppermute x1, waiting for transfers between devices, local_pair(): first = lax.ppermute(sent, axes, alpha)  2.12 us
    ppermute x1, waiting for transfers between devices, local_pair(): second = lax.ppermute(sent, axes, beta)  2.04 us
    ppermute x1, starting transfers between devices, local_pair(): first = lax.ppermute(sent, axes, alpha)  1.64 us
    ppermute x1, starting transfers between devices, local_pair(): out_got = lax.ppermute(out_sent, 'hid', swap_hid)  1.27 us
  transfers between devices with their start and end apart: 11, of which 6 were waited for; matrix products, arithmetic and copies ran while one was open for 0% of the time, Pallas kernels for 13%

profile of v7, /device:TPU:17, one launch (start us, length us, event | category | flops | bytes accessed | tf_op | source)
XLA Modules:
  0.0 25.0 jit_solution(12676729209789509476)
XLA Ops:
  0.0 4.0 %shard_map.82 = (f32[384,128]{1,0:T(8,128)S(1)}, bf16[384,128]{1,0:T(8,128)(2,1)S(1)}, bf16[64,2048]{1,0:T(8,128)(2,1)S(1)}) custom-call(bf16[768,2048]{1,0:T(8,128)(2,1)} %bitcast.7, bf16[64,2048]{1,0:T(8,128)(2,1)} %bitcast.8, bf16[64,2048]{1,0:T(8,128)(2,1)} %query_hbm.1, f32[64,64]{1,0:T(8,128)} %inv_hbm.1), custom_call_target="tpu_custom_call" | custom-call | flops 6039797760 | bytes 94371840 | tf_op jit(solution)/shard_map/pallas_call | solution.py:87
  4.0 0.0 copy-start.2
  4.0 0.0 copy-start.3
  4.0 1.3 %collective-permute-start.1 = (bf16[384,128]{1,0:T(8,128)(2,1)S(1)}, bf16[384,128]{1,0:T(8,128)(2,1)S(1)}, u32[]{:S(2)}, u32[]{:S(2)}) collective-permute-start(bf16[384,128]{1,0:T(8,128)(2,1)S(1)} %get-tuple-element.12), channel_id=1, source_target_pairs={{0,1},{1,0},{2,3},{3,2},{4,5},{5,4},{6,7},{7,6},{8,9},{9,8},{10,11... | collective-permute-start | bytes 294920 | tf_op jit(solution)/shard_map/ppermute | solution.py:268
  5.3 0.1 copy-done.1
  5.4 3.2 %shard_map.84.in_ref = f32[384,128]{1,0:T(8,128)S(1)} custom-call(bf16[768,7168]{1,0:T(8,128)(2,1)S(1)} %bitcast.5, bf16[64,7168]{1,0:T(8,128)(2,1)S(1)} %bitcast.6), custom_call_target="tpu_custom_call" | custom-call | flops 704643072 | bytes 11010048 | tf_op jit(solution)/shard_map/pallas_call | solution.py:126
  8.7 0.7 %shard_map.85 = (f32[4,4096]{1,0:T(4,128)S(1)}, bf16[4,4096]{1,0:T(4,128)(2,1)S(1)}) custom-call(f32[384,128]{1,0:T(8,128)S(1)} %shard_map.84.in_ref, f32[384,128]{1,0:T(8,128)S(1)} %get-tuple-element.11.own_ref, bf16[384,128]{1,0:T(8,128)(2,1)S(1)} %collective-permute-done.1.got_ref, s32[4,192]{1,0:T(4,128)S(1)} %copy-done.3, f32[64,64]{1,0:T(8,128)S(1)} %copy-done.2), custom_call_target="tpu_custom_call" | custom-call | tf_op jit(solution)/shard_map/pallas_call | solution.py:193
  9.4 1.6 %collective-permute-start.3 = (bf16[4,4096]{1,0:T(4,128)(2,1)S(1)}, bf16[4,4096]{1,0:T(4,128)(2,1)S(1)}, u32[]{:S(2)}, u32[]{:S(2)}) collective-permute-start(bf16[4,4096]{1,0:T(4,128)(2,1)S(1)} %get-tuple-element.14), channel_id=1, source_target_pairs={{1,0},{0,18},{16,3},{17,19},{3,2},{2,16},{18,1},{19,17},{5,4},{4,2... | collective-permute-start | bytes 98312 | tf_op jit(solution)/shard_map/ppermute | solution.py:279
  11.0 0.3 %collective-permute-start.2 = (bf16[4,4096]{1,0:T(4,128)(2,1)S(1)}, bf16[4,4096]{1,0:T(4,128)(2,1)S(1)}, u32[]{:S(2)}, u32[]{:S(2)}) collective-permute-start(bf16[4,4096]{1,0:T(4,128)(2,1)S(1)} %get-tuple-element.14), channel_id=1, source_target_pairs={{16,17},{17,3},{1,18},{0,2},{18,19},{19,1},{3,16},{2,0},{20,21},{2... | collective-permute-start | bytes 98312 | tf_op jit(solution)/shard_map/ppermute | solution.py:278
  11.4 0.7 %collective-permute-start = (bf16[64,2048]{1,0:T(8,128)(2,1)S(1)}, bf16[64,2048]{1,0:T(8,128)(2,1)S(1)}, u32[]{:S(2)}, u32[]{:S(2)}) collective-permute-start(bf16[64,2048]{1,0:T(8,128)(2,1)S(1)} %shard_map.83), channel_id=1, source_target_pairs={{0,1},{1,0},{2,3},{3,2},{4,5},{5,4},{6,7},{7,6},{8,9},{9,8},{10,11... | collective-permute-start | bytes 786440 | tf_op jit(solution)/shard_map/ppermute | solution.py:287
  12.0 2.1 %collective-permute-done.3 = bf16[4,4096]{1,0:T(4,128)(2,1)S(1)} collective-permute-done((bf16[4,4096]{1,0:T(4,128)(2,1)S(1)}, bf16[4,4096]{1,0:T(4,128)(2,1)S(1)}, u32[]{:S(2)}, u32[]{:S(2)}) %collective-permute-start.3) | collective-permute-done | bytes 32800 | tf_op jit(solution)/shard_map/ppermute | solution.py:279
  14.2 2.0 %collective-permute-done.2 = bf16[4,4096]{1,0:T(4,128)(2,1)S(1)} collective-permute-done((bf16[4,4096]{1,0:T(4,128)(2,1)S(1)}, bf16[4,4096]{1,0:T(4,128)(2,1)S(1)}, u32[]{:S(2)}, u32[]{:S(2)}) %collective-permute-start.2) | collective-permute-done | bytes 32800 | tf_op jit(solution)/shard_map/ppermute | solution.py:278
  16.2 2.3 %collective-permute-start.9 = (bf16[4,4096]{1,0:T(4,128)(2,1)S(1)}, bf16[4,4096]{1,0:T(4,128)(2,1)S(1)}, u32[]{:S(2)}, u32[]{:S(2)}) collective-permute-start(bf16[4,4096]{1,0:T(4,128)(2,1)S(1)} %add_convert_fusion.rest_0_), channel_id=1, source_target_pairs={{0,14},{2,12},{4,10},{6,8},{8,6},{10,4},{12,2},{14,0},{16,30},{18,... | collective-permute-start | bytes 98312 | tf_op jit(solution)/shard_map/ppermute | solution.py:293
  18.5 0.5 %collective-permute-start.7 = (bf16[4,4096]{1,0:T(4,128)(2,1)S(1)}, bf16[4,4096]{1,0:T(4,128)(2,1)S(1)}, u32[]{:S(2)}, u32[]{:S(2)}) collective-permute-start(bf16[4,4096]{1,0:T(4,128)(2,1)S(1)} %add_convert_fusion.rest_0_), channel_id=1, source_target_pairs={{0,10},{2,8},{4,14},{6,12},{8,2},{10,0},{12,6},{14,4},{16,26},{18,... | collective-permute-start | bytes 98312 | tf_op jit(solution)/shard_map/ppermute | solution.py:293
  19.0 0.4 %collective-permute-start.5 = (bf16[4,4096]{1,0:T(4,128)(2,1)S(1)}, bf16[4,4096]{1,0:T(4,128)(2,1)S(1)}, u32[]{:S(2)}, u32[]{:S(2)}) collective-permute-start(bf16[4,4096]{1,0:T(4,128)(2,1)S(1)} %add_convert_fusion.rest_0_), channel_id=1, source_target_pairs={{0,6},{2,4},{4,2},{6,0},{8,14},{10,12},{12,10},{14,8},{16,22},{18,... | collective-permute-start | bytes 98312 | tf_op jit(solution)/shard_map/ppermute | solution.py:293
  19.4 0.2 collective-permute-start.4
  19.6 0.9 %collective-permute-done.9.rest_7_ = bf16[4,4096]{1,0:T(4,128)(2,1)S(1)} collective-permute-done((bf16[4,4096]{1,0:T(4,128)(2,1)S(1)}, bf16[4,4096]{1,0:T(4,128)(2,1)S(1)}, u32[]{:S(2)}, u32[]{:S(2)}) %collective-permute-start.9) | collective-permute-done | bytes 32800 | tf_op jit(solution)/shard_map/ppermute | solution.py:293
  20.5 0.2 collective-permute-start.10
  20.8 1.6 %collective-permute-done.7.rest_5_ = bf16[4,4096]{1,0:T(4,128)(2,1)S(1)} collective-permute-done((bf16[4,4096]{1,0:T(4,128)(2,1)S(1)}, bf16[4,4096]{1,0:T(4,128)(2,1)S(1)}, u32[]{:S(2)}, u32[]{:S(2)}) %collective-permute-start.7) | collective-permute-done | bytes 32800 | tf_op jit(solution)/shard_map/ppermute | solution.py:293
  22.4 0.4 %collective-permute-start.8 = (bf16[4,4096]{1,0:T(4,128)(2,1)S(1)}, bf16[4,4096]{1,0:T(4,128)(2,1)S(1)}, u32[]{:S(2)}, u32[]{:S(2)}) collective-permute-start(bf16[4,4096]{1,0:T(4,128)(2,1)S(1)} %collective-permute-done.7.rest_5_), channel_id=1, source_target_pairs={{0,2},{2,0},{4,6},{6,4},{8,10},{10,8},{12,14},{14,12},{16,18},{18,... | collective-permute-start | bytes 98312 | tf_op jit(solution)/shard_map/ppermute | solution.py:295
  22.8 0.1 collective-permute-start.6
  23.0 0.7 %collective-permute-done.8.rest_4_ = bf16[4,4096]{1,0:T(4,128)(2,1)S(1)} collective-permute-done((bf16[4,4096]{1,0:T(4,128)(2,1)S(1)}, bf16[4,4096]{1,0:T(4,128)(2,1)S(1)}, u32[]{:S(2)}, u32[]{:S(2)}) %collective-permute-start.8) | collective-permute-done | bytes 32800 | tf_op jit(solution)/shard_map/ppermute | solution.py:295
  23.7 0.4 %collective-permute-done.6.rest_2_ = bf16[4,4096]{1,0:T(4,128)(2,1)S(1)} collective-permute-done((bf16[4,4096]{1,0:T(4,128)(2,1)S(1)}, bf16[4,4096]{1,0:T(4,128)(2,1)S(1)}, u32[]{:S(2)}, u32[]{:S(2)}) %collective-permute-start.6) | collective-permute-done | bytes 32800 | tf_op jit(solution)/shard_map/ppermute | solution.py:295
  24.0 1.0 %shard_map.86 = f32[32,64]{1,0:T(8,128)} custom-call(s32[32,64]{1,0:T(8,128)S(1)} %broadcast_in_dim.3.place_ref, bf16[64,2048]{1,0:T(8,128)(2,1)S(1)} %get-tuple-element.16.low_ref, bf16[64,2048]{1,0:T(8,128)(2,1)S(1)} %get-tuple-element.15.high_ref, bf16[4,4096]{1,0:T(4,128)(2,1)S(1)} %add_convert_fusion.rest_0_, ...), custom_call_target="tpu_custom_call" | custom-call | tf_op jit(solution)/shard_map/pallas_call | solution.py:245
  (14 shorter events, 0.1 us)
Async XLA Ops:
  0.0 5.3 %copy-start = (bf16[4,192,7168]{2,1,0:T(8,128)(2,1)S(1)}, bf16[4,192,7168]{2,1,0:T(8,128)(2,1)}, u32[]{:S(2)}) copy-start(bf16[4,192,7168]{2,1,0:T(8,128)(2,1)} %param.8) | copy-start | bytes 33030148
  0.0 5.4 %copy-start.1 = (bf16[7168,64]{0,1:T(8,128)(2,1)S(1)}, bf16[7168,64]{0,1:T(8,128)(2,1)}, u32[]{:S(2)}) copy-start(bf16[7168,64]{0,1:T(8,128)(2,1)} %param.11) | copy-start | bytes 2752516
  4.0 4.6 %copy-start.2 = (f32[64,64]{1,0:T(8,128)S(1)}, f32[64,64]{1,0:T(8,128)}, u32[]{:S(2)}) copy-start(f32[64,64]{1,0:T(8,128)} %inv_ref.1) | copy-start | bytes 49156
  4.0 4.6 %copy-start.3 = (s32[4,192]{1,0:T(4,128)S(1)}, s32[4,192]{1,0:T(4,128)}, u32[]{:S(2)}) copy-start(s32[4,192]{1,0:T(4,128)} %mask_ref.1) | copy-start | bytes 9220
  4.0 4.6 %collective-permute-start.1 = (bf16[384,128]{1,0:T(8,128)(2,1)S(1)}, bf16[384,128]{1,0:T(8,128)(2,1)S(1)}, u32[]{:S(2)}, u32[]{:S(2)}) collective-permute-start(bf16[384,128]{1,0:T(8,128)(2,1)S(1)} %get-tuple-element.12), channel_id=1, source_target_pairs={{0,1},{1,0},{2,3},{3,2},{4,5},{5,4},{6,7},{7,6},{8,9},{9,8},{10,11... | collective-permute-start | bytes 294920 | tf_op jit(solution)/shard_map/ppermute | solution.py:268
  9.4 4.8 %collective-permute-start.3 = (bf16[4,4096]{1,0:T(4,128)(2,1)S(1)}, bf16[4,4096]{1,0:T(4,128)(2,1)S(1)}, u32[]{:S(2)}, u32[]{:S(2)}) collective-permute-start(bf16[4,4096]{1,0:T(4,128)(2,1)S(1)} %get-tuple-element.14), channel_id=1, source_target_pairs={{1,0},{0,18},{16,3},{17,19},{3,2},{2,16},{18,1},{19,17},{5,4},{4,2... | collective-permute-start | bytes 98312 | tf_op jit(solution)/shard_map/ppermute | solution.py:279
  11.0 5.2 %collective-permute-start.2 = (bf16[4,4096]{1,0:T(4,128)(2,1)S(1)}, bf16[4,4096]{1,0:T(4,128)(2,1)S(1)}, u32[]{:S(2)}, u32[]{:S(2)}) collective-permute-start(bf16[4,4096]{1,0:T(4,128)(2,1)S(1)} %get-tuple-element.14), channel_id=1, source_target_pairs={{16,17},{17,3},{1,18},{0,2},{18,19},{19,1},{3,16},{2,0},{20,21},{2... | collective-permute-start | bytes 98312 | tf_op jit(solution)/shard_map/ppermute | solution.py:278
  11.4 11.5 %collective-permute-start = (bf16[64,2048]{1,0:T(8,128)(2,1)S(1)}, bf16[64,2048]{1,0:T(8,128)(2,1)S(1)}, u32[]{:S(2)}, u32[]{:S(2)}) collective-permute-start(bf16[64,2048]{1,0:T(8,128)(2,1)S(1)} %shard_map.83), channel_id=1, source_target_pairs={{0,1},{1,0},{2,3},{3,2},{4,5},{5,4},{6,7},{7,6},{8,9},{9,8},{10,11... | collective-permute-start | bytes 786440 | tf_op jit(solution)/shard_map/ppermute | solution.py:287
  16.2 4.3 %collective-permute-start.9 = (bf16[4,4096]{1,0:T(4,128)(2,1)S(1)}, bf16[4,4096]{1,0:T(4,128)(2,1)S(1)}, u32[]{:S(2)}, u32[]{:S(2)}) collective-permute-start(bf16[4,4096]{1,0:T(4,128)(2,1)S(1)} %add_convert_fusion.rest_0_), channel_id=1, source_target_pairs={{0,14},{2,12},{4,10},{6,8},{8,6},{10,4},{12,2},{14,0},{16,30},{18,... | collective-permute-start | bytes 98312 | tf_op jit(solution)/shard_map/ppermute | solution.py:293
  18.5 3.9 %collective-permute-start.7 = (bf16[4,4096]{1,0:T(4,128)(2,1)S(1)}, bf16[4,4096]{1,0:T(4,128)(2,1)S(1)}, u32[]{:S(2)}, u32[]{:S(2)}) collective-permute-start(bf16[4,4096]{1,0:T(4,128)(2,1)S(1)} %add_convert_fusion.rest_0_), channel_id=1, source_target_pairs={{0,10},{2,8},{4,14},{6,12},{8,2},{10,0},{12,6},{14,4},{16,26},{18,... | collective-permute-start | bytes 98312 | tf_op jit(solution)/shard_map/ppermute | solution.py:293
  19.0 3.8 %collective-permute-start.5 = (bf16[4,4096]{1,0:T(4,128)(2,1)S(1)}, bf16[4,4096]{1,0:T(4,128)(2,1)S(1)}, u32[]{:S(2)}, u32[]{:S(2)}) collective-permute-start(bf16[4,4096]{1,0:T(4,128)(2,1)S(1)} %add_convert_fusion.rest_0_), channel_id=1, source_target_pairs={{0,6},{2,4},{4,2},{6,0},{8,14},{10,12},{12,10},{14,8},{16,22},{18,... | collective-permute-start | bytes 98312 | tf_op jit(solution)/shard_map/ppermute | solution.py:293
  19.4 3.6 %collective-permute-start.4 = (bf16[4,4096]{1,0:T(4,128)(2,1)S(1)}, bf16[4,4096]{1,0:T(4,128)(2,1)S(1)}, u32[]{:S(2)}, u32[]{:S(2)}) collective-permute-start(bf16[4,4096]{1,0:T(4,128)(2,1)S(1)} %add_convert_fusion.rest_0_), channel_id=1, source_target_pairs={{0,2},{2,0},{4,6},{6,4},{8,10},{10,8},{12,14},{14,12},{16,18},{18,... | collective-permute-start | bytes 98312 | tf_op jit(solution)/shard_map/ppermute | solution.py:295
  20.5 2.5 %collective-permute-start.10 = (bf16[4,4096]{1,0:T(4,128)(2,1)S(1)}, bf16[4,4096]{1,0:T(4,128)(2,1)S(1)}, u32[]{:S(2)}, u32[]{:S(2)}) collective-permute-start(bf16[4,4096]{1,0:T(4,128)(2,1)S(1)} %collective-permute-done.9.rest_7_), channel_id=1, source_target_pairs={{0,2},{2,0},{4,6},{6,4},{8,10},{10,8},{12,14},{14,12},{16,18},{18,... | collective-permute-start | bytes 98312 | tf_op jit(solution)/shard_map/ppermute | solution.py:295
  22.4 1.3 %collective-permute-start.8 = (bf16[4,4096]{1,0:T(4,128)(2,1)S(1)}, bf16[4,4096]{1,0:T(4,128)(2,1)S(1)}, u32[]{:S(2)}, u32[]{:S(2)}) collective-permute-start(bf16[4,4096]{1,0:T(4,128)(2,1)S(1)} %collective-permute-done.7.rest_5_), channel_id=1, source_target_pairs={{0,2},{2,0},{4,6},{6,4},{8,10},{10,8},{12,14},{14,12},{16,18},{18,... | collective-permute-start | bytes 98312 | tf_op jit(solution)/shard_map/ppermute | solution.py:295
  22.8 1.2 %collective-permute-start.6 = (bf16[4,4096]{1,0:T(4,128)(2,1)S(1)}, bf16[4,4096]{1,0:T(4,128)(2,1)S(1)}, u32[]{:S(2)}, u32[]{:S(2)}) collective-permute-start(bf16[4,4096]{1,0:T(4,128)(2,1)S(1)} %collective-permute-done.5.rest_3_), channel_id=1, source_target_pairs={{0,2},{2,0},{4,6},{6,4},{8,10},{10,8},{12,14},{14,12},{16,18},{18,... | collective-permute-start | bytes 98312 | tf_op jit(solution)/shard_map/ppermute | solution.py:295

commit v8 on v7

--- a/solution.py
+++ b/solution.py
@@ -289,7 +289,8 @@
     high = jnp.where(hid == 0, query_got, query_own)
 
     pieces = {0: mine}
-    for k in range(half - 1, 1, -2):
+    for k in range(half - 2, 0, -2):
+        k = k if k & (k - 1) else k ^ 1
         pieces[k] = lax.ppermute(mine, "ex", [(i, i ^ k) for i in range(ex_size)])
     for k in list(pieces):
         pieces[k ^ 1] = lax.ppermute(pieces[k], "ex", [(i, i ^ 1) for i in range(ex_size)])

time: 25.1 us -> 24.7 us (0.984)
  the two profiles are of different devices: /device:TPU:17 before, /device:TPU:0 now
where the time goes in v8:
time: 24.7 us; the launch traced here: 24.4 us
  starting transfers between devices  11.9 us (48%)
  Pallas kernels  8.87 us (36%)
  waiting for transfers between devices  3.47 us (14%)
    pallas_call x1, Pallas kernels, project_out(): pl.pallas_call(functools.partial(out_kernel, chunks), out_shape=[jax.Shap...  3.99 us
    ppermute x3, starting transfers between devices, local_pair(): pieces[k] = lax.ppermute(mine, 'ex', [(i, i ^ k) for i in range(ex_size)])  3.27 us
    pallas_call x1, Pallas kernels, project_in(): pl.pallas_call(in_kernel, out_shape=jax.ShapeDtypeStruct((rows // 2, 2 *...  3.21 us
    ppermute x1, starting transfers between devices, local_pair(): out_got = lax.ppermute(out_sent, 'hid', swap_hid)  3 us
    ppermute x3, waiting for transfers between devices, local_pair(): pieces[k] = lax.ppermute(mine, 'ex', [(i, i ^ k) for i in range(ex_size)])  2.66 us
    ppermute x1, starting transfers between devices, local_pair(): query_got = lax.ppermute(query_own, 'hid', swap_hid)  2.29 us
    ppermute x1, starting transfers between devices, local_pair(): first = lax.ppermute(sent, axes, alpha)  1.92 us
    pallas_call x1, Pallas kernels, score(): pl.pallas_call(score_kernel, out_shape=jax.ShapeDtypeStruct((rows, low.sh...  0.96 us
  transfers between devices with their start and end apart: 11, of which 4 were waited for; matrix products, arithmetic and copies ran while one was open for 0% of the time, Pallas kernels for 13%

profile of v8, /device:TPU:0, one launch (start us, length us, event | category | flops | bytes accessed | tf_op | source)
XLA Modules:
  0.0 24.4 jit_solution(4598340711846186798)
XLA Ops:
  0.0 4.0 %shard_map.82 = (f32[384,128]{1,0:T(8,128)S(1)}, bf16[384,128]{1,0:T(8,128)(2,1)S(1)}, bf16[64,2048]{1,0:T(8,128)(2,1)S(1)}) custom-call(bf16[768,2048]{1,0:T(8,128)(2,1)} %bitcast.7, bf16[64,2048]{1,0:T(8,128)(2,1)} %bitcast.8, bf16[64,2048]{1,0:T(8,128)(2,1)} %query_hbm.1, f32[64,64]{1,0:T(8,128)} %inv_hbm.1), custom_call_target="tpu_custom_call" | custom-call | flops 6039797760 | bytes 94371840 | tf_op jit(solution)/shard_map/pallas_call | solution.py:87
  4.0 0.0 copy-start.2
  4.0 0.0 copy-start.3
  4.0 3.0 %collective-permute-start.1 = (bf16[384,128]{1,0:T(8,128)(2,1)S(1)}, bf16[384,128]{1,0:T(8,128)(2,1)S(1)}, u32[]{:S(2)}, u32[]{:S(2)}) collective-permute-start(bf16[384,128]{1,0:T(8,128)(2,1)S(1)} %get-tuple-element.12), channel_id=1, source_target_pairs={{0,1},{1,0},{2,3},{3,2},{4,5},{5,4},{6,7},{7,6},{8,9},{9,8},{10,11... | collective-permute-start | bytes 294920 | tf_op jit(solution)/shard_map/ppermute | solution.py:268
  7.0 3.2 %shard_map.84.in_ref = f32[384,128]{1,0:T(8,128)S(1)} custom-call(bf16[768,7168]{1,0:T(8,128)(2,1)S(1)} %bitcast.5, bf16[64,7168]{1,0:T(8,128)(2,1)S(1)} %bitcast.6), custom_call_target="tpu_custom_call" | custom-call | flops 704643072 | bytes 11010048 | tf_op jit(solution)/shard_map/pallas_call | solution.py:126
  10.2 0.0 collective-permute-done.1.got_ref
  10.3 0.7 %shard_map.85 = (f32[4,4096]{1,0:T(4,128)S(1)}, bf16[4,4096]{1,0:T(4,128)(2,1)S(1)}) custom-call(f32[384,128]{1,0:T(8,128)S(1)} %shard_map.84.in_ref, f32[384,128]{1,0:T(8,128)S(1)} %get-tuple-element.11.own_ref, bf16[384,128]{1,0:T(8,128)(2,1)S(1)} %collective-permute-done.1.got_ref, s32[4,192]{1,0:T(4,128)S(1)} %copy-done.3, f32[64,64]{1,0:T(8,128)S(1)} %copy-done.2), custom_call_target="tpu_custom_call" | custom-call | tf_op jit(solution)/shard_map/pallas_call | solution.py:193
  11.0 1.9 %collective-permute-start.3 = (bf16[4,4096]{1,0:T(4,128)(2,1)S(1)}, bf16[4,4096]{1,0:T(4,128)(2,1)S(1)}, u32[]{:S(2)}, u32[]{:S(2)}) collective-permute-start(bf16[4,4096]{1,0:T(4,128)(2,1)S(1)} %get-tuple-element.14), channel_id=1, source_target_pairs={{1,0},{0,18},{16,3},{17,19},{3,2},{2,16},{18,1},{19,17},{5,4},{4,2... | collective-permute-start | bytes 98312 | tf_op jit(solution)/shard_map/ppermute | solution.py:279
  12.9 0.8 %collective-permute-start.2 = (bf16[4,4096]{1,0:T(4,128)(2,1)S(1)}, bf16[4,4096]{1,0:T(4,128)(2,1)S(1)}, u32[]{:S(2)}, u32[]{:S(2)}) collective-permute-start(bf16[4,4096]{1,0:T(4,128)(2,1)S(1)} %get-tuple-element.14), channel_id=1, source_target_pairs={{16,17},{17,3},{1,18},{0,2},{18,19},{19,1},{3,16},{2,0},{20,21},{2... | collective-permute-start | bytes 98312 | tf_op jit(solution)/shard_map/ppermute | solution.py:278
  13.8 2.3 %collective-permute-start = (bf16[64,2048]{1,0:T(8,128)(2,1)S(1)}, bf16[64,2048]{1,0:T(8,128)(2,1)S(1)}, u32[]{:S(2)}, u32[]{:S(2)}) collective-permute-start(bf16[64,2048]{1,0:T(8,128)(2,1)S(1)} %shard_map.83), channel_id=1, source_target_pairs={{0,1},{1,0},{2,3},{3,2},{4,5},{5,4},{6,7},{7,6},{8,9},{9,8},{10,11... | collective-permute-start | bytes 786440 | tf_op jit(solution)/shard_map/ppermute | solution.py:287
  16.0 0.0 collective-permute-done.3
  16.0 0.0 collective-permute-done.2
  16.1 2.6 %collective-permute-start.9 = (bf16[4,4096]{1,0:T(4,128)(2,1)S(1)}, bf16[4,4096]{1,0:T(4,128)(2,1)S(1)}, u32[]{:S(2)}, u32[]{:S(2)}) collective-permute-start(bf16[4,4096]{1,0:T(4,128)(2,1)S(1)} %add_convert_fusion.rest_0_), channel_id=1, source_target_pairs={{0,12},{2,14},{4,8},{6,10},{8,4},{10,6},{12,0},{14,2},{16,28},{18,... | collective-permute-start | bytes 98312 | tf_op jit(solution)/shard_map/ppermute | solution.py:294
  18.7 0.0 collective-permute-start.7
  18.7 0.7 %collective-permute-start.5 = (bf16[4,4096]{1,0:T(4,128)(2,1)S(1)}, bf16[4,4096]{1,0:T(4,128)(2,1)S(1)}, u32[]{:S(2)}, u32[]{:S(2)}) collective-permute-start(bf16[4,4096]{1,0:T(4,128)(2,1)S(1)} %add_convert_fusion.rest_0_), channel_id=1, source_target_pairs={{0,6},{2,4},{4,2},{6,0},{8,14},{10,12},{12,10},{14,8},{16,22},{18,... | collective-permute-start | bytes 98312 | tf_op jit(solution)/shard_map/ppermute | solution.py:294
  19.4 0.0 collective-permute-start.4
  19.4 1.6 %collective-permute-done.9.rest_6_ = bf16[4,4096]{1,0:T(4,128)(2,1)S(1)} collective-permute-done((bf16[4,4096]{1,0:T(4,128)(2,1)S(1)}, bf16[4,4096]{1,0:T(4,128)(2,1)S(1)}, u32[]{:S(2)}, u32[]{:S(2)}) %collective-permute-start.9) | collective-permute-done | bytes 32800 | tf_op jit(solution)/shard_map/ppermute | solution.py:294
  21.0 0.0 collective-permute-start.10
  21.0 1.1 %collective-permute-done.7.rest_5_ = bf16[4,4096]{1,0:T(4,128)(2,1)S(1)} collective-permute-done((bf16[4,4096]{1,0:T(4,128)(2,1)S(1)}, bf16[4,4096]{1,0:T(4,128)(2,1)S(1)}, u32[]{:S(2)}, u32[]{:S(2)}) %collective-permute-start.7) | collective-permute-done | bytes 32800 | tf_op jit(solution)/shard_map/ppermute | solution.py:294
  22.0 0.6 %collective-permute-start.6 = (bf16[4,4096]{1,0:T(4,128)(2,1)S(1)}, bf16[4,4096]{1,0:T(4,128)(2,1)S(1)}, u32[]{:S(2)}, u32[]{:S(2)}) collective-permute-start(bf16[4,4096]{1,0:T(4,128)(2,1)S(1)} %collective-permute-done.5.rest_3_), channel_id=1, source_target_pairs={{0,2},{2,0},{4,6},{6,4},{8,10},{10,8},{12,14},{14,12},{16,18},{18,... | collective-permute-start | bytes 98312 | tf_op jit(solution)/shard_map/ppermute | solution.py:296
  22.6 0.0 collective-permute-done.10.rest_7_
  22.7 0.6 %collective-permute-done.8.rest_4_ = bf16[4,4096]{1,0:T(4,128)(2,1)S(1)} collective-permute-done((bf16[4,4096]{1,0:T(4,128)(2,1)S(1)}, bf16[4,4096]{1,0:T(4,128)(2,1)S(1)}, u32[]{:S(2)}, u32[]{:S(2)}) %collective-permute-start.8) | collective-permute-done | bytes 32800 | tf_op jit(solution)/shard_map/ppermute | solution.py:296
  23.2 0.2 collective-permute-done.6.rest_2_
  23.4 1.0 %shard_map.86 = f32[32,64]{1,0:T(8,128)} custom-call(s32[32,64]{1,0:T(8,128)S(1)} %broadcast_in_dim.3.place_ref, bf16[64,2048]{1,0:T(8,128)(2,1)S(1)} %get-tuple-element.16.low_ref, bf16[64,2048]{1,0:T(8,128)(2,1)S(1)} %get-tuple-element.15.high_ref, bf16[4,4096]{1,0:T(4,128)(2,1)S(1)} %add_convert_fusion.rest_0_, ...), custom_call_target="tpu_custom_call" | custom-call | tf_op jit(solution)/shard_map/pallas_call | solution.py:245
  (14 shorter events, 0.1 us)
Async XLA Ops:
  0.0 7.0 %copy-start = (bf16[4,192,7168]{2,1,0:T(8,128)(2,1)S(1)}, bf16[4,192,7168]{2,1,0:T(8,128)(2,1)}, u32[]{:S(2)}) copy-start(bf16[4,192,7168]{2,1,0:T(8,128)(2,1)} %param.8) | copy-start | bytes 33030148
  0.0 7.0 %copy-start.1 = (bf16[7168,64]{0,1:T(8,128)(2,1)S(1)}, bf16[7168,64]{0,1:T(8,128)(2,1)}, u32[]{:S(2)}) copy-start(bf16[7168,64]{0,1:T(8,128)(2,1)} %param.11) | copy-start | bytes 2752516
  4.0 6.3 %copy-start.2 = (f32[64,64]{1,0:T(8,128)S(1)}, f32[64,64]{1,0:T(8,128)}, u32[]{:S(2)}) copy-start(f32[64,64]{1,0:T(8,128)} %inv_ref.1) | copy-start | bytes 49156
  4.0 6.3 %copy-start.3 = (s32[4,192]{1,0:T(4,128)S(1)}, s32[4,192]{1,0:T(4,128)}, u32[]{:S(2)}) copy-start(s32[4,192]{1,0:T(4,128)} %mask_ref.1) | copy-start | bytes 9220
  4.0 6.2 %collective-permute-start.1 = (bf16[384,128]{1,0:T(8,128)(2,1)S(1)}, bf16[384,128]{1,0:T(8,128)(2,1)S(1)}, u32[]{:S(2)}, u32[]{:S(2)}) collective-permute-start(bf16[384,128]{1,0:T(8,128)(2,1)S(1)} %get-tuple-element.12), channel_id=1, source_target_pairs={{0,1},{1,0},{2,3},{3,2},{4,5},{5,4},{6,7},{7,6},{8,9},{9,8},{10,11... | collective-permute-start | bytes 294920 | tf_op jit(solution)/shard_map/ppermute | solution.py:268
  11.0 5.1 %collective-permute-start.3 = (bf16[4,4096]{1,0:T(4,128)(2,1)S(1)}, bf16[4,4096]{1,0:T(4,128)(2,1)S(1)}, u32[]{:S(2)}, u32[]{:S(2)}) collective-permute-start(bf16[4,4096]{1,0:T(4,128)(2,1)S(1)} %get-tuple-element.14), channel_id=1, source_target_pairs={{1,0},{0,18},{16,3},{17,19},{3,2},{2,16},{18,1},{19,17},{5,4},{4,2... | collective-permute-start | bytes 98312 | tf_op jit(solution)/shard_map/ppermute | solution.py:279
  12.9 3.1 %collective-permute-start.2 = (bf16[4,4096]{1,0:T(4,128)(2,1)S(1)}, bf16[4,4096]{1,0:T(4,128)(2,1)S(1)}, u32[]{:S(2)}, u32[]{:S(2)}) collective-permute-start(bf16[4,4096]{1,0:T(4,128)(2,1)S(1)} %get-tuple-element.14), channel_id=1, source_target_pairs={{16,17},{17,3},{1,18},{0,2},{18,19},{19,1},{3,16},{2,0},{20,21},{2... | collective-permute-start | bytes 98312 | tf_op jit(solution)/shard_map/ppermute | solution.py:278
  13.8 8.8 %collective-permute-start = (bf16[64,2048]{1,0:T(8,128)(2,1)S(1)}, bf16[64,2048]{1,0:T(8,128)(2,1)S(1)}, u32[]{:S(2)}, u32[]{:S(2)}) collective-permute-start(bf16[64,2048]{1,0:T(8,128)(2,1)S(1)} %shard_map.83), channel_id=1, source_target_pairs={{0,1},{1,0},{2,3},{3,2},{4,5},{5,4},{6,7},{7,6},{8,9},{9,8},{10,11... | collective-permute-start | bytes 786440 | tf_op jit(solution)/shard_map/ppermute | solution.py:287
  16.1 4.9 %collective-permute-start.9 = (bf16[4,4096]{1,0:T(4,128)(2,1)S(1)}, bf16[4,4096]{1,0:T(4,128)(2,1)S(1)}, u32[]{:S(2)}, u32[]{:S(2)}) collective-permute-start(bf16[4,4096]{1,0:T(4,128)(2,1)S(1)} %add_convert_fusion.rest_0_), channel_id=1, source_target_pairs={{0,12},{2,14},{4,8},{6,10},{8,4},{10,6},{12,0},{14,2},{16,28},{18,... | collective-permute-start | bytes 98312 | tf_op jit(solution)/shard_map/ppermute | solution.py:294
  18.7 3.3 %collective-permute-start.7 = (bf16[4,4096]{1,0:T(4,128)(2,1)S(1)}, bf16[4,4096]{1,0:T(4,128)(2,1)S(1)}, u32[]{:S(2)}, u32[]{:S(2)}) collective-permute-start(bf16[4,4096]{1,0:T(4,128)(2,1)S(1)} %add_convert_fusion.rest_0_), channel_id=1, source_target_pairs={{0,10},{2,8},{4,14},{6,12},{8,2},{10,0},{12,6},{14,4},{16,26},{18,... | collective-permute-start | bytes 98312 | tf_op jit(solution)/shard_map/ppermute | solution.py:294
  18.7 3.3 %collective-permute-start.5 = (bf16[4,4096]{1,0:T(4,128)(2,1)S(1)}, bf16[4,4096]{1,0:T(4,128)(2,1)S(1)}, u32[]{:S(2)}, u32[]{:S(2)}) collective-permute-start(bf16[4,4096]{1,0:T(4,128)(2,1)S(1)} %add_convert_fusion.rest_0_), channel_id=1, source_target_pairs={{0,6},{2,4},{4,2},{6,0},{8,14},{10,12},{12,10},{14,8},{16,22},{18,... | collective-permute-start | bytes 98312 | tf_op jit(solution)/shard_map/ppermute | solution.py:294
  19.4 3.3 %collective-permute-start.4 = (bf16[4,4096]{1,0:T(4,128)(2,1)S(1)}, bf16[4,4096]{1,0:T(4,128)(2,1)S(1)}, u32[]{:S(2)}, u32[]{:S(2)}) collective-permute-start(bf16[4,4096]{1,0:T(4,128)(2,1)S(1)} %add_convert_fusion.rest_0_), channel_id=1, source_target_pairs={{0,2},{2,0},{4,6},{6,4},{8,10},{10,8},{12,14},{14,12},{16,18},{18,... | collective-permute-start | bytes 98312 | tf_op jit(solution)/shard_map/ppermute | solution.py:296
  21.0 1.7 %collective-permute-start.10 = (bf16[4,4096]{1,0:T(4,128)(2,1)S(1)}, bf16[4,4096]{1,0:T(4,128)(2,1)S(1)}, u32[]{:S(2)}, u32[]{:S(2)}) collective-permute-start(bf16[4,4096]{1,0:T(4,128)(2,1)S(1)} %collective-permute-done.9.rest_6_), channel_id=1, source_target_pairs={{0,2},{2,0},{4,6},{6,4},{8,10},{10,8},{12,14},{14,12},{16,18},{18,... | collective-permute-start | bytes 98312 | tf_op jit(solution)/shard_map/ppermute | solution.py:296
  22.0 1.2 %collective-permute-start.8 = (bf16[4,4096]{1,0:T(4,128)(2,1)S(1)}, bf16[4,4096]{1,0:T(4,128)(2,1)S(1)}, u32[]{:S(2)}, u32[]{:S(2)}) collective-permute-start(bf16[4,4096]{1,0:T(4,128)(2,1)S(1)} %collective-permute-done.7.rest_5_), channel_id=1, source_target_pairs={{0,2},{2,0},{4,6},{6,4},{8,10},{10,8},{12,14},{14,12},{16,18},{18,... | collective-permute-start | bytes 98312 | tf_op jit(solution)/shard_map/ppermute | solution.py:296
  22.0 1.4 %collective-permute-start.6 = (bf16[4,4096]{1,0:T(4,128)(2,1)S(1)}, bf16[4,4096]{1,0:T(4,128)(2,1)S(1)}, u32[]{:S(2)}, u32[]{:S(2)}) collective-permute-start(bf16[4,4096]{1,0:T(4,128)(2,1)S(1)} %collective-permute-done.5.rest_3_), channel_id=1, source_target_pairs={{0,2},{2,0},{4,6},{6,4},{8,10},{10,8},{12,14},{14,12},{16,18},{18,... | collective-permute-start | bytes 98312 | tf_op jit(solution)/shard_map/ppermute | solution.py:296

commit v9 on v8

--- a/solution.py
+++ b/solution.py
@@ -34,13 +34,19 @@
     rest = block - top.astype(F32)
     middle = rest.astype(BF16)
     last = (rest - middle.astype(F32)).astype(BF16)
-    for b in range(query_ref.shape[1] // (2 * rank)):
-        lanes = pl.ds(b * 2 * rank, 2 * rank)
-        query = query_ref[:, lanes]
-        total = jnp.dot(query, last, preferred_element_type=F32)
-        total += jnp.dot(query, middle, preferred_element_type=F32)
-        total += jnp.dot(query, top, preferred_element_type=F32)
-        pre_ref[:, lanes] = total.astype(BF16)
+    count, feats = query_ref.shape
+    width = 2 * rank
+    tiles = feats // width
+    stacked = jnp.concatenate(
+        [query_ref[:, b * width : (b + 1) * width] for b in range(tiles)], axis=0
+    )
+    terms = jnp.dot(
+        stacked, jnp.concatenate([last, middle, top], axis=1), preferred_element_type=F32
+    )
+    total = terms[:, :width] + terms[:, width : 2 * width] + terms[:, 2 * width :]
+    for b in range(tiles):
+        tile = total[b * count : (b + 1) * count]
+        pre_ref[:, pl.ds(b * width, width)] = tile.astype(BF16)
 
 
 def out_kernel(
@@ -153,7 +159,7 @@
 
 
 def outer_kernel(
-    length, in_ref, own_ref, got_ref, mask_ref, inv_ref, part_ref, sent_ref, pairs_ref
+    length, in_ref, own_ref, got_ref, mask_ref, inv_ref, part_ref, sent_ref, rows_ref, pairs_ref
 ):
     rank = inv_ref.shape[0]
     seqs = mask_ref.shape[0]
@@ -172,8 +178,9 @@
         grams[pair] = both[:rank, :rank] / low
         grams[pair + seqs // 2] = both[rank:, rank:] / high
     gram = jnp.concatenate(grams, axis=1)
+    rows_ref[pl.ds(0, rank), :] = inv_ref[...]
     mixed = jnp.concatenate(
-        [inv_ref[pl.ds(0, half, stride=2), :], inv_ref[pl.ds(1, half, stride=2), :]], axis=0
+        [rows_ref[pl.ds(0, half, stride=2), :], rows_ref[pl.ds(1, half, stride=2), :]], axis=0
     )
     pre = precise_dot(mixed, gram, (1, 0))
     for s in range(seqs):
@@ -196,7 +203,8 @@
         in_specs=[VMEM] * 5,
         out_specs=[VMEM] * 2,
         scratch_shapes=[
-            pltpu.VMEM((seqs * rank // 2, 2 * rank), F32),
+            pltpu.VMEM((rank + 16, rank), F32),
+            pltpu.VMEM(((seqs + 8) * rank // 2, 2 * rank), F32),
         ],
         compiler_params=params(16),
     )(in_part, out_own, out_got, token_mask, inv_input)

time: 24.7 us -> 24.6 us (level)
  no operation moved by 1% of the time
where the time goes in v9:
time: 24.6 us; the launch traced here: 24.4 us
  starting transfers between devices  12 us (49%)
  Pallas kernels  8.68 us (35%)
  waiting for transfers between devices  3.47 us (14%)
    pallas_call x1, Pallas kernels, project_out(): pl.pallas_call(functools.partial(out_kernel, chunks), out_shape=[jax.Shap...  3.8 us
    ppermute x3, starting transfers between devices, local_pair(): pieces[k] = lax.ppermute(mine, 'ex', [(i, i ^ k) for i in range(ex_size)])  3.27 us
    pallas_call x1, Pallas kernels, project_in(): pl.pallas_call(in_kernel, out_shape=jax.ShapeDtypeStruct((rows // 2, 2 *...  3.21 us
    ppermute x1, starting transfers between devices, local_pair(): out_got = lax.ppermute(out_sent, 'hid', swap_hid)  3 us
    ppermute x3, waiting for transfers between devices, local_pair(): pieces[k] = lax.ppermute(mine, 'ex', [(i, i ^ k) for i in range(ex_size)])  2.66 us
    ppermute x1, starting transfers between devices, local_pair(): query_got = lax.ppermute(query_own, 'hid', swap_hid)  2.41 us
    ppermute x1, starting transfers between devices, local_pair(): first = lax.ppermute(sent, axes, alpha)  2.11 us
    pallas_call x1, Pallas kernels, score(): pl.pallas_call(score_kernel, out_shape=jax.ShapeDtypeStruct((rows, low.sh...  0.96 us
  transfers between devices with their start and end apart: 11, of which 4 were waited for; matrix products, arithmetic and copies ran while one was open for 0% of the time, Pallas kernels for 13%

profile of v9, /device:TPU:0, one launch (start us, length us, event | category | flops | bytes accessed | tf_op | source)
XLA Modules:
  0.0 24.4 jit_solution(12479735612487775791)
XLA Ops:
  0.0 3.8 %shard_map.82 = (f32[384,128]{1,0:T(8,128)S(1)}, bf16[384,128]{1,0:T(8,128)(2,1)S(1)}, bf16[64,2048]{1,0:T(8,128)(2,1)S(1)}) custom-call(bf16[768,2048]{1,0:T(8,128)(2,1)} %bitcast.7, bf16[64,2048]{1,0:T(8,128)(2,1)} %bitcast.8, bf16[64,2048]{1,0:T(8,128)(2,1)} %query_hbm.1, f32[64,64]{1,0:T(8,128)} %inv_hbm.1), custom_call_target="tpu_custom_call" | custom-call | flops 6039797760 | bytes 94371840 | tf_op jit(solution)/shard_map/pallas_call | solution.py:93
  3.8 0.0 copy-start.2
  3.8 0.0 copy-start.3
  3.8 3.0 %collective-permute-start.1 = (bf16[384,128]{1,0:T(8,128)(2,1)S(1)}, bf16[384,128]{1,0:T(8,128)(2,1)S(1)}, u32[]{:S(2)}, u32[]{:S(2)}) collective-permute-start(bf16[384,128]{1,0:T(8,128)(2,1)S(1)} %get-tuple-element.12), channel_id=1, source_target_pairs={{0,1},{1,0},{2,3},{3,2},{4,5},{5,4},{6,7},{7,6},{8,9},{9,8},{10,11... | collective-permute-start | bytes 294920 | tf_op jit(solution)/shard_map/ppermute | solution.py:276
  6.8 3.2 %shard_map.84.in_ref = f32[384,128]{1,0:T(8,128)S(1)} custom-call(bf16[768,7168]{1,0:T(8,128)(2,1)S(1)} %bitcast.5, bf16[64,7168]{1,0:T(8,128)(2,1)S(1)} %bitcast.6), custom_call_target="tpu_custom_call" | custom-call | flops 704643072 | bytes 11010048 | tf_op jit(solution)/shard_map/pallas_call | solution.py:132
  10.1 0.7 %shard_map.85 = (f32[4,4096]{1,0:T(4,128)S(1)}, bf16[4,4096]{1,0:T(4,128)(2,1)S(1)}) custom-call(f32[384,128]{1,0:T(8,128)S(1)} %shard_map.84.in_ref, f32[384,128]{1,0:T(8,128)S(1)} %get-tuple-element.11.own_ref, bf16[384,128]{1,0:T(8,128)(2,1)S(1)} %collective-permute-done.1.got_ref, s32[4,192]{1,0:T(4,128)S(1)} %copy-done.3, f32[64,64]{1,0:T(8,128)S(1)} %copy-done.2), custom_call_target="tpu_custom_call" | custom-call | tf_op jit(solution)/shard_map/pallas_call | solution.py:200
  10.8 2.1 %collective-permute-start.3 = (bf16[4,4096]{1,0:T(4,128)(2,1)S(1)}, bf16[4,4096]{1,0:T(4,128)(2,1)S(1)}, u32[]{:S(2)}, u32[]{:S(2)}) collective-permute-start(bf16[4,4096]{1,0:T(4,128)(2,1)S(1)} %get-tuple-element.14), channel_id=1, source_target_pairs={{1,0},{0,18},{16,3},{17,19},{3,2},{2,16},{18,1},{19,17},{5,4},{4,2... | collective-permute-start | bytes 98312 | tf_op jit(solution)/shard_map/ppermute | solution.py:287
  12.9 0.7 %collective-permute-start.2 = (bf16[4,4096]{1,0:T(4,128)(2,1)S(1)}, bf16[4,4096]{1,0:T(4,128)(2,1)S(1)}, u32[]{:S(2)}, u32[]{:S(2)}) collective-permute-start(bf16[4,4096]{1,0:T(4,128)(2,1)S(1)} %get-tuple-element.14), channel_id=1, source_target_pairs={{16,17},{17,3},{1,18},{0,2},{18,19},{19,1},{3,16},{2,0},{20,21},{2... | collective-permute-start | bytes 98312 | tf_op jit(solution)/shard_map/ppermute | solution.py:286
  13.6 2.4 %collective-permute-start = (bf16[64,2048]{1,0:T(8,128)(2,1)S(1)}, bf16[64,2048]{1,0:T(8,128)(2,1)S(1)}, u32[]{:S(2)}, u32[]{:S(2)}) collective-permute-start(bf16[64,2048]{1,0:T(8,128)(2,1)S(1)} %shard_map.83), channel_id=1, source_target_pairs={{0,1},{1,0},{2,3},{3,2},{4,5},{5,4},{6,7},{7,6},{8,9},{9,8},{10,11... | collective-permute-start | bytes 786440 | tf_op jit(solution)/shard_map/ppermute | solution.py:295
  16.0 0.0 collective-permute-done.3
  16.0 0.0 collective-permute-done.2
  16.0 2.6 %collective-permute-start.9 = (bf16[4,4096]{1,0:T(4,128)(2,1)S(1)}, bf16[4,4096]{1,0:T(4,128)(2,1)S(1)}, u32[]{:S(2)}, u32[]{:S(2)}) collective-permute-start(bf16[4,4096]{1,0:T(4,128)(2,1)S(1)} %add_convert_fusion.rest_0_), channel_id=1, source_target_pairs={{0,12},{2,14},{4,8},{6,10},{8,4},{10,6},{12,0},{14,2},{16,28},{18,... | collective-permute-start | bytes 98312 | tf_op jit(solution)/shard_map/ppermute | solution.py:302
  18.6 0.0 collective-permute-start.7
  18.6 0.7 %collective-permute-start.5 = (bf16[4,4096]{1,0:T(4,128)(2,1)S(1)}, bf16[4,4096]{1,0:T(4,128)(2,1)S(1)}, u32[]{:S(2)}, u32[]{:S(2)}) collective-permute-start(bf16[4,4096]{1,0:T(4,128)(2,1)S(1)} %add_convert_fusion.rest_0_), channel_id=1, source_target_pairs={{0,6},{2,4},{4,2},{6,0},{8,14},{10,12},{12,10},{14,8},{16,22},{18,... | collective-permute-start | bytes 98312 | tf_op jit(solution)/shard_map/ppermute | solution.py:302
  19.3 0.0 collective-permute-start.4
  19.3 1.6 %collective-permute-done.9.rest_6_ = bf16[4,4096]{1,0:T(4,128)(2,1)S(1)} collective-permute-done((bf16[4,4096]{1,0:T(4,128)(2,1)S(1)}, bf16[4,4096]{1,0:T(4,128)(2,1)S(1)}, u32[]{:S(2)}, u32[]{:S(2)}) %collective-permute-start.9) | collective-permute-done | bytes 32800 | tf_op jit(solution)/shard_map/ppermute | solution.py:302
  20.9 1.1 %collective-permute-done.7.rest_5_ = bf16[4,4096]{1,0:T(4,128)(2,1)S(1)} collective-permute-done((bf16[4,4096]{1,0:T(4,128)(2,1)S(1)}, bf16[4,4096]{1,0:T(4,128)(2,1)S(1)}, u32[]{:S(2)}, u32[]{:S(2)}) %collective-permute-start.7) | collective-permute-done | bytes 32800 | tf_op jit(solution)/shard_map/ppermute | solution.py:302
  22.0 0.0 collective-permute-start.8
  22.0 0.0 collective-permute-done.5.rest_3_
  22.0 0.6 %collective-permute-start.6 = (bf16[4,4096]{1,0:T(4,128)(2,1)S(1)}, bf16[4,4096]{1,0:T(4,128)(2,1)S(1)}, u32[]{:S(2)}, u32[]{:S(2)}) collective-permute-start(bf16[4,4096]{1,0:T(4,128)(2,1)S(1)} %collective-permute-done.5.rest_3_), channel_id=1, source_target_pairs={{0,2},{2,0},{4,6},{6,4},{8,10},{10,8},{12,14},{14,12},{16,18},{18,... | collective-permute-start | bytes 98312 | tf_op jit(solution)/shard_map/ppermute | solution.py:304
  22.6 0.0 collective-permute-done.4.rest_1_
  22.6 0.6 %collective-permute-done.8.rest_4_ = bf16[4,4096]{1,0:T(4,128)(2,1)S(1)} collective-permute-done((bf16[4,4096]{1,0:T(4,128)(2,1)S(1)}, bf16[4,4096]{1,0:T(4,128)(2,1)S(1)}, u32[]{:S(2)}, u32[]{:S(2)}) %collective-permute-start.8) | collective-permute-done | bytes 32800 | tf_op jit(solution)/shard_map/ppermute | solution.py:304
  23.2 0.2 collective-permute-done.6.rest_2_
  23.4 1.0 %shard_map.86 = f32[32,64]{1,0:T(8,128)} custom-call(s32[32,64]{1,0:T(8,128)S(1)} %broadcast_in_dim.3.place_ref, bf16[64,2048]{1,0:T(8,128)(2,1)S(1)} %get-tuple-element.16.low_ref, bf16[64,2048]{1,0:T(8,128)(2,1)S(1)} %get-tuple-element.15.high_ref, bf16[4,4096]{1,0:T(4,128)(2,1)S(1)} %add_convert_fusion.rest_0_, ...), custom_call_target="tpu_custom_call" | custom-call | tf_op jit(solution)/shard_map/pallas_call | solution.py:253
  (14 shorter events, 0.1 us)
Async XLA Ops:
  0.0 6.8 %copy-start = (bf16[4,192,7168]{2,1,0:T(8,128)(2,1)S(1)}, bf16[4,192,7168]{2,1,0:T(8,128)(2,1)}, u32[]{:S(2)}) copy-start(bf16[4,192,7168]{2,1,0:T(8,128)(2,1)} %param.8) | copy-start | bytes 33030148
  0.0 6.8 %copy-start.1 = (bf16[7168,64]{0,1:T(8,128)(2,1)S(1)}, bf16[7168,64]{0,1:T(8,128)(2,1)}, u32[]{:S(2)}) copy-start(bf16[7168,64]{0,1:T(8,128)(2,1)} %param.11) | copy-start | bytes 2752516
  3.8 6.3 %copy-start.2 = (f32[64,64]{1,0:T(8,128)S(1)}, f32[64,64]{1,0:T(8,128)}, u32[]{:S(2)}) copy-start(f32[64,64]{1,0:T(8,128)} %inv_ref.1) | copy-start | bytes 49156
  3.8 6.3 %copy-start.3 = (s32[4,192]{1,0:T(4,128)S(1)}, s32[4,192]{1,0:T(4,128)}, u32[]{:S(2)}) copy-start(s32[4,192]{1,0:T(4,128)} %mask_ref.1) | copy-start | bytes 9220
  3.8 6.2 %collective-permute-start.1 = (bf16[384,128]{1,0:T(8,128)(2,1)S(1)}, bf16[384,128]{1,0:T(8,128)(2,1)S(1)}, u32[]{:S(2)}, u32[]{:S(2)}) collective-permute-start(bf16[384,128]{1,0:T(8,128)(2,1)S(1)} %get-tuple-element.12), channel_id=1, source_target_pairs={{0,1},{1,0},{2,3},{3,2},{4,5},{5,4},{6,7},{7,6},{8,9},{9,8},{10,11... | collective-permute-start | bytes 294920 | tf_op jit(solution)/shard_map/ppermute | solution.py:276
  10.8 5.2 %collective-permute-start.3 = (bf16[4,4096]{1,0:T(4,128)(2,1)S(1)}, bf16[4,4096]{1,0:T(4,128)(2,1)S(1)}, u32[]{:S(2)}, u32[]{:S(2)}) collective-permute-start(bf16[4,4096]{1,0:T(4,128)(2,1)S(1)} %get-tuple-element.14), channel_id=1, source_target_pairs={{1,0},{0,18},{16,3},{17,19},{3,2},{2,16},{18,1},{19,17},{5,4},{4,2... | collective-permute-start | bytes 98312 | tf_op jit(solution)/shard_map/ppermute | solution.py:287
  12.9 3.1 %collective-permute-start.2 = (bf16[4,4096]{1,0:T(4,128)(2,1)S(1)}, bf16[4,4096]{1,0:T(4,128)(2,1)S(1)}, u32[]{:S(2)}, u32[]{:S(2)}) collective-permute-start(bf16[4,4096]{1,0:T(4,128)(2,1)S(1)} %get-tuple-element.14), channel_id=1, source_target_pairs={{16,17},{17,3},{1,18},{0,2},{18,19},{19,1},{3,16},{2,0},{20,21},{2... | collective-permute-start | bytes 98312 | tf_op jit(solution)/shard_map/ppermute | solution.py:286
  13.6 9.0 %collective-permute-start = (bf16[64,2048]{1,0:T(8,128)(2,1)S(1)}, bf16[64,2048]{1,0:T(8,128)(2,1)S(1)}, u32[]{:S(2)}, u32[]{:S(2)}) collective-permute-start(bf16[64,2048]{1,0:T(8,128)(2,1)S(1)} %shard_map.83), channel_id=1, source_target_pairs={{0,1},{1,0},{2,3},{3,2},{4,5},{5,4},{6,7},{7,6},{8,9},{9,8},{10,11... | collective-permute-start | bytes 786440 | tf_op jit(solution)/shard_map/ppermute | solution.py:295
  16.0 4.9 %collective-permute-start.9 = (bf16[4,4096]{1,0:T(4,128)(2,1)S(1)}, bf16[4,4096]{1,0:T(4,128)(2,1)S(1)}, u32[]{:S(2)}, u32[]{:S(2)}) collective-permute-start(bf16[4,4096]{1,0:T(4,128)(2,1)S(1)} %add_convert_fusion.rest_0_), channel_id=1, source_target_pairs={{0,12},{2,14},{4,8},{6,10},{8,4},{10,6},{12,0},{14,2},{16,28},{18,... | collective-permute-start | bytes 98312 | tf_op jit(solution)/shard_map/ppermute | solution.py:302
  18.6 3.3 %collective-permute-start.7 = (bf16[4,4096]{1,0:T(4,128)(2,1)S(1)}, bf16[4,4096]{1,0:T(4,128)(2,1)S(1)}, u32[]{:S(2)}, u32[]{:S(2)}) collective-permute-start(bf16[4,4096]{1,0:T(4,128)(2,1)S(1)} %add_convert_fusion.rest_0_), channel_id=1, source_target_pairs={{0,10},{2,8},{4,14},{6,12},{8,2},{10,0},{12,6},{14,4},{16,26},{18,... | collective-permute-start | bytes 98312 | tf_op jit(solution)/shard_map/ppermute | solution.py:302
  18.6 3.3 %collective-permute-start.5 = (bf16[4,4096]{1,0:T(4,128)(2,1)S(1)}, bf16[4,4096]{1,0:T(4,128)(2,1)S(1)}, u32[]{:S(2)}, u32[]{:S(2)}) collective-permute-start(bf16[4,4096]{1,0:T(4,128)(2,1)S(1)} %add_convert_fusion.rest_0_), channel_id=1, source_target_pairs={{0,6},{2,4},{4,2},{6,0},{8,14},{10,12},{12,10},{14,8},{16,22},{18,... | collective-permute-start | bytes 98312 | tf_op jit(solution)/shard_map/ppermute | solution.py:302
  19.3 3.3 %collective-permute-start.4 = (bf16[4,4096]{1,0:T(4,128)(2,1)S(1)}, bf16[4,4096]{1,0:T(4,128)(2,1)S(1)}, u32[]{:S(2)}, u32[]{:S(2)}) collective-permute-start(bf16[4,4096]{1,0:T(4,128)(2,1)S(1)} %add_convert_fusion.rest_0_), channel_id=1, source_target_pairs={{0,2},{2,0},{4,6},{6,4},{8,10},{10,8},{12,14},{14,12},{16,18},{18,... | collective-permute-start | bytes 98312 | tf_op jit(solution)/shard_map/ppermute | solution.py:304
  20.9 1.7 %collective-permute-start.10 = (bf16[4,4096]{1,0:T(4,128)(2,1)S(1)}, bf16[4,4096]{1,0:T(4,128)(2,1)S(1)}, u32[]{:S(2)}, u32[]{:S(2)}) collective-permute-start(bf16[4,4096]{1,0:T(4,128)(2,1)S(1)} %collective-permute-done.9.rest_6_), channel_id=1, source_target_pairs={{0,2},{2,0},{4,6},{6,4},{8,10},{10,8},{12,14},{14,12},{16,18},{18,... | collective-permute-start | bytes 98312 | tf_op jit(solution)/shard_map/ppermute | solution.py:304
  22.0 1.2 %collective-permute-start.8 = (bf16[4,4096]{1,0:T(4,128)(2,1)S(1)}, bf16[4,4096]{1,0:T(4,128)(2,1)S(1)}, u32[]{:S(2)}, u32[]{:S(2)}) collective-permute-start(bf16[4,4096]{1,0:T(4,128)(2,1)S(1)} %collective-permute-done.7.rest_5_), channel_id=1, source_target_pairs={{0,2},{2,0},{4,6},{6,4},{8,10},{10,8},{12,14},{14,12},{16,18},{18,... | collective-permute-start | bytes 98312 | tf_op jit(solution)/shard_map/ppermute | solution.py:304
  22.0 1.4 %collective-permute-start.6 = (bf16[4,4096]{1,0:T(4,128)(2,1)S(1)}, bf16[4,4096]{1,0:T(4,128)(2,1)S(1)}, u32[]{:S(2)}, u32[]{:S(2)}) collective-permute-start(bf16[4,4096]{1,0:T(4,128)(2,1)S(1)} %collective-permute-done.5.rest_3_), channel_id=1, source_target_pairs={{0,2},{2,0},{4,6},{6,4},{8,10},{10,8},{12,14},{14,12},{16,18},{18,... | collective-permute-start | bytes 98312 | tf_op jit(solution)/shard_map/ppermute | solution.py:304

commit v10 on v9

--- a/solution.py
+++ b/solution.py
@@ -271,7 +271,7 @@
     swap_hid = [(0, 1), (1, 0)]
 
     out_own, out_sent, query_own = project_out(
-        out_grads.reshape(seqs * length, -1), proj_out.T, query_feats, inv_output, 4
+        out_grads.reshape(seqs * length, -1), proj_out.T, query_feats, inv_output, 2
     )
     out_got = lax.ppermute(out_sent, "hid", swap_hid)
     in_part = project_in(activations.reshape(seqs * length, depth), proj_in.T)

time: 24.6 us -> 24.6 us (level)
  no operation moved by 1% of the time
where the time goes in v10:
time: 24.6 us; the launch traced here: 24.4 us
  starting transfers between devices  12.1 us (49%)
  Pallas kernels  8.66 us (35%)
  waiting for transfers between devices  3.47 us (14%)
    pallas_call x1, Pallas kernels, project_out(): pl.pallas_call(functools.partial(out_kernel, chunks), out_shape=[jax.Shap...  3.78 us
    ppermute x3, starting transfers between devices, local_pair(): pieces[k] = lax.ppermute(mine, 'ex', [(i, i ^ k) for i in range(ex_size)])  3.27 us
    pallas_call x1, Pallas kernels, project_in(): pl.pallas_call(in_kernel, out_shape=jax.ShapeDtypeStruct((rows // 2, 2 *...  3.21 us
    ppermute x1, starting transfers between devices, local_pair(): out_got = lax.ppermute(out_sent, 'hid', swap_hid)  3 us
    ppermute x3, waiting for transfers between devices, local_pair(): pieces[k] = lax.ppermute(mine, 'ex', [(i, i ^ k) for i in range(ex_size)])  2.66 us
    ppermute x1, starting transfers between devices, local_pair(): query_got = lax.ppermute(query_own, 'hid', swap_hid)  2.41 us
    ppermute x1, starting transfers between devices, local_pair(): first = lax.ppermute(sent, axes, alpha)  2.13 us
    pallas_call x1, Pallas kernels, score(): pl.pallas_call(score_kernel, out_shape=jax.ShapeDtypeStruct((rows, low.sh...  0.96 us
  transfers between devices with their start and end apart: 11, of which 4 were waited for; matrix products, arithmetic and copies ran while one was open for 0% of the time, Pallas kernels for 13%

profile of v10, /device:TPU:0, one launch (start us, length us, event | category | flops | bytes accessed | tf_op | source)
XLA Modules:
  0.0 24.4 jit_solution(17371563413564507330)
XLA Ops:
  0.0 3.8 %shard_map.82 = (f32[384,128]{1,0:T(8,128)S(1)}, bf16[384,128]{1,0:T(8,128)(2,1)S(1)}, bf16[64,2048]{1,0:T(8,128)(2,1)S(1)}) custom-call(bf16[768,2048]{1,0:T(8,128)(2,1)} %bitcast.7, bf16[64,2048]{1,0:T(8,128)(2,1)} %bitcast.8, bf16[64,2048]{1,0:T(8,128)(2,1)} %query_hbm.1, f32[64,64]{1,0:T(8,128)} %inv_hbm.1), custom_call_target="tpu_custom_call" | custom-call | flops 6039797760 | bytes 94371840 | tf_op jit(solution)/shard_map/pallas_call | solution.py:93
  3.8 0.0 copy-start.2
  3.8 0.0 copy-start.3
  3.8 3.0 %collective-permute-start.1 = (bf16[384,128]{1,0:T(8,128)(2,1)S(1)}, bf16[384,128]{1,0:T(8,128)(2,1)S(1)}, u32[]{:S(2)}, u32[]{:S(2)}) collective-permute-start(bf16[384,128]{1,0:T(8,128)(2,1)S(1)} %get-tuple-element.12), channel_id=1, source_target_pairs={{0,1},{1,0},{2,3},{3,2},{4,5},{5,4},{6,7},{7,6},{8,9},{9,8},{10,11... | collective-permute-start | bytes 294920 | tf_op jit(solution)/shard_map/ppermute | solution.py:276
  6.8 3.2 %shard_map.84.in_ref = f32[384,128]{1,0:T(8,128)S(1)} custom-call(bf16[768,7168]{1,0:T(8,128)(2,1)S(1)} %bitcast.5, bf16[64,7168]{1,0:T(8,128)(2,1)S(1)} %bitcast.6), custom_call_target="tpu_custom_call" | custom-call | flops 704643072 | bytes 11010048 | tf_op jit(solution)/shard_map/pallas_call | solution.py:132
  10.1 0.7 %shard_map.85 = (f32[4,4096]{1,0:T(4,128)S(1)}, bf16[4,4096]{1,0:T(4,128)(2,1)S(1)}) custom-call(f32[384,128]{1,0:T(8,128)S(1)} %shard_map.84.in_ref, f32[384,128]{1,0:T(8,128)S(1)} %get-tuple-element.11.own_ref, bf16[384,128]{1,0:T(8,128)(2,1)S(1)} %collective-permute-done.1.got_ref, s32[4,192]{1,0:T(4,128)S(1)} %copy-done.3, f32[64,64]{1,0:T(8,128)S(1)} %copy-done.2), custom_call_target="tpu_custom_call" | custom-call | tf_op jit(solution)/shard_map/pallas_call | solution.py:200
  10.8 2.1 %collective-permute-start.3 = (bf16[4,4096]{1,0:T(4,128)(2,1)S(1)}, bf16[4,4096]{1,0:T(4,128)(2,1)S(1)}, u32[]{:S(2)}, u32[]{:S(2)}) collective-permute-start(bf16[4,4096]{1,0:T(4,128)(2,1)S(1)} %get-tuple-element.14), channel_id=1, source_target_pairs={{1,0},{0,18},{16,3},{17,19},{3,2},{2,16},{18,1},{19,17},{5,4},{4,2... | collective-permute-start | bytes 98312 | tf_op jit(solution)/shard_map/ppermute | solution.py:287
  12.9 0.7 %collective-permute-start.2 = (bf16[4,4096]{1,0:T(4,128)(2,1)S(1)}, bf16[4,4096]{1,0:T(4,128)(2,1)S(1)}, u32[]{:S(2)}, u32[]{:S(2)}) collective-permute-start(bf16[4,4096]{1,0:T(4,128)(2,1)S(1)} %get-tuple-element.14), channel_id=1, source_target_pairs={{16,17},{17,3},{1,18},{0,2},{18,19},{19,1},{3,16},{2,0},{20,21},{2... | collective-permute-start | bytes 98312 | tf_op jit(solution)/shard_map/ppermute | solution.py:286
  13.6 2.4 %collective-permute-start = (bf16[64,2048]{1,0:T(8,128)(2,1)S(1)}, bf16[64,2048]{1,0:T(8,128)(2,1)S(1)}, u32[]{:S(2)}, u32[]{:S(2)}) collective-permute-start(bf16[64,2048]{1,0:T(8,128)(2,1)S(1)} %shard_map.83), channel_id=1, source_target_pairs={{0,1},{1,0},{2,3},{3,2},{4,5},{5,4},{6,7},{7,6},{8,9},{9,8},{10,11... | collective-permute-start | bytes 786440 | tf_op jit(solution)/shard_map/ppermute | solution.py:295
  16.0 0.0 collective-permute-done.3
  16.0 0.0 collective-permute-done.2
  16.0 2.6 %collective-permute-start.9 = (bf16[4,4096]{1,0:T(4,128)(2,1)S(1)}, bf16[4,4096]{1,0:T(4,128)(2,1)S(1)}, u32[]{:S(2)}, u32[]{:S(2)}) collective-permute-start(bf16[4,4096]{1,0:T(4,128)(2,1)S(1)} %add_convert_fusion.rest_0_), channel_id=1, source_target_pairs={{0,12},{2,14},{4,8},{6,10},{8,4},{10,6},{12,0},{14,2},{16,28},{18,... | collective-permute-start | bytes 98312 | tf_op jit(solution)/shard_map/ppermute | solution.py:302
  18.6 0.0 collective-permute-start.7
  18.6 0.7 %collective-permute-start.5 = (bf16[4,4096]{1,0:T(4,128)(2,1)S(1)}, bf16[4,4096]{1,0:T(4,128)(2,1)S(1)}, u32[]{:S(2)}, u32[]{:S(2)}) collective-permute-start(bf16[4,4096]{1,0:T(4,128)(2,1)S(1)} %add_convert_fusion.rest_0_), channel_id=1, source_target_pairs={{0,6},{2,4},{4,2},{6,0},{8,14},{10,12},{12,10},{14,8},{16,22},{18,... | collective-permute-start | bytes 98312 | tf_op jit(solution)/shard_map/ppermute | solution.py:302
  19.3 0.0 collective-permute-start.4
  19.3 1.6 %collective-permute-done.9.rest_6_ = bf16[4,4096]{1,0:T(4,128)(2,1)S(1)} collective-permute-done((bf16[4,4096]{1,0:T(4,128)(2,1)S(1)}, bf16[4,4096]{1,0:T(4,128)(2,1)S(1)}, u32[]{:S(2)}, u32[]{:S(2)}) %collective-permute-start.9) | collective-permute-done | bytes 32800 | tf_op jit(solution)/shard_map/ppermute | solution.py:302
  20.9 1.1 %collective-permute-done.7.rest_5_ = bf16[4,4096]{1,0:T(4,128)(2,1)S(1)} collective-permute-done((bf16[4,4096]{1,0:T(4,128)(2,1)S(1)}, bf16[4,4096]{1,0:T(4,128)(2,1)S(1)}, u32[]{:S(2)}, u32[]{:S(2)}) %collective-permute-start.7) | collective-permute-done | bytes 32800 | tf_op jit(solution)/shard_map/ppermute | solution.py:302
  22.0 0.0 collective-permute-start.8
  22.0 0.0 collective-permute-done.5.rest_3_
  22.0 0.6 %collective-permute-start.6 = (bf16[4,4096]{1,0:T(4,128)(2,1)S(1)}, bf16[4,4096]{1,0:T(4,128)(2,1)S(1)}, u32[]{:S(2)}, u32[]{:S(2)}) collective-permute-start(bf16[4,4096]{1,0:T(4,128)(2,1)S(1)} %collective-permute-done.5.rest_3_), channel_id=1, source_target_pairs={{0,2},{2,0},{4,6},{6,4},{8,10},{10,8},{12,14},{14,12},{16,18},{18,... | collective-permute-start | bytes 98312 | tf_op jit(solution)/shard_map/ppermute | solution.py:304
  22.6 0.0 collective-permute-done.4.rest_1_
  22.6 0.6 %collective-permute-done.8.rest_4_ = bf16[4,4096]{1,0:T(4,128)(2,1)S(1)} collective-permute-done((bf16[4,4096]{1,0:T(4,128)(2,1)S(1)}, bf16[4,4096]{1,0:T(4,128)(2,1)S(1)}, u32[]{:S(2)}, u32[]{:S(2)}) %collective-permute-start.8) | collective-permute-done | bytes 32800 | tf_op jit(solution)/shard_map/ppermute | solution.py:304
  23.2 0.2 collective-permute-done.6.rest_2_
  23.4 1.0 %shard_map.86 = f32[32,64]{1,0:T(8,128)} custom-call(s32[32,64]{1,0:T(8,128)S(1)} %broadcast_in_dim.3.place_ref, bf16[64,2048]{1,0:T(8,128)(2,1)S(1)} %get-tuple-element.16.low_ref, bf16[64,2048]{1,0:T(8,128)(2,1)S(1)} %get-tuple-element.15.high_ref, bf16[4,4096]{1,0:T(4,128)(2,1)S(1)} %add_convert_fusion.rest_0_, ...), custom_call_target="tpu_custom_call" | custom-call | tf_op jit(solution)/shard_map/pallas_call | solution.py:253
  (14 shorter events, 0.1 us)
Async XLA Ops:
  0.0 6.8 %copy-start = (bf16[4,192,7168]{2,1,0:T(8,128)(2,1)S(1)}, bf16[4,192,7168]{2,1,0:T(8,128)(2,1)}, u32[]{:S(2)}) copy-start(bf16[4,192,7168]{2,1,0:T(8,128)(2,1)} %param.8) | copy-start | bytes 33030148
  0.0 6.8 %copy-start.1 = (bf16[7168,64]{0,1:T(8,128)(2,1)S(1)}, bf16[7168,64]{0,1:T(8,128)(2,1)}, u32[]{:S(2)}) copy-start(bf16[7168,64]{0,1:T(8,128)(2,1)} %param.11) | copy-start | bytes 2752516
  3.8 6.3 %copy-start.2 = (f32[64,64]{1,0:T(8,128)S(1)}, f32[64,64]{1,0:T(8,128)}, u32[]{:S(2)}) copy-start(f32[64,64]{1,0:T(8,128)} %inv_ref.1) | copy-start | bytes 49156
  3.8 6.3 %copy-start.3 = (s32[4,192]{1,0:T(4,128)S(1)}, s32[4,192]{1,0:T(4,128)}, u32[]{:S(2)}) copy-start(s32[4,192]{1,0:T(4,128)} %mask_ref.1) | copy-start | bytes 9220
  3.8 6.2 %collective-permute-start.1 = (bf16[384,128]{1,0:T(8,128)(2,1)S(1)}, bf16[384,128]{1,0:T(8,128)(2,1)S(1)}, u32[]{:S(2)}, u32[]{:S(2)}) collective-permute-start(bf16[384,128]{1,0:T(8,128)(2,1)S(1)} %get-tuple-element.12), channel_id=1, source_target_pairs={{0,1},{1,0},{2,3},{3,2},{4,5},{5,4},{6,7},{7,6},{8,9},{9,8},{10,11... | collective-permute-start | bytes 294920 | tf_op jit(solution)/shard_map/ppermute | solution.py:276
  10.8 5.2 %collective-permute-start.3 = (bf16[4,4096]{1,0:T(4,128)(2,1)S(1)}, bf16[4,4096]{1,0:T(4,128)(2,1)S(1)}, u32[]{:S(2)}, u32[]{:S(2)}) collective-permute-start(bf16[4,4096]{1,0:T(4,128)(2,1)S(1)} %get-tuple-element.14), channel_id=1, source_target_pairs={{1,0},{0,18},{16,3},{17,19},{3,2},{2,16},{18,1},{19,17},{5,4},{4,2... | collective-permute-start | bytes 98312 | tf_op jit(solution)/shard_map/ppermute | solution.py:287
  12.9 3.1 %collective-permute-start.2 = (bf16[4,4096]{1,0:T(4,128)(2,1)S(1)}, bf16[4,4096]{1,0:T(4,128)(2,1)S(1)}, u32[]{:S(2)}, u32[]{:S(2)}) collective-permute-start(bf16[4,4096]{1,0:T(4,128)(2,1)S(1)} %get-tuple-element.14), channel_id=1, source_target_pairs={{16,17},{17,3},{1,18},{0,2},{18,19},{19,1},{3,16},{2,0},{20,21},{2... | collective-permute-start | bytes 98312 | tf_op jit(solution)/shard_map/ppermute | solution.py:286
  13.6 9.0 %collective-permute-start = (bf16[64,2048]{1,0:T(8,128)(2,1)S(1)}, bf16[64,2048]{1,0:T(8,128)(2,1)S(1)}, u32[]{:S(2)}, u32[]{:S(2)}) collective-permute-start(bf16[64,2048]{1,0:T(8,128)(2,1)S(1)} %shard_map.83), channel_id=1, source_target_pairs={{0,1},{1,0},{2,3},{3,2},{4,5},{5,4},{6,7},{7,6},{8,9},{9,8},{10,11... | collective-permute-start | bytes 786440 | tf_op jit(solution)/shard_map/ppermute | solution.py:295
  16.0 4.9 %collective-permute-start.9 = (bf16[4,4096]{1,0:T(4,128)(2,1)S(1)}, bf16[4,4096]{1,0:T(4,128)(2,1)S(1)}, u32[]{:S(2)}, u32[]{:S(2)}) collective-permute-start(bf16[4,4096]{1,0:T(4,128)(2,1)S(1)} %add_convert_fusion.rest_0_), channel_id=1, source_target_pairs={{0,12},{2,14},{4,8},{6,10},{8,4},{10,6},{12,0},{14,2},{16,28},{18,... | collective-permute-start | bytes 98312 | tf_op jit(solution)/shard_map/ppermute | solution.py:302
  18.6 3.3 %collective-permute-start.7 = (bf16[4,4096]{1,0:T(4,128)(2,1)S(1)}, bf16[4,4096]{1,0:T(4,128)(2,1)S(1)}, u32[]{:S(2)}, u32[]{:S(2)}) collective-permute-start(bf16[4,4096]{1,0:T(4,128)(2,1)S(1)} %add_convert_fusion.rest_0_), channel_id=1, source_target_pairs={{0,10},{2,8},{4,14},{6,12},{8,2},{10,0},{12,6},{14,4},{16,26},{18,... | collective-permute-start | bytes 98312 | tf_op jit(solution)/shard_map/ppermute | solution.py:302
  18.6 3.3 %collective-permute-start.5 = (bf16[4,4096]{1,0:T(4,128)(2,1)S(1)}, bf16[4,4096]{1,0:T(4,128)(2,1)S(1)}, u32[]{:S(2)}, u32[]{:S(2)}) collective-permute-start(bf16[4,4096]{1,0:T(4,128)(2,1)S(1)} %add_convert_fusion.rest_0_), channel_id=1, source_target_pairs={{0,6},{2,4},{4,2},{6,0},{8,14},{10,12},{12,10},{14,8},{16,22},{18,... | collective-permute-start | bytes 98312 | tf_op jit(solution)/shard_map/ppermute | solution.py:302
  19.3 3.3 %collective-permute-start.4 = (bf16[4,4096]{1,0:T(4,128)(2,1)S(1)}, bf16[4,4096]{1,0:T(4,128)(2,1)S(1)}, u32[]{:S(2)}, u32[]{:S(2)}) collective-permute-start(bf16[4,4096]{1,0:T(4,128)(2,1)S(1)} %add_convert_fusion.rest_0_), channel_id=1, source_target_pairs={{0,2},{2,0},{4,6},{6,4},{8,10},{10,8},{12,14},{14,12},{16,18},{18,... | collective-permute-start | bytes 98312 | tf_op jit(solution)/shard_map/ppermute | solution.py:304
  20.9 1.7 %collective-permute-start.10 = (bf16[4,4096]{1,0:T(4,128)(2,1)S(1)}, bf16[4,4096]{1,0:T(4,128)(2,1)S(1)}, u32[]{:S(2)}, u32[]{:S(2)}) collective-permute-start(bf16[4,4096]{1,0:T(4,128)(2,1)S(1)} %collective-permute-done.9.rest_6_), channel_id=1, source_target_pairs={{0,2},{2,0},{4,6},{6,4},{8,10},{10,8},{12,14},{14,12},{16,18},{18,... | collective-permute-start | bytes 98312 | tf_op jit(solution)/shard_map/ppermute | solution.py:304
  22.0 1.2 %collective-permute-start.8 = (bf16[4,4096]{1,0:T(4,128)(2,1)S(1)}, bf16[4,4096]{1,0:T(4,128)(2,1)S(1)}, u32[]{:S(2)}, u32[]{:S(2)}) collective-permute-start(bf16[4,4096]{1,0:T(4,128)(2,1)S(1)} %collective-permute-done.7.rest_5_), channel_id=1, source_target_pairs={{0,2},{2,0},{4,6},{6,4},{8,10},{10,8},{12,14},{14,12},{16,18},{18,... | collective-permute-start | bytes 98312 | tf_op jit(solution)/shard_map/ppermute | solution.py:304
  22.0 1.4 %collective-permute-start.6 = (bf16[4,4096]{1,0:T(4,128)(2,1)S(1)}, bf16[4,4096]{1,0:T(4,128)(2,1)S(1)}, u32[]{:S(2)}, u32[]{:S(2)}) collective-permute-start(bf16[4,4096]{1,0:T(4,128)(2,1)S(1)} %collective-permute-done.5.rest_3_), channel_id=1, source_target_pairs={{0,2},{2,0},{4,6},{6,4},{8,10},{10,8},{12,14},{14,12},{16,18},{18,... | collective-permute-start | bytes 98312 | tf_op jit(solution)/shard_map/ppermute | solution.py:304
